TPU v7x, 32 devices: a whole 2x2x4 slice. The times are simulated.
32 devices in a mesh: dp: 4 (over z), blk: 4 (over x, core), head: 2 (over y).
Axes of the slice: x: 2, y: 2, z: 4, core: 2. Of those that a mesh axis runs over, the one named last changes fastest.
Arguments:
- tokens: bfloat16 [8, 1024, 2048], P('dp', ('blk', 'head')), may hold values from -6 to 6
- segments: int32 [8, 1024], P('dp'), may hold values from 0 to 3, never falling along the last dimension, each value on 1 to 512 neighbouring positions
- routes: int32 [8, 1024, 8], P('dp', ('blk', 'head')), may hold values from 0 to 31, all different within a row; in each aligned block of 128 rows (0 to 127, 128 to 255, ..., all dimensions but the last counted through in order) at most 36 rows name the same one
- cotangent: bfloat16 [8, 1024, 2048], P('dp', ('blk', 'head')), may hold values from -6 to 6
- attn_gain: float32 [2048], replicated, may hold values from 0.25 to 1.75
- qkv_weight: bfloat16 [2048, 5120], P('dp'), may hold values from -0.125 to 0.125
- q_gain: float32 [128], replicated, may hold values from 0.25 to 1.75
- k_gain: float32 [128], replicated, may hold values from 0.25 to 1.75
- out_weight: bfloat16 [2048, 4096], P('dp'), may hold values from -0.75 to 0.75
- ffn_gain: float32 [2048], replicated, may hold values from 0.25 to 1.75
- router_weight: bfloat16 [2048, 32], replicated, may hold values from -0.0625 to 0.0625
- gate_weight: bfloat16 [32, 2048, 768], P(('dp', 'blk', 'head')), may hold values from -0.125 to 0.125
- up_weight: bfloat16 [32, 2048, 768], P(('dp', 'blk', 'head')), may hold values from -0.125 to 0.125
- down_weight: bfloat16 [32, 768, 2048], P(('dp', 'blk', 'head')), may hold values from -0.875 to 0.875
Outputs:
- layer_out: bfloat16 [8, 1024, 2048], P('dp', ('blk', 'head'))
- input_grad: bfloat16 [8, 1024, 2048], P('dp', ('blk', 'head'))
- attn_gain_grad: float32 [2048], P(('dp', 'blk', 'head'))
- qkv_grad: float32 [2048, 5120], P(('dp', 'blk', 'head'))
- q_gain_grad: float32 [128], P(('dp', 'blk', 'head'))
- k_gain_grad: float32 [128], P(('dp', 'blk', 'head'))
- out_grad: float32 [2048, 4096], P(('dp', 'blk', 'head'))
- ffn_gain_grad: float32 [2048], P(('dp', 'blk', 'head'))
- router_grad: float32 [2048, 32], P(('dp', 'blk', 'head'))
- gate_grad: float32 [32, 2048, 768], P(('dp', 'blk', 'head'))
- up_grad: float32 [32, 2048, 768], P(('dp', 'blk', 'head'))
- down_grad: float32 [32, 768, 2048], P(('dp', 'blk', 'head'))
Inputs may be any that keep to these rules, and one draw needn't show every extreme that they name: `segments`: within each sequence the document numbers never fall; every document covers 1 to 512 consecutive positions and one covers exactly 512. `routes`: each position names 8 different experts. In each aligned block of 128 positions of a sequence (the positions of one device) no expert is named more than 36 times, and in some blocks an expert is named exactly 36 times.
All inputs are finite; a program needn't handle non-finite values.
Results may differ from a plain program's by a relative error of at most 0.029.
Values may be sent and summed in bfloat16 or wider, within the bound.
No kernel may reach another device: no remote copies, remote signals or barrier semaphores. Data moves between devices by JAX's collectives and lax.ppermute only.
A program may use at most 384 MiB of HBM per device.

v0:
```python
import math

import jax
import jax.numpy as jnp
from jax import lax
from jax.sharding import PartitionSpec as P

Q_HEADS = 32
KV_HEADS = 4
HEAD_DIM = 128


EPSILON = 1e-06
NEG_FILL = -1e30


def rms_scale(values, gain_vec):
    return (
        values * lax.rsqrt(jnp.mean(values * values, axis=-1, keepdims=True) + EPSILON) * gain_vec
    )


def rotary_tables(positions, head_width):
    half_width = head_width // 2
    frequency = 1000000.0 ** (-2.0 * jnp.arange(half_width, dtype=jnp.float32) / head_width)
    angles = positions.astype(jnp.float32)[:, None] * frequency[None, :]
    angles = jnp.concatenate([angles, angles], axis=-1)
    return (jnp.cos(angles), jnp.sin(angles))


def rotate(values, cosines, sines):
    half_width = values.shape[-1] // 2
    turned = jnp.concatenate([-values[..., half_width:], values[..., :half_width]], axis=-1)
    return values * cosines + turned * sines


def softmax_rows(scores):
    shifted = jnp.exp(scores - jnp.max(scores, axis=-1, keepdims=True))
    return shifted / jnp.sum(shifted, axis=-1, keepdims=True)


def contract_rows(left_side, right_side):
    return lax.dot_general(
        left_side, right_side, (((0,), (0,)), ((), ())), preferred_element_type=jnp.float32
    )


def contract_cols(left_side, right_side):
    return lax.dot_general(
        left_side, right_side, (((1,), (1,)), ((), ())), preferred_element_type=jnp.float32
    )


def block_allowed(segment, query_pos, query_seg, start, key_rows):
    key_pos = start + jnp.arange(key_rows, dtype=jnp.int32)
    key_seg = lax.dynamic_slice_in_dim(segment, jnp.maximum(start, 0), key_rows)
    return (
        (key_pos[None, :] <= query_pos[:, None])
        & (key_seg[None, :] == query_seg[:, None])
        & (start >= 0)
    )


def block_active(segment, query_start, start, key_rows):
    last_seg = lax.dynamic_slice_in_dim(segment, jnp.maximum(start, 0) + key_rows - 1, 1)[0]
    first_seg = lax.dynamic_slice_in_dim(segment, query_start, 1)[0]
    return (start >= 0) & (start <= query_start) & (last_seg >= first_seg)


def block_scores(grouped, key_block, allowed, score_scale):
    raw_scores = (
        jnp.einsum("qhgd,khd->hgqk", grouped, key_block, preferred_element_type=jnp.float32)
        * score_scale
    )
    return jnp.where(allowed[None, None], raw_scores, NEG_FILL)


def attend_forward(grouped, key_blocks, value_blocks, starts, segment, query_start, score_scale):
    query_rows = grouped.shape[0]
    key_rows = key_blocks.shape[1]
    query_pos = query_start + jnp.arange(query_rows, dtype=jnp.int32)
    query_seg = lax.dynamic_slice_in_dim(segment, query_start, query_rows)
    stat_shape = (grouped.shape[1], grouped.shape[2], query_rows)

    def stat_step(stats, item):
        key_block, start = item

        def stat_compute(previous):
            row_top, row_total = previous
            scores = block_scores(
                grouped,
                key_block,
                block_allowed(segment, query_pos, query_seg, start, key_rows),
                score_scale,
            )
            new_top = jnp.maximum(row_top, jnp.max(scores, axis=3))
            new_total = row_total * jnp.exp(row_top - new_top) + jnp.sum(
                jnp.exp(scores - new_top[:, :, :, None]), axis=3
            )
            return (new_top, new_total)

        def keep_stats(previous):
            return previous

        return (
            lax.cond(
                block_active(segment, query_start, start, key_rows), stat_compute, keep_stats, stats
            ),
            0,
        )

    stat_init = (jnp.full(stat_shape, NEG_FILL, jnp.float32), jnp.zeros(stat_shape, jnp.float32))
    (row_top, row_total), unused_stat = lax.scan(stat_step, stat_init, (key_blocks, starts))
    log_total = row_top + jnp.log(row_total)

    def value_step(accum, item):
        key_block, value_block, start = item

        def value_compute(previous):
            scores = block_scores(
                grouped,
                key_block,
                block_allowed(segment, query_pos, query_seg, start, key_rows),
                score_scale,
            )
            probs = jnp.exp(scores - log_total[:, :, :, None]).astype(jnp.bfloat16)
            return previous + jnp.einsum(
                "hgqk,khd->qhgd", probs, value_block, preferred_element_type=jnp.float32
            )

        def value_keep_accum(previous):
            return previous

        return (
            lax.cond(
                block_active(segment, query_start, start, key_rows),
                value_compute,
                value_keep_accum,
                accum,
            ),
            0,
        )

    attended, unused_ys = lax.scan(
        value_step, jnp.zeros(grouped.shape, jnp.float32), (key_blocks, value_blocks, starts)
    )
    return (attended, log_total)


def attend_backward(
    grouped,
    key_blocks,
    value_blocks,
    starts,
    segment,
    query_start,
    score_scale,
    log_total,
    grad_grouped,
):
    query_rows = grouped.shape[0]
    key_rows = key_blocks.shape[1]
    query_pos = query_start + jnp.arange(query_rows, dtype=jnp.int32)
    query_seg = lax.dynamic_slice_in_dim(segment, query_start, query_rows)

    def probs_and_grads(key_block, value_block, start):
        allowed = block_allowed(segment, query_pos, query_seg, start, key_rows)
        probs = jnp.exp(
            block_scores(grouped, key_block, allowed, score_scale) - log_total[:, :, :, None]
        )
        grad_probs = jnp.einsum(
            "qhgd,khd->hgqk", grad_grouped, value_block, preferred_element_type=jnp.float32
        )
        return (probs, grad_probs)

    def delta_step(accum, item):
        key_block, value_block, start = item

        def delta_compute(previous):
            probs, grad_probs = probs_and_grads(key_block, value_block, start)
            return previous + jnp.sum(probs * grad_probs, axis=3)

        def delta_keep_accum(previous):
            return previous

        return (
            lax.cond(
                block_active(segment, query_start, start, key_rows),
                delta_compute,
                delta_keep_accum,
                accum,
            ),
            0,
        )

    delta, unused_ys = lax.scan(
        delta_step, jnp.zeros(log_total.shape, jnp.float32), (key_blocks, value_blocks, starts)
    )

    def grad_step(accum, item):
        key_block, value_block, start = item

        def grad_compute(previous):
            probs, grad_probs = probs_and_grads(key_block, value_block, start)
            grad_scores = (probs * (grad_probs - delta[:, :, :, None])).astype(jnp.bfloat16)
            updated = previous + jnp.einsum(
                "hgqk,khd->qhgd", grad_scores, key_block, preferred_element_type=jnp.float32
            )
            key_grad = (
                jnp.einsum(
                    "hgqk,qhgd->khd", grad_scores, grouped, preferred_element_type=jnp.float32
                )
                * score_scale
            )
            value_grad = jnp.einsum(
                "hgqk,qhgd->khd",
                probs.astype(jnp.bfloat16),
                grad_grouped,
                preferred_element_type=jnp.float32,
            )
            return (updated, key_grad, value_grad)

        def skipped(previous):
            empty_grad = jnp.zeros(key_block.shape, jnp.float32)
            return (previous, empty_grad, empty_grad)

        updated, key_grad, value_grad = lax.cond(
            block_active(segment, query_start, start, key_rows), grad_compute, skipped, accum
        )
        return (updated, (key_grad, value_grad))

    query_grad, block_grads = lax.scan(
        grad_step, jnp.zeros(grouped.shape, jnp.float32), (key_blocks, value_blocks, starts)
    )
    return (query_grad * score_scale, block_grads[0], block_grads[1])


def body(
    tokens,
    segments,
    routes,
    cotangent,
    attn_gain,
    qkv_weight,
    q_gain,
    k_gain,
    out_weight,
    ffn_gain,
    router_weight,
    gate_weight,
    up_weight,
    down_weight,
):
    tok_rows = tokens.shape[1]
    model_width = tokens.shape[2]
    head_ways = lax.axis_size("head")
    cycle_ways = lax.axis_size("blk")
    seq_total = segments.shape[1]
    block_rows = tok_rows * head_ways
    query_dim = Q_HEADS * HEAD_DIM
    kv_dim = KV_HEADS * HEAD_DIM
    local_kv = KV_HEADS // head_ways
    group_size = Q_HEADS // KV_HEADS
    top_count = routes.shape[2]
    expert_total = router_weight.shape[1]
    capacity = (9 * tok_rows * top_count + 8 * expert_total - 1) // (8 * expert_total)
    score_scale = 1.0 / math.sqrt(HEAD_DIM)
    cycle_index = lax.axis_index("blk")
    head_index = lax.axis_index("head")
    block_start = cycle_index * block_rows
    my_start = block_start + head_index * tok_rows
    positions = my_start + jnp.arange(tok_rows, dtype=jnp.int32)
    cosines, sines = rotary_tables(positions, HEAD_DIM)
    qkv_full, out_full = (
        lax.all_gather(qkv_weight, "dp", axis=0, tiled=True),
        lax.all_gather(out_weight, "dp", axis=0, tiled=True),
    )
    expert_gate = gate_weight[0]
    expert_up = up_weight[0]
    expert_down = down_weight[0]

    def head_prepare(qkv_rows, query_gain, key_gain):
        queries = qkv_rows[:, :query_dim].reshape(tok_rows, Q_HEADS, HEAD_DIM)
        keys_pre = qkv_rows[:, query_dim : query_dim + kv_dim].reshape(tok_rows, KV_HEADS, HEAD_DIM)
        values_pre = qkv_rows[:, query_dim + kv_dim :].reshape(tok_rows, KV_HEADS, HEAD_DIM)
        queries = rotate(rms_scale(queries, query_gain), cosines[:, None], sines[:, None])
        keys_pre = rotate(rms_scale(keys_pre, key_gain), cosines[:, None], sines[:, None])
        return (queries, keys_pre, values_pre)

    def micro_step(shared_acc, inputs):
        layer_rows, segment, route, cot_rows = inputs
        layer_in = layer_rows.astype(jnp.float32)
        normed, norm_back = jax.vjp(rms_scale, layer_in, attn_gain)
        normed_b = normed.astype(jnp.bfloat16)
        qkv_rows = jnp.dot(normed_b, qkv_full, preferred_element_type=jnp.float32)
        prepared, prep_back = jax.vjp(head_prepare, qkv_rows, q_gain, k_gain)
        q_heads, k_heads, v_heads = (
            lax.all_to_all(
                prepared[0].astype(jnp.bfloat16), "head", split_axis=1, concat_axis=0, tiled=True
            ),
            lax.all_to_all(
                prepared[1].astype(jnp.bfloat16), "head", split_axis=1, concat_axis=0, tiled=True
            ),
            lax.all_to_all(
                prepared[2].astype(jnp.bfloat16), "head", split_axis=1, concat_axis=0, tiled=True
            ),
        )
        k_every, v_every = (
            lax.all_gather(k_heads, "blk", axis=0, tiled=True),
            lax.all_gather(v_heads, "blk", axis=0, tiled=True),
        )
        key_blocks = k_every.reshape(cycle_ways, block_rows, local_kv, HEAD_DIM)
        value_blocks = v_every.reshape(cycle_ways, block_rows, local_kv, HEAD_DIM)
        starts = jnp.arange(cycle_ways, dtype=jnp.int32) * block_rows
        grouped = q_heads.reshape(block_rows, local_kv, group_size, HEAD_DIM)
        attended, log_total = attend_forward(
            grouped, key_blocks, value_blocks, starts, segment, block_start, score_scale
        )
        attn_heads = attended.reshape(block_rows, local_kv * group_size, HEAD_DIM).astype(
            jnp.bfloat16
        )
        attn_rows = lax.all_to_all(
            attn_heads, "head", split_axis=0, concat_axis=1, tiled=True
        ).reshape(tok_rows, query_dim)
        middle = layer_in + contract_cols(attn_rows, out_full)
        normed2, norm2_back = jax.vjp(rms_scale, middle, ffn_gain)
        normed2_b = normed2.astype(jnp.bfloat16)
        logits = jnp.dot(normed2_b, router_weight, preferred_element_type=jnp.float32)
        gates = softmax_rows(jnp.take_along_axis(logits, route, axis=1))
        route_flat = route.reshape(-1)
        onehot = (route_flat[:, None] == jnp.arange(expert_total, dtype=jnp.int32)[None, :]).astype(
            jnp.int32
        )
        slots = jnp.sum((jnp.cumsum(onehot, axis=0) - onehot) * onehot, axis=1)

        def dispatch(rows_out):
            buffer = (
                jnp.zeros((expert_total, capacity, model_width), jnp.bfloat16)
                .at[route_flat, slots]
                .set(rows_out)
            )
            arrived = lax.all_to_all(
                buffer, ("dp", "blk", "head"), split_axis=0, concat_axis=0, tiled=True
            )
            return arrived.reshape(expert_total * capacity, model_width)

        def collect(rows_back):
            returned_buf = lax.all_to_all(
                rows_back.reshape(expert_total, capacity, model_width),
                ("dp", "blk", "head"),
                split_axis=0,
                concat_axis=0,
                tiled=True,
            )
            return returned_buf[route_flat, slots].reshape(tok_rows, top_count, model_width)

        expert_in = dispatch(jnp.repeat(normed2_b, top_count, axis=0))
        gate_pre = jnp.dot(expert_in, expert_gate, preferred_element_type=jnp.float32)
        up_pre = jnp.dot(expert_in, expert_up, preferred_element_type=jnp.float32)
        sigma = 1.0 / (1.0 + jnp.exp(-gate_pre))
        hidden = (gate_pre * sigma * up_pre).astype(jnp.bfloat16)
        produced = jnp.dot(hidden, expert_down, preferred_element_type=jnp.float32).astype(
            jnp.bfloat16
        )
        returned = collect(produced)
        mixture = jnp.sum(gates[:, :, None] * returned, axis=1)
        layer_out = (middle + mixture).astype(jnp.bfloat16)
        grad_out = cot_rows.astype(jnp.float32)
        grad_returned = (
            (gates[:, :, None] * grad_out[:, None, :])
            .astype(jnp.bfloat16)
            .reshape(tok_rows * top_count, model_width)
        )
        grad_gates = jnp.einsum(
            "tkd,td->tk", returned, cot_rows, preferred_element_type=jnp.float32
        )
        grad_produced = dispatch(grad_returned)
        grad_hidden = contract_cols(grad_produced, expert_down)
        grad_gate_pre = (grad_hidden * up_pre * sigma * (1.0 + gate_pre * (1.0 - sigma))).astype(
            jnp.bfloat16
        )
        grad_up_pre = (grad_hidden * gate_pre * sigma).astype(jnp.bfloat16)
        grad_expert_in = (
            contract_cols(grad_gate_pre, expert_gate) + contract_cols(grad_up_pre, expert_up)
        ).astype(jnp.bfloat16)
        grad_copies = collect(grad_expert_in)
        grad_picked = (
            gates * (grad_gates - jnp.sum(gates * grad_gates, axis=1, keepdims=True))
        ).astype(jnp.bfloat16)
        pick_table = (
            route[:, :, None] == jnp.arange(expert_total, dtype=jnp.int32)[None, None, :]
        ).astype(jnp.bfloat16)
        grad_logits = jnp.einsum(
            "tke,tk->te", pick_table, grad_picked, preferred_element_type=jnp.float32
        ).astype(jnp.bfloat16)
        router_grad = contract_rows(normed2_b, grad_logits)
        grad_normed2 = jnp.sum(grad_copies.astype(jnp.float32), axis=1) + contract_cols(
            grad_logits, router_weight
        )
        grad_mid_norm, ffn_gain_grad = norm2_back(grad_normed2)
        grad_mid = grad_out + grad_mid_norm
        grad_attn_out = grad_mid.astype(jnp.bfloat16)
        grad_attn = jnp.dot(grad_attn_out, out_full, preferred_element_type=jnp.float32).astype(
            jnp.bfloat16
        )
        grad_heads = lax.all_to_all(
            grad_attn.reshape(tok_rows, Q_HEADS, HEAD_DIM),
            "head",
            split_axis=1,
            concat_axis=0,
            tiled=True,
        )
        grad_grouped = grad_heads.reshape(block_rows, local_kv, group_size, HEAD_DIM)
        query_grad, key_grads, value_grads = attend_backward(
            grouped,
            key_blocks,
            value_blocks,
            starts,
            segment,
            block_start,
            score_scale,
            log_total,
            grad_grouped,
        )
        key_grad, value_grad = (
            lax.psum_scatter(
                key_grads.reshape(seq_total, local_kv, HEAD_DIM).astype(jnp.bfloat16),
                "blk",
                scatter_dimension=0,
                tiled=True,
            ).astype(jnp.float32),
            lax.psum_scatter(
                value_grads.reshape(seq_total, local_kv, HEAD_DIM).astype(jnp.bfloat16),
                "blk",
                scatter_dimension=0,
                tiled=True,
            ).astype(jnp.float32),
        )
        grad_q, grad_k, grad_v = (
            lax.all_to_all(
                query_grad.reshape(block_rows, local_kv * group_size, HEAD_DIM).astype(
                    jnp.bfloat16
                ),
                "head",
                split_axis=0,
                concat_axis=1,
                tiled=True,
            ),
            lax.all_to_all(
                key_grad.astype(jnp.bfloat16), "head", split_axis=0, concat_axis=1, tiled=True
            ),
            lax.all_to_all(
                value_grad.astype(jnp.bfloat16), "head", split_axis=0, concat_axis=1, tiled=True
            ),
        )
        grad_qkv, q_gain_grad, k_gain_grad = prep_back(
            (grad_q.astype(jnp.float32), grad_k.astype(jnp.float32), grad_v.astype(jnp.float32))
        )
        grad_qkv_b = grad_qkv.astype(jnp.bfloat16)
        grad_normed = contract_cols(grad_qkv_b, qkv_full)
        grad_in_norm, attn_gain_grad = norm_back(grad_normed)
        input_grad = (grad_mid + grad_in_norm).astype(jnp.bfloat16)
        kept_expert = (expert_in, hidden, grad_produced, grad_gate_pre, grad_up_pre)
        step_grads = (attn_gain_grad, q_gain_grad, k_gain_grad, ffn_gain_grad, router_grad)
        shared_acc = tuple((total + grad for total, grad in zip(shared_acc, step_grads)))
        kept = (normed_b, grad_qkv_b, grad_attn_out, attn_rows)
        return (shared_acc, (layer_out, input_grad, kept_expert, kept))

    shared_zero = (
        jnp.zeros((model_width,), jnp.float32),
        jnp.zeros((HEAD_DIM,), jnp.float32),
        jnp.zeros((HEAD_DIM,), jnp.float32),
        jnp.zeros((model_width,), jnp.float32),
        jnp.zeros((model_width, expert_total), jnp.float32),
    )
    shared_acc, outputs = lax.scan(micro_step, shared_zero, (tokens, segments, routes, cotangent))
    layer_outs, input_grads, kept_expert, kept = outputs
    expert_rows = kept_expert[0].reshape(-1, model_width)
    gate_grad = contract_rows(expert_rows, kept_expert[3].reshape(-1, kept_expert[3].shape[2]))
    up_grad = contract_rows(expert_rows, kept_expert[4].reshape(-1, kept_expert[4].shape[2]))
    down_grad = contract_rows(
        kept_expert[1].reshape(-1, kept_expert[1].shape[2]), kept_expert[2].reshape(-1, model_width)
    )
    qkv_grad = contract_rows(
        kept[0].reshape(-1, model_width), kept[1].reshape(-1, query_dim + 2 * kv_dim)
    )
    out_grad = contract_rows(kept[2].reshape(-1, model_width), kept[3].reshape(-1, query_dim))
    shards = (
        lax.psum_scatter(shared_acc[0], ("dp", "blk", "head"), scatter_dimension=0, tiled=True),
        lax.psum_scatter(qkv_grad, ("dp", "blk", "head"), scatter_dimension=0, tiled=True),
        lax.psum_scatter(shared_acc[1], ("dp", "blk", "head"), scatter_dimension=0, tiled=True),
        lax.psum_scatter(shared_acc[2], ("dp", "blk", "head"), scatter_dimension=0, tiled=True),
        lax.psum_scatter(out_grad, ("dp", "blk", "head"), scatter_dimension=0, tiled=True),
        lax.psum_scatter(shared_acc[3], ("dp", "blk", "head"), scatter_dimension=0, tiled=True),
        lax.psum_scatter(shared_acc[4], ("dp", "blk", "head"), scatter_dimension=0, tiled=True),
    )
    return (
        layer_outs,
        input_grads,
        shards[0],
        shards[1],
        shards[2],
        shards[3],
        shards[4],
        shards[5],
        shards[6],
        gate_grad[None],
        up_grad[None],
        down_grad[None],
    )


def solution(mesh):
    placed = (
        P("dp", ("blk", "head"), None),
        P("dp", None),
        P("dp", ("blk", "head"), None),
        P("dp", ("blk", "head"), None),
        P(),
        P("dp", None),
        P(),
        P(),
        P("dp", None),
        P(),
        P(),
        P(("dp", "blk", "head"), None, None),
        P(("dp", "blk", "head"), None, None),
        P(("dp", "blk", "head"), None, None),
    )
    return jax.shard_map(
        body,
        mesh=mesh,
        in_specs=placed,
        out_specs=(
            P("dp", ("blk", "head"), None),
            P("dp", ("blk", "head"), None),
            P(("dp", "blk", "head")),
            P(("dp", "blk", "head"), None),
            P(("dp", "blk", "head")),
            P(("dp", "blk", "head")),
            P(("dp", "blk", "head"), None),
            P(("dp", "blk", "head")),
            P(("dp", "blk", "head"), None),
            P(("dp", "blk", "head"), None, None),
            P(("dp", "blk", "head"), None, None),
            P(("dp", "blk", "head"), None, None),
        ),
        check_vma=False,
    )
```

profile of v0, /device:TPU:0, one launch (start us, length us, event | category | flops | bytes accessed | tf_op | source)
XLA Modules:
  0.0 4290.6 jit_solution(16213973724690290834)
XLA Ops:
  10.0 289.1 %all-gather.5.cloned.1.call-done = bf16[2048,4096]{1,0:T(8,128)(2,1)} async-done(((bf16[512,4096]{1,0:T(8,128)(2,1)}), bf16[2048,4096]{1,0:T(8,128)(2,1)}) %all-gather.5.cloned.1.call-update) | async-done | bytes 16777232 | tf_op jit(solution)/shard_map/all_gather | solution.py:276
  299.1 356.6 %all-gather.3.cloned.1.call-done = bf16[2048,5120]{1,0:T(8,128)(2,1)} async-done(((bf16[512,5120]{1,0:T(8,128)(2,1)}), bf16[2048,5120]{1,0:T(8,128)(2,1)}) %all-gather.3.cloned.1.call-update) | async-done | bytes 20971536 | tf_op jit(solution)/shard_map/all_gather | solution.py:275
  655.8 1899.9 %while.221 = (s32[]{:T(128)}, f32[2048]{0:T(1024)}, f32[128]{0:T(128)}, f32[128]{0:T(128)}, f32[2048]{0:T(1024)}, /*index=5*/f32[2048,32]{0,1:T(8,128)}, bf16[2,...) while((s32[]{:T(128)}, f32[2048]{0:T(1024)}, ...), condition=%wide.region_44.45_spmd.clone, body=%wide.region_0.44_spmd.clone.sunk | while | flops 34252191744 | bytes 847672704 | solution.py:476
  724.4 22.0 while.222
  747.9 24.9 while.223
  820.0 21.8 all-to-all-start.4
  869.6 89.9 %all-to-all-done.4 = bf16[32,36,2048]{2,1,0:T(8,128)(2,1)} async-done(((bf16[32,36,2048]{2,1,0:T(8,128)(2,1)}), bf16[32,36,2048]{2,1,0:T(8,128)(2,1)}, u32[]{:S(2)}, u32[]{:S(2)}) %all-to-all-start.4) | async-done | bytes 4718624 | tf_op jit(solution)/shard_map/while/body/eval_jaxpr/all_to_all | solution.py:342
  979.3 101.4 %all-to-all-done.5 = bf16[32,36,2048]{2,1,0:T(8,128)(2,1)} async-done(((bf16[32,36,2048]{2,1,0:T(8,128)(2,1)}), bf16[32,36,2048]{2,1,0:T(8,128)(2,1)}, u32[]{:S(2)}, u32[]{:S(2)}) %all-to-all-start.5) | async-done | bytes 4718624 | tf_op jit(solution)/shard_map/while/body/eval_jaxpr/all_to_all | solution.py:342
  1145.0 98.3 %all-to-all-done.7 = bf16[32,36,2048]{2,1,0:T(8,128)(2,1)} async-done(((bf16[32,36,2048]{2,1,0:T(8,128)(2,1)}), bf16[32,36,2048]{2,1,0:T(8,128)(2,1)}, u32[]{:S(2)}, u32[]{:S(2)}) %all-to-all-start.7) | async-done | bytes 4718624 | tf_op jit(solution)/shard_map/while/body/eval_jaxpr/all_to_all | solution.py:348
  1269.8 25.7 gather_fusion.2
  1305.3 59.3 %all-to-all-done.6 = bf16[32,36,2048]{2,1,0:T(8,128)(2,1)} async-done(((bf16[32,36,2048]{2,1,0:T(8,128)(2,1)}), bf16[32,36,2048]{2,1,0:T(8,128)(2,1)}, u32[]{:S(2)}, u32[]{:S(2)}) %all-to-all-start.6) | async-done | bytes 4718624 | tf_op jit(solution)/shard_map/while/body/eval_jaxpr/all_to_all | solution.py:348
  1371.8 25.4 gather_fusion.1
  1433.1 24.3 while.224
  1458.6 31.2 while.225
  1512.0 27.5 reduce-scatter.16.cloned.1.call-done
  1668.3 22.0 while.222
  1691.9 24.9 while.223
  1763.9 25.9 all-to-all-start.4
  1817.6 89.7 %all-to-all-done.4 = bf16[32,36,2048]{2,1,0:T(8,128)(2,1)} async-done(((bf16[32,36,2048]{2,1,0:T(8,128)(2,1)}), bf16[32,36,2048]{2,1,0:T(8,128)(2,1)}, u32[]{:S(2)}, u32[]{:S(2)}) %all-to-all-start.4) | async-done | bytes 4718624 | tf_op jit(solution)/shard_map/while/body/eval_jaxpr/all_to_all | solution.py:342
  1927.1 101.4 %all-to-all-done.5 = bf16[32,36,2048]{2,1,0:T(8,128)(2,1)} async-done(((bf16[32,36,2048]{2,1,0:T(8,128)(2,1)}), bf16[32,36,2048]{2,1,0:T(8,128)(2,1)}, u32[]{:S(2)}, u32[]{:S(2)}) %all-to-all-start.5) | async-done | bytes 4718624 | tf_op jit(solution)/shard_map/while/body/eval_jaxpr/all_to_all | solution.py:342
  2092.8 98.3 %all-to-all-done.7 = bf16[32,36,2048]{2,1,0:T(8,128)(2,1)} async-done(((bf16[32,36,2048]{2,1,0:T(8,128)(2,1)}), bf16[32,36,2048]{2,1,0:T(8,128)(2,1)}, u32[]{:S(2)}, u32[]{:S(2)}) %all-to-all-start.7) | async-done | bytes 4718624 | tf_op jit(solution)/shard_map/while/body/eval_jaxpr/all_to_all | solution.py:348
  2217.6 25.7 gather_fusion.2
  2253.1 59.3 %all-to-all-done.6 = bf16[32,36,2048]{2,1,0:T(8,128)(2,1)} async-done(((bf16[32,36,2048]{2,1,0:T(8,128)(2,1)}), bf16[32,36,2048]{2,1,0:T(8,128)(2,1)}, u32[]{:S(2)}, u32[]{:S(2)}) %all-to-all-start.6) | async-done | bytes 4718624 | tf_op jit(solution)/shard_map/while/body/eval_jaxpr/all_to_all | solution.py:348
  2319.6 25.4 gather_fusion.1
  2380.9 24.3 while.224
  2406.4 31.2 while.225
  2459.8 30.0 reduce-scatter.16.cloned.1.call-done
  2494.9 18.9 reduce-scatter.14.cloned.1.call-done
  2592.8 40.7 all-reduce.11
  2671.1 23.1 reduce-scatter.12.cloned.1.call-done
  2695.6 703.6 %reduce-scatter.10.cloned.1.call-done = f32[64,4096]{1,0:T(8,128)} async-done(((f32[2048,4096]{1,0:T(8,128)}), f32[64,4096]{1,0:T(8,128)}) %reduce-scatter.10.cloned.1.call-update) | async-done | bytes 1048592 | tf_op jit(solution)/shard_map/reduce_scatter | solution.py:493
  3399.2 884.6 %reduce-scatter.8.cloned.1.call-done = f32[64,5120]{1,0:T(8,128)} async-done(((f32[2048,5120]{1,0:T(8,128)}), f32[64,5120]{1,0:T(8,128)}) %reduce-scatter.8.cloned.1.call-update) | async-done | bytes 1310736 | tf_op jit(solution)/shard_map/reduce_scatter | solution.py:490
  (909 shorter events, 984.9 us)
Async XLA Ops:
  7.2 291.9 %all-gather.5.cloned.1.call-start = ((), (), s32[]{:S(2)}) async-start(), calls=%async_computation.18 | async-start | bytes 20971520 | tf_op jit(solution)/shard_map/all_gather | solution.py:276
  8.0 647.8 %all-gather.3.cloned.1.call-start = ((), (), s32[]{:S(2)}) async-start(), calls=%async_computation.17 | async-start | bytes 26214400 | tf_op jit(solution)/shard_map/all_gather | solution.py:275
  666.9 27.3 all-to-all-start.2
  694.2 7.9 all-to-all-start
  702.1 22.2 all-to-all-start.1
  776.9 13.2 all-to-all-start.3
  820.0 139.6 %all-to-all-start.4 = ((bf16[32,36,2048]{2,1,0:T(8,128)(2,1)}), bf16[32,36,2048]{2,1,0:T(8,128)(2,1)}, u32[]{:S(2)}, u32[]{:S(2)}) async-start(bf16[32,36,2048]{2,1,0:T(8,128)(2,1)} %copy.518), calls=%async_computation.4 | async-start | bytes 10485760 | tf_op jit(solution)/shard_map/while/body/eval_jaxpr/all_to_all | solution.py:342
  959.5 121.2 %all-to-all-start.5 = ((bf16[32,36,2048]{2,1,0:T(8,128)(2,1)}), bf16[32,36,2048]{2,1,0:T(8,128)(2,1)}, u32[]{:S(2)}, u32[]{:S(2)}) async-start(bf16[32,36,2048]{2,1,0:T(8,128)(2,1)} %copy.519), calls=%async_computation.5 | async-start | bytes 10485760 | tf_op jit(solution)/shard_map/while/body/eval_jaxpr/all_to_all | solution.py:342
  1122.0 121.4 %all-to-all-start.7 = ((bf16[32,36,2048]{2,1,0:T(8,128)(2,1)}), bf16[32,36,2048]{2,1,0:T(8,128)(2,1)}, u32[]{:S(2)}, u32[]{:S(2)}) async-start(bf16[32,36,2048]{2,1,0:T(8,128)(2,1)} %reshape.1166), calls=%async_computation.7 | async-start | bytes 10485760 | tf_op jit(solution)/shard_map/while/body/eval_jaxpr/all_to_all | solution.py:348
  1243.4 121.2 %all-to-all-start.6 = ((bf16[32,36,2048]{2,1,0:T(8,128)(2,1)}), bf16[32,36,2048]{2,1,0:T(8,128)(2,1)}, u32[]{:S(2)}, u32[]{:S(2)}) async-start(bf16[32,36,2048]{2,1,0:T(8,128)(2,1)} %reshape.1165), calls=%async_computation.6 | async-start | bytes 10485760 | tf_op jit(solution)/shard_map/while/body/eval_jaxpr/all_to_all | solution.py:348
  1415.7 17.3 all-to-all-start.8
  1419.3 120.2 %reduce-scatter.16.cloned.1.call-start = ((), (), s32[]{:S(2)}) async-start(), calls=%async_computation.23 | async-start | bytes 655360 | tf_op jit(solution)/shard_map/while/body/eval_jaxpr/reduce_scatter | solution.py:432
  1491.8 13.0 all-to-all-start.9
  1495.4 68.1 %reduce-scatter.14.cloned.1.call-start = ((), (), s32[]{:S(2)}) async-start(), calls=%async_computation.22 | async-start | bytes 655360 | tf_op jit(solution)/shard_map/while/body/eval_jaxpr/reduce_scatter | solution.py:426
  1541.2 24.0 all-to-all-start.11
  1565.2 12.4 all-to-all-start.10
  1611.5 27.3 all-to-all-start.2
  1646.7 21.5 all-to-all-start.1
  1720.9 13.2 all-to-all-start.3
  1763.9 143.4 %all-to-all-start.4 = ((bf16[32,36,2048]{2,1,0:T(8,128)(2,1)}), bf16[32,36,2048]{2,1,0:T(8,128)(2,1)}, u32[]{:S(2)}, u32[]{:S(2)}) async-start(bf16[32,36,2048]{2,1,0:T(8,128)(2,1)} %copy.518), calls=%async_computation.4 | async-start | bytes 10485760 | tf_op jit(solution)/shard_map/while/body/eval_jaxpr/all_to_all | solution.py:342
  1907.3 121.2 %all-to-all-start.5 = ((bf16[32,36,2048]{2,1,0:T(8,128)(2,1)}), bf16[32,36,2048]{2,1,0:T(8,128)(2,1)}, u32[]{:S(2)}, u32[]{:S(2)}) async-start(bf16[32,36,2048]{2,1,0:T(8,128)(2,1)} %copy.519), calls=%async_computation.5 | async-start | bytes 10485760 | tf_op jit(solution)/shard_map/while/body/eval_jaxpr/all_to_all | solution.py:342
  2069.8 121.4 %all-to-all-start.7 = ((bf16[32,36,2048]{2,1,0:T(8,128)(2,1)}), bf16[32,36,2048]{2,1,0:T(8,128)(2,1)}, u32[]{:S(2)}, u32[]{:S(2)}) async-start(bf16[32,36,2048]{2,1,0:T(8,128)(2,1)} %reshape.1166), calls=%async_computation.7 | async-start | bytes 10485760 | tf_op jit(solution)/shard_map/while/body/eval_jaxpr/all_to_all | solution.py:348
  2191.2 121.2 %all-to-all-start.6 = ((bf16[32,36,2048]{2,1,0:T(8,128)(2,1)}), bf16[32,36,2048]{2,1,0:T(8,128)(2,1)}, u32[]{:S(2)}, u32[]{:S(2)}) async-start(bf16[32,36,2048]{2,1,0:T(8,128)(2,1)} %reshape.1165), calls=%async_computation.6 | async-start | bytes 10485760 | tf_op jit(solution)/shard_map/while/body/eval_jaxpr/all_to_all | solution.py:348
  2363.5 17.3 all-to-all-start.8
  2367.1 122.8 %reduce-scatter.16.cloned.1.call-start = ((), (), s32[]{:S(2)}) async-start(), calls=%async_computation.23 | async-start | bytes 655360 | tf_op jit(solution)/shard_map/while/body/eval_jaxpr/reduce_scatter | solution.py:432
  2439.6 13.0 all-to-all-start.9
  2443.2 70.7 %reduce-scatter.14.cloned.1.call-start = ((), (), s32[]{:S(2)}) async-start(), calls=%async_computation.22 | async-start | bytes 655360 | tf_op jit(solution)/shard_map/while/body/eval_jaxpr/reduce_scatter | solution.py:426
  2491.5 24.0 all-to-all-start.11
  2515.6 12.4 all-to-all-start.10
  2555.7 138.5 %reduce-scatter.12.cloned.1.call-start = ((), (), s32[]{:S(2)}) async-start(), calls=%async_computation.21 | async-start | bytes 1081344
  2558.2 841.0 %reduce-scatter.10.cloned.1.call-start = ((), (), s32[]{:S(2)}) async-start(), calls=%async_computation.20 | async-start | bytes 34603008 | tf_op jit(solution)/shard_map/reduce_scatter | solution.py:493
  2572.9 1710.9 %reduce-scatter.8.cloned.1.call-start = ((), (), s32[]{:S(2)}) async-start(), calls=%async_computation.19 | async-start | bytes 43253760 | tf_op jit(solution)/shard_map/reduce_scatter | solution.py:490
  (173 other events, 4414.3 us)
Sparse Core Ops, SparseCore 0:
  9.6 289.4 all-gather.4
  300.7 355.0 all-gather.2
  1490.0 49.4 reduce-scatter.15
  1541.8 21.6 reduce-scatter.13
  2437.8 51.9 reduce-scatter.15
  2492.2 21.6 reduce-scatter.13
  2558.8 135.3 reduce-scatter.11
  2697.2 702.0 reduce-scatter.9
  3402.2 881.5 reduce-scatter.7
where the time goes:
time: 4300 us; the launch traced here: 4290 us
  waiting for transfers between devices  3100 us (72%)
  local copies, waits for them, and re-layouts  440 us (10%)
  matrix products  283 us (7%)
  other arithmetic  131 us (3%)
  starting transfers between devices  130 us (3%)
  loops' own time  124 us (3%)
  blocking collectives  68.9 us (2%)
    reduce_scatter x1, waiting for transfers between devices, body(): lax.psum_scatter(qkv_grad, ('dp', 'blk', 'head'), scatter_dimension=0, ti...  885 us
    reduce_scatter x1, waiting for transfers between devices, body(): lax.psum_scatter(out_grad, ('dp', 'blk', 'head'), scatter_dimension=0, ti...  704 us
    all_to_all x4, waiting for transfers between devices, dispatch(): lax.all_to_all(buffer, ('dp', 'blk', 'head'), split_axis=0, concat_axis=0...  382 us
    all_gather x1, waiting for transfers between devices, body(): lax.all_gather(qkv_weight, 'dp', axis=0, tiled=True)  357 us
    all_to_all x4, waiting for transfers between devices, collect(): lax.all_to_all(rows_back.reshape(expert_total, capacity, model_width), ('...  315 us
    all_gather x1, waiting for transfers between devices, body(): lax.all_gather(out_weight, 'dp', axis=0, tiled=True)  289 us
    gather x4, local copies, waits for them, and re-layouts, collect(): returned_buf[route_flat, slots].reshape(tok_rows, top_count, model_width)  102 us
  transfers between devices with their start and end apart: 33, of which 25 were waited for; matrix products, arithmetic and copies ran while one was open for 10% of the time, Pallas kernels for 0%

commit v1 on v0

v1 whole, which is shorter than its diff:
```python
import functools
import math

import jax
import jax.numpy as jnp
from jax import lax
from jax.experimental import pallas as pl
from jax.experimental.pallas import tpu as pltpu
from jax.sharding import PartitionSpec as P

Q_HEADS = 32
KV_HEADS = 4
HEAD_DIM = 128
EPSILON = 1e-06
NEG_FILL = -1e30
PLANE = ("blk", "head")
EVERY = ("dp", "blk", "head")
F32 = jnp.float32
BF16 = jnp.bfloat16


def dot_nn(a, b):
    return jnp.dot(a, b, preferred_element_type=F32)


def dot_nt(a, b):
    return lax.dot_general(a, b, (((1,), (1,)), ((), ())), preferred_element_type=F32)


def dot_tn(a, b):
    return lax.dot_general(a, b, (((0,), (0,)), ((), ())), preferred_element_type=F32)


def rms_parts(values):
    scale = lax.rsqrt(jnp.mean(values * values, axis=-1, keepdims=True) + EPSILON)
    return values * scale, scale


def rms_back(grad, unit, scale, gain_vec):
    scaled = grad * gain_vec
    return scale * (scaled - unit * jnp.mean(scaled * unit, axis=-1, keepdims=True))


def turn_head(unit, cosines, sines):
    return unit * cosines + pltpu.roll(unit, HEAD_DIM // 2, 1) * sines


def turn_back(grad, cosines, sines):
    return grad * cosines + pltpu.roll(grad * sines, HEAD_DIM // 2, 1)


def head_forward(raw, gain_row, cosines, sines):
    unit, scale = rms_parts(raw)
    return turn_head(unit * gain_row, cosines, sines), unit, scale


def fill_keys(heads, order_ref, qkv_ref, cos_ref, sin_ref, k_gain_ref, k_scr, v_scr):
    start = heads * HEAD_DIM

    def one(block, carry):
        place = order_ref[block]
        raw = qkv_ref[place, :, start : start + HEAD_DIM]
        turned, _, _ = head_forward(raw, k_gain_ref[...], cos_ref[block], sin_ref[block])
        k_scr[block] = turned.astype(BF16)
        v_scr[block] = qkv_ref[place, :, start + HEAD_DIM : start + 2 * HEAD_DIM].astype(BF16)
        return carry

    lax.fori_loop(0, qkv_ref.shape[0], one, 0)


def allowed_keys(row_seg, key_seg, row_block, key_block, heads):
    rows = lax.broadcasted_iota(jnp.int32, (row_seg.shape[0], key_seg.shape[1]), 0)
    cols = lax.broadcasted_iota(jnp.int32, (row_seg.shape[0], key_seg.shape[1]), 1)
    rows = rows + (row_block - key_block) * row_seg.shape[0]
    keep = jnp.where((row_seg == key_seg) & (cols <= rows), 0.0, NEG_FILL)
    return jnp.concatenate([keep] * heads, axis=0)


def attend_kernel(
    heads,
    score_scale,
    order_ref,
    low_ref,
    qkv_ref,
    cos_ref,
    sin_ref,
    q_gain_ref,
    k_gain_ref,
    seg_row_ref,
    seg_col_ref,
    attn_ref,
    stat_ref,
    k_scr,
    v_scr,
):
    block = pl.program_id(0)

    @pl.when(block == 0)
    def _():
        fill_keys(heads, order_ref, qkv_ref, cos_ref, sin_ref, k_gain_ref, k_scr, v_scr)

    place = order_ref[block]
    cosines, sines = cos_ref[block], sin_ref[block]
    rows = []
    for h in range(heads):
        raw = qkv_ref[place, :, h * HEAD_DIM : (h + 1) * HEAD_DIM]
        rows.append(head_forward(raw, q_gain_ref[...], cosines, sines)[0].astype(BF16))
    queries = jnp.concatenate(rows, axis=0)
    count = queries.shape[0]
    row_seg = seg_col_ref[block]

    def step(key_block, carry):
        top, total, acc = carry
        scores = dot_nt(queries, k_scr[key_block]) * score_scale
        scores = scores + allowed_keys(row_seg, seg_row_ref[key_block], block, key_block, heads)
        new_top = jnp.maximum(top, jnp.max(scores, axis=1, keepdims=True))
        shrink = jnp.exp(top - new_top)
        weights = jnp.exp(scores - new_top)
        total = total * shrink + jnp.sum(weights, axis=1, keepdims=True)
        acc = acc * shrink + dot_nn(weights.astype(BF16), v_scr[key_block])
        return new_top, total, acc

    first = step(
        block,
        (
            jnp.full((count, 1), NEG_FILL, F32),
            jnp.zeros((count, 1), F32),
            jnp.zeros((count, HEAD_DIM), F32),
        ),
    )
    top, total, acc = lax.fori_loop(low_ref[block], block, step, first)
    acc = acc / total
    size = attn_ref.shape[1]
    for h in range(heads):
        attn_ref[0, :, h * HEAD_DIM : (h + 1) * HEAD_DIM] = acc[h * size : (h + 1) * size].astype(
            BF16
        )
    stat_ref[0] = jnp.broadcast_to(top + jnp.log(total), (count, HEAD_DIM))


def attend_back_kernel(
    heads,
    score_scale,
    order_ref,
    low_ref,
    qkv_ref,
    cos_ref,
    sin_ref,
    q_gain_ref,
    k_gain_ref,
    seg_row_ref,
    seg_col_ref,
    attn_ref,
    grad_ref,
    stat_ref,
    out_ref,
    gain_ref,
    k_scr,
    v_scr,
    dk_scr,
    dv_scr,
):
    block = pl.program_id(0)
    blocks = pl.num_programs(0)
    start = heads * HEAD_DIM

    @pl.when(block == 0)
    def _():
        fill_keys(heads, order_ref, qkv_ref, cos_ref, sin_ref, k_gain_ref, k_scr, v_scr)
        dk_scr[...] = jnp.zeros_like(dk_scr)
        dv_scr[...] = jnp.zeros_like(dv_scr)
        gain_ref[...] = jnp.zeros_like(gain_ref)

    place = order_ref[block]
    cosines, sines = cos_ref[block], sin_ref[block]
    rows, units, scales, grads, deltas = [], [], [], [], []
    for h in range(heads):
        raw = qkv_ref[place, :, h * HEAD_DIM : (h + 1) * HEAD_DIM]
        turned, unit, scale = head_forward(raw, q_gain_ref[...], cosines, sines)
        rows.append(turned.astype(BF16))
        units.append(unit)
        scales.append(scale)
        grad = grad_ref[0, :, h * HEAD_DIM : (h + 1) * HEAD_DIM]
        grads.append(grad)
        attn = attn_ref[0, :, h * HEAD_DIM : (h + 1) * HEAD_DIM]
        deltas.append(jnp.sum(grad.astype(F32) * attn.astype(F32), axis=1, keepdims=True))
    queries = jnp.concatenate(rows, axis=0)
    grad_rows = jnp.concatenate(grads, axis=0)
    delta = jnp.concatenate(deltas, axis=0)
    stat = stat_ref[0]
    row_seg = seg_col_ref[block]
    count = queries.shape[0]

    def step(key_block, acc):
        keys, values = k_scr[key_block], v_scr[key_block]
        scores = dot_nt(queries, keys) * score_scale
        scores = scores + allowed_keys(row_seg, seg_row_ref[key_block], block, key_block, heads)
        probs = jnp.exp(scores - stat)
        grad_probs = dot_nt(grad_rows, values)
        grad_scores = (probs * (grad_probs - delta)).astype(BF16)
        dk_scr[key_block] += dot_tn(grad_scores, queries)
        dv_scr[key_block] += dot_tn(probs.astype(BF16), grad_rows)
        return acc + dot_nn(grad_scores, keys)

    acc = lax.fori_loop(
        low_ref[block], block + 1, step, jnp.zeros((count, HEAD_DIM), F32)
    )
    acc = acc * score_scale
    size = grad_ref.shape[1]
    gain_sum = jnp.zeros((1, HEAD_DIM), F32)
    for h in range(heads):
        grad = turn_back(acc[h * size : (h + 1) * size], cosines, sines)
        gain_sum = gain_sum + jnp.sum(grad * units[h], axis=0, keepdims=True)
        out_ref[place, :, h * HEAD_DIM : (h + 1) * HEAD_DIM] = rms_back(
            grad, units[h], scales[h], q_gain_ref[...]
        ).astype(BF16)
    gain_ref[0:1, :] += gain_sum

    @pl.when(block == blocks - 1)
    def _():
        def one(key_block, carry):
            spot = order_ref[key_block]
            raw = qkv_ref[spot, :, start : start + HEAD_DIM]
            unit, scale = rms_parts(raw)
            grad = turn_back(dk_scr[key_block] * score_scale, cos_ref[key_block], sin_ref[key_block])
            out_ref[spot, :, start : start + HEAD_DIM] = rms_back(
                grad, unit, scale, k_gain_ref[...]
            ).astype(BF16)
            out_ref[spot, :, start + HEAD_DIM : start + 2 * HEAD_DIM] = dv_scr[key_block].astype(
                BF16
            )
            return carry + jnp.sum(grad * unit, axis=0, keepdims=True)

        gain_ref[1:2, :] += lax.fori_loop(0, blocks, one, jnp.zeros((1, HEAD_DIM), F32))


def whole_block(shape):
    zeros = (0,) * len(shape)
    return pl.BlockSpec(shape, lambda block, order, low: zeros)


def row_block(shape):
    return pl.BlockSpec(shape, lambda block, order, low: (order[block], 0, 0))


def attention_inputs(qkv, tables, gains, segment):
    blocks, size, _ = qkv.shape
    rows = segment.reshape(blocks, 1, size)
    cols = segment.reshape(blocks, size, 1)
    arrays = (qkv, *tables, *gains, rows, cols)
    return arrays, [whole_block(a.shape) for a in arrays]


def attend(qkv, tables, gains, segment, order, low, heads):
    blocks, size, _ = qkv.shape
    arrays, specs = attention_inputs(qkv, tables, gains, segment)
    return pl.pallas_call(
        functools.partial(attend_kernel, heads, 1.0 / math.sqrt(HEAD_DIM)),
        grid_spec=pltpu.PrefetchScalarGridSpec(
            num_scalar_prefetch=2,
            grid=(blocks,),
            in_specs=specs,
            out_specs=[
                row_block((1, size, heads * HEAD_DIM)),
                row_block((1, heads * size, HEAD_DIM)),
            ],
            scratch_shapes=[pltpu.VMEM((blocks, size, HEAD_DIM), BF16)] * 2,
        ),
        out_shape=[
            jax.ShapeDtypeStruct((blocks, size, heads * HEAD_DIM), BF16),
            jax.ShapeDtypeStruct((blocks, heads * size, HEAD_DIM), F32),
        ],
        compiler_params=pltpu.CompilerParams(vmem_limit_bytes=48 * 2**20),
    )(order, low, *arrays)


def attend_back(qkv, tables, gains, segment, order, low, heads, attn, grad, stat):
    blocks, size, width = qkv.shape
    arrays, specs = attention_inputs(qkv, tables, gains, segment)
    return pl.pallas_call(
        functools.partial(attend_back_kernel, heads, 1.0 / math.sqrt(HEAD_DIM)),
        grid_spec=pltpu.PrefetchScalarGridSpec(
            num_scalar_prefetch=2,
            grid=(blocks,),
            in_specs=specs
            + [
                row_block((1, size, heads * HEAD_DIM)),
                row_block((1, size, heads * HEAD_DIM)),
                row_block((1, heads * size, HEAD_DIM)),
            ],
            out_specs=[whole_block((blocks, size, width)), whole_block((8, HEAD_DIM))],
            scratch_shapes=[pltpu.VMEM((blocks, size, HEAD_DIM), BF16)] * 2
            + [pltpu.VMEM((blocks, size, HEAD_DIM), F32)] * 2,
        ),
        out_shape=[
            jax.ShapeDtypeStruct((blocks, size, width), BF16),
            jax.ShapeDtypeStruct((8, HEAD_DIM), F32),
        ],
        compiler_params=pltpu.CompilerParams(vmem_limit_bytes=56 * 2**20),
    )(order, low, *arrays, attn, grad, stat)


def ring_steps(ways):
    ring = list(range(1, ways, 2)) + list(range(0, ways, 2))[::-1]
    return [(ring[i], ring[(i + 1) % ways]) for i in range(ways)]


def line_gather(rows, ways):
    held, out = rows, [rows]
    for _ in range(ways - 1):
        held = lax.ppermute(held, "dp", ring_steps(ways))
        out.append(held)
    return jnp.concatenate(out, axis=0)


def line_reduce(parts, ways):
    size = parts.shape[0] // ways
    back = [(b, a) for a, b in ring_steps(ways)]
    acc = parts[(ways - 1) * size :]
    for k in range(ways - 2, -1, -1):
        acc = lax.ppermute(acc, "dp", back)
        acc = (acc.astype(F32) + parts[k * size : (k + 1) * size].astype(F32)).astype(BF16)
    return acc


def paired(blk_ways, head_ways):
    return blk_ways == 4 and head_ways == 2


def flips(bit):
    return [(i, i ^ bit) for i in range(8)]


def plane_flips(turn):
    return (flips(4), flips(1)) if turn % 2 == 0 else (flips(1), flips(4))


def plane_gather(rows, turn, pair):
    if not pair:
        return lax.all_gather(rows, PLANE, axis=0, tiled=False)
    first, second = plane_flips(turn)
    two = jnp.stack([rows, lax.ppermute(rows, PLANE, first)])
    four = jnp.concatenate([two, lax.ppermute(two, PLANE, second)])
    return jnp.concatenate([four, lax.ppermute(four, PLANE, flips(2))])


def plane_order(plane_index, plane_ways, turn, pair):
    blocks = jnp.arange(plane_ways, dtype=jnp.int32)
    if not pair:
        return blocks
    away = blocks ^ plane_index
    x, core, y = (away >> 2) & 1, (away >> 1) & 1, away & 1
    near, far = (x, y) if turn % 2 == 0 else (y, x)
    return (core * 4 + far * 2 + near).astype(jnp.int32)


def plane_reduce(parts, turn, pair):
    if not pair:
        return lax.psum_scatter(parts, PLANE, scatter_dimension=0, tiled=False)
    first, second = plane_flips(turn)
    for half, move in ((4, flips(2)), (2, second), (1, first)):
        came = lax.ppermute(parts[half:], PLANE, move)
        parts = (parts[:half].astype(F32) + came.astype(F32)).astype(BF16)
    return parts[0]


def plane_exchange(rows):
    return lax.all_to_all(rows, PLANE, split_axis=0, concat_axis=0, tiled=True)


def body(
    tokens,
    segments,
    routes,
    cotangent,
    attn_gain,
    qkv_weight,
    q_gain,
    k_gain,
    out_weight,
    ffn_gain,
    router_weight,
    gate_weight,
    up_weight,
    down_weight,
):
    seqs, size, width = tokens.shape
    dp_ways = lax.axis_size("dp")
    blk_ways = lax.axis_size("blk")
    head_ways = lax.axis_size("head")
    plane_ways = blk_ways * head_ways
    pair = paired(blk_ways, head_ways)
    dp_index = lax.axis_index("dp")
    plane_index = lax.axis_index("blk") * head_ways + lax.axis_index("head")
    seq_total = segments.shape[1]
    experts = router_weight.shape[1]
    top_count = routes.shape[2]
    capacity = (9 * size * top_count + 8 * experts - 1) // (8 * experts)
    query_dim = Q_HEADS * HEAD_DIM
    kv_dim = KV_HEADS * HEAD_DIM
    heads = Q_HEADS // plane_ways
    share = plane_ways // KV_HEADS
    kv_index = plane_index // share
    local_dim = heads * HEAD_DIM
    extra = -(-2 * experts // 128) * 128

    weight_rows = qkv_weight.shape[0]

    def columns(weight, start, count):
        return lax.dynamic_slice(weight, (0, start), (weight_rows, count))

    qkv_local = lax.all_gather(
        jnp.concatenate(
            [
                columns(qkv_weight, plane_index * local_dim, local_dim),
                columns(qkv_weight, query_dim + kv_index * HEAD_DIM, HEAD_DIM),
                columns(qkv_weight, query_dim + kv_dim + kv_index * HEAD_DIM, HEAD_DIM),
            ],
            axis=1,
        ),
        "dp",
        axis=0,
        tiled=True,
    )
    out_local = lax.all_gather(
        columns(out_weight, plane_index * local_dim, local_dim), "dp", axis=0, tiled=True
    )

    half = HEAD_DIM // 2
    frequency = 1000000.0 ** (-2.0 * jnp.arange(half, dtype=F32) / HEAD_DIM)
    angles = jnp.arange(seq_total, dtype=jnp.int32).astype(F32)[:, None] * frequency[None, :]
    cosines, sines = jnp.cos(angles), jnp.sin(angles)
    tables = (
        jnp.concatenate([cosines, cosines], axis=1).reshape(plane_ways, size, HEAD_DIM),
        jnp.concatenate([-sines, sines], axis=1).reshape(plane_ways, size, HEAD_DIM),
    )
    gains = (q_gain[None], k_gain[None])
    attn_gain_row, ffn_gain_row = attn_gain[None], ffn_gain[None]

    expert_ids = dp_index * plane_ways + jnp.arange(plane_ways, dtype=jnp.int32)
    before = (
        jnp.arange(size, dtype=jnp.int32)[:, None] > jnp.arange(size, dtype=jnp.int32)[None, :]
    ).astype(BF16)
    slot_ids = jnp.arange(dp_ways * capacity, dtype=jnp.int32)

    def picks_of(route):
        line_routes = line_gather(route, dp_ways)
        chosen = jnp.any(line_routes[:, :, None] == expert_ids[None, None, :], axis=1)
        chosen = chosen.reshape(dp_ways, size, plane_ways)
        ranks = jnp.einsum(
            "ij,zje->zie", before, chosen.astype(BF16), preferred_element_type=F32
        ).astype(jnp.int32)
        ranks = ranks + jnp.arange(dp_ways, dtype=jnp.int32)[:, None, None] * capacity
        keys = jnp.where(chosen, ranks, -1).reshape(dp_ways * size, plane_ways).T
        picks = (keys[:, None, :] == slot_ids[None, :, None]).astype(BF16)
        return picks.reshape(plane_ways * dp_ways * capacity, dp_ways * size)

    picks = [picks_of(routes[s]) for s in range(seqs)]

    def dispatch(rows, s):
        return plane_exchange(dot_nn(picks[s], line_gather(rows, dp_ways)).astype(BF16))

    def collect(rows, s):
        return line_reduce(dot_tn(picks[s], plane_exchange(rows)).astype(BF16), dp_ways)

    orders, lows = [], []
    for s in range(seqs):
        blocks = segments[s].reshape(plane_ways, size)
        lows.append(
            jnp.sum(
                (blocks[None, :, size - 1] < blocks[:, None, 0]).astype(jnp.int32), axis=1
            ).astype(jnp.int32)
        )
        orders.append(plane_order(plane_index, plane_ways, s, pair))

    inputs, units, scales, spread = [], [], [], []
    for s in range(seqs):
        rows = tokens[s].astype(F32)
        unit, scale = rms_parts(rows)
        inputs.append(rows)
        units.append(unit)
        scales.append(scale)
        spread.append(plane_gather((unit * attn_gain_row).astype(BF16), s, pair))
    cot_rows = [dispatch(cotangent[s], s) for s in range(seqs)]
    projected, attended, stats, middles = [], [], [], []
    for s in range(seqs):
        qkv = dot_nn(spread[s].reshape(seq_total, width), qkv_local)
        qkv = qkv.reshape(plane_ways, size, local_dim + 2 * HEAD_DIM)
        attn, stat = attend(qkv, tables, gains, segments[s], orders[s], lows[s], heads)
        mixed = dot_nt(attn.reshape(seq_total, local_dim), out_local).astype(BF16)
        mixed = plane_reduce(mixed.reshape(plane_ways, size, width), s, pair)
        projected.append(qkv)
        attended.append(attn)
        stats.append(stat)
        middles.append(inputs[s] + mixed.astype(F32))

    normed2s, mid_units, mid_scales, gate_tables, came = [], [], [], [], []
    for s in range(seqs):
        unit, scale = rms_parts(middles[s])
        normed2 = (unit * ffn_gain_row).astype(BF16)
        logits = dot_nn(normed2, router_weight)
        chosen = jnp.any(
            routes[s][:, :, None] == jnp.arange(experts, dtype=jnp.int32)[None, None, :], axis=1
        )
        top = jnp.max(jnp.where(chosen, logits, -jnp.inf), axis=1, keepdims=True)
        powers = jnp.where(chosen, jnp.exp(jnp.where(chosen, logits - top, 0.0)), 0.0)
        gates = powers / jnp.sum(powers, axis=1, keepdims=True)
        coarse = gates.astype(BF16)
        fine = (gates - coarse.astype(F32)).astype(BF16)
        payload = [normed2, coarse, fine]
        if extra > 2 * experts:
            payload.append(jnp.zeros((size, extra - 2 * experts), BF16))
        normed2s.append(normed2)
        mid_units.append(unit)
        mid_scales.append(scale)
        gate_tables.append(gates)
        came.append(dispatch(jnp.concatenate(payload, axis=1), s))

    gate_w, up_w, down_w = gate_weight[0], up_weight[0], down_weight[0]
    expert_id = dp_index * plane_ways + plane_index
    extra_ids = jnp.arange(extra, dtype=jnp.int32)
    mine_coarse = (extra_ids == expert_id).astype(F32)[None, :]
    mine_fine = (extra_ids == experts + expert_id).astype(F32)[None, :]
    mine = mine_coarse + mine_fine
    kept = []
    grad_backs, out_backs = [], []
    for s in range(seqs):
        rows = came[s][:, :width]
        gate = jnp.sum(came[s][:, width:].astype(F32) * mine, axis=1, keepdims=True)
        gate_pre = dot_nn(rows, gate_w)
        up_pre = dot_nn(rows, up_w)
        pulled = dot_nt(cot_rows[s], down_w)
        sigma = 1.0 / (1.0 + jnp.exp(-gate_pre))
        hidden = (gate_pre * sigma * up_pre).astype(BF16).astype(F32)
        gate_grad_rows = jnp.sum(hidden * pulled, axis=1, keepdims=True)
        gated = (hidden * gate).astype(BF16)
        grad_hidden = pulled * gate
        grad_gate = (grad_hidden * up_pre * sigma * (1.0 + gate_pre * (1.0 - sigma))).astype(BF16)
        grad_up = (grad_hidden * gate_pre * sigma).astype(BF16)
        grad_rows = (dot_nt(grad_gate, gate_w) + dot_nt(grad_up, up_w)).astype(BF16)
        coarse = gate_grad_rows.astype(BF16)
        fine = gate_grad_rows - coarse.astype(F32)
        tail = (coarse.astype(F32) * mine_coarse + fine * mine_fine).astype(BF16)
        grad_backs.append(collect(jnp.concatenate([grad_rows, tail], axis=1), s))
        kept.append((rows, gated, cot_rows[s], grad_gate, grad_up))
    for s in range(seqs):
        out_backs.append(collect(dot_nn(kept[s][1], down_w).astype(BF16), s))
    layer_out = jnp.stack(
        [(middles[s] + out_backs[s].astype(F32)).astype(BF16) for s in range(seqs)]
    )
    every = [jnp.concatenate([kept[s][i] for s in range(seqs)], axis=0) for i in range(5)]
    gate_grad = dot_tn(every[0], every[3])
    up_grad = dot_tn(every[0], every[4])
    down_grad = dot_tn(every[1], every[2])

    grad_mids, grad_spread = [], []
    router_grad = jnp.zeros((width, experts), F32)
    ffn_sum = jnp.zeros((width,), F32)
    for s in range(seqs):
        tail = grad_backs[s][:, width:].astype(F32)
        gates = gate_tables[s]
        grad_gates = tail[:, :experts] + tail[:, experts : 2 * experts]
        grad_logits = (
            gates * (grad_gates - jnp.sum(gates * grad_gates, axis=1, keepdims=True))
        ).astype(BF16)
        router_grad = router_grad + dot_tn(normed2s[s], grad_logits)
        grad_normed2 = grad_backs[s][:, :width].astype(F32) + dot_nt(grad_logits, router_weight)
        ffn_sum = ffn_sum + jnp.sum(grad_normed2 * mid_units[s], axis=0)
        grad_mid = cotangent[s].astype(F32) + rms_back(
            grad_normed2, mid_units[s], mid_scales[s], ffn_gain_row
        )
        grad_mids.append(grad_mid)
        grad_spread.append(plane_gather(grad_mid.astype(BF16), s, pair))
    grad_qkvs, grad_ins = [], []
    head_sums = jnp.zeros((2, HEAD_DIM), F32)
    for s in range(seqs):
        flat = grad_spread[s].reshape(seq_total, width)
        grad_attn = dot_nn(flat, out_local).astype(BF16).reshape(plane_ways, size, local_dim)
        grad_qkv, sums = attend_back(
            projected[s],
            tables,
            gains,
            segments[s],
            orders[s],
            lows[s],
            heads,
            attended[s],
            grad_attn,
            stats[s],
        )
        head_sums = head_sums + sums[:2]
        grad_qkv = grad_qkv.reshape(seq_total, local_dim + 2 * HEAD_DIM)
        grad_qkvs.append(grad_qkv)
        grad_normed = dot_nt(grad_qkv, qkv_local).astype(BF16)
        grad_normed = plane_reduce(grad_normed.reshape(plane_ways, size, width), s, pair)
        grad_in = rms_back(grad_normed.astype(F32), units[s], scales[s], attn_gain_row)
        grad_ins.append((grad_mids[s] + grad_in).astype(BF16))
    input_grad = jnp.stack(grad_ins)

    def shared_grad(lefts, rights):
        total = sum(
            dot_tn(a.reshape(seq_total, -1), b.reshape(seq_total, -1))
            for a, b in zip(lefts, rights)
        ).astype(BF16)
        total = lax.psum_scatter(total, "dp", scatter_dimension=0, tiled=True)
        return plane_exchange(total).reshape(plane_ways, weight_rows // plane_ways, -1)

    def side_by_side(pieces):
        return pieces.transpose(1, 0, 2).reshape(pieces.shape[1], -1)

    out_grad = side_by_side(shared_grad(grad_spread, attended)).astype(F32)
    pieces = shared_grad(spread, grad_qkvs).astype(F32)
    row_count = pieces.shape[1]

    def kv_columns(start):
        part = pieces[:, :, start : start + HEAD_DIM]
        return side_by_side(part.reshape(KV_HEADS, share, row_count, HEAD_DIM).sum(axis=1))

    qkv_grad = jnp.concatenate(
        [
            side_by_side(pieces[:, :, :local_dim]),
            kv_columns(local_dim),
            kv_columns(local_dim + HEAD_DIM),
        ],
        axis=1,
    )
    own_rows = lax.dynamic_slice(
        qkv_weight, (plane_index * row_count, 0), (row_count, qkv_weight.shape[1])
    )
    own_gain = lax.dynamic_slice(
        attn_gain, ((dp_index * plane_ways + plane_index) * row_count,), (row_count,)
    )
    attn_gain_grad = jnp.sum(own_rows.astype(F32) * qkv_grad, axis=1) / own_gain

    def every_reduce(parts):
        return jnp.sum(
            lax.all_to_all(parts, EVERY, split_axis=0, concat_axis=0, tiled=True), axis=0
        )

    devices = dp_ways * plane_ways
    small = every_reduce(
        jnp.concatenate(
            [router_grad.reshape(devices, -1), ffn_sum.reshape(devices, -1)], axis=1
        )
    )
    head_small = every_reduce(
        head_sums.reshape(2, devices, -1).transpose(1, 0, 2).reshape(devices, -1)
    )
    head_small = head_small.reshape(2, -1)
    cut = row_count * experts
    return (
        layer_out,
        input_grad,
        attn_gain_grad,
        qkv_grad,
        head_small[0],
        head_small[1],
        out_grad,
        small[cut:],
        small[:cut].reshape(row_count, experts),
        gate_grad[None],
        up_grad[None],
        down_grad[None],
    )


def solution(mesh):
    placed = (
        P("dp", PLANE, None),
        P("dp", None),
        P("dp", PLANE, None),
        P("dp", PLANE, None),
        P(),
        P("dp", None),
        P(),
        P(),
        P("dp", None),
        P(),
        P(),
        P(EVERY, None, None),
        P(EVERY, None, None),
        P(EVERY, None, None),
    )
    return jax.shard_map(
        body,
        mesh=mesh,
        in_specs=placed,
        out_specs=(
            P("dp", PLANE, None),
            P("dp", PLANE, None),
            P(EVERY),
            P(EVERY, None),
            P(EVERY),
            P(EVERY),
            P(EVERY, None),
            P(EVERY),
            P(EVERY, None),
            P(EVERY, None, None),
            P(EVERY, None, None),
            P(EVERY, None, None),
        ),
        check_vma=False,
    )
```

time: 4300 us -> 1140 us (0.27)
  waiting for transfers between devices: 3100 us -> 550 us
  local copies, waits for them, and re-layouts: 440 us -> 55.3 us
  loops' own time: 124 us -> 0 us
  Pallas kernels: 0 us -> 92.2 us
  blocking collectives: 68.9 us -> 0 us
  matrix products: 283 us -> 226 us
  other arithmetic: 131 us -> 80.5 us
    reduce_scatter x6 -> x2, waiting for transfers between devices: 1680 us -> 0.01 us  [shared_grad(): total = lax.psum_scatter(total, 'dp', scatter_dimension=0, tiled=True)]
    all_gather x2, waiting for transfers between devices: 646 us -> 0.02 us  [the longest x1 0.02 us: body(): lax.all_gather(jnp.concatenate([columns(qkv_weight, plane_index * local_d...]
    all_to_all x24 -> x12, waiting for transfers between devices: 746 us -> 186 us  [the longest x10 182 us: plane_exchange(): return lax.all_to_all(rows, PLANE, split_axis=0, concat_axis=0, tiled=True)]
    ppermute x0 -> x54, waiting for transfers between devices: none -> 364 us  [the longest x18 143 us: line_gather(): held = lax.ppermute(held, 'dp', ring_steps(ways))]
    another operation x41 -> x0, loops' own time: 124 us -> none  [the longest x2 26.8 us: attend_backward(): lax.scan(delta_step, jnp.zeros(log_total.shape, jnp.float32), (key_blocks...]
    gather x10 -> x0, local copies, waits for them, and re-layouts: 117 us -> none  [the longest x4 102 us: collect(): returned_buf[route_flat, slots].reshape(tok_rows, top_count, model_width)]
    pallas_call x0 -> x4, Pallas kernels: none -> 92.2 us  [the longest x2 55 us: attend_back(): pl.pallas_call(functools.partial(attend_back_kernel, heads, 1.0 / math.sq...]
    all_to_all x24 -> x12, starting transfers between devices: 129 us -> 52.8 us  [the longest x10 46.3 us: plane_exchange(): return lax.all_to_all(rows, PLANE, split_axis=0, concat_axis=0, tiled=True)]
  transfers between devices with their start and end apart: 33 -> 70, of which waited for: 25 -> 40; matrix products, arithmetic and copies ran while one was open for 10% -> 29% of each run, Pallas kernels for 0% -> 8%
where the time goes in v1:
time: 1140 us; the launch traced here: 1130 us
  waiting for transfers between devices  550 us (48%)
  matrix products  226 us (20%)
  starting transfers between devices  112 us (10%)
  Pallas kernels  92.2 us (8%)
  other arithmetic  80.5 us (7%)
  local copies, waits for them, and re-layouts  55.3 us (5%)
  between operations  16.3 us (1%)
    all_to_all x10, waiting for transfers between devices, plane_exchange(): return lax.all_to_all(rows, PLANE, split_axis=0, concat_axis=0, tiled=True)  182 us
    ppermute x18, waiting for transfers between devices, line_gather(): held = lax.ppermute(held, 'dp', ring_steps(ways))  143 us
    ppermute x12, waiting for transfers between devices, line_reduce(): acc = lax.ppermute(acc, 'dp', back)  86 us
    dot_general x16, matrix products, dot_nn(): return jnp.dot(a, b, preferred_element_type=F32)  84.9 us
    dot_general x13, matrix products, dot_tn(): lax.dot_general(a, b, (((0,), (0,)), ((), ())), preferred_element_type=F32)  79.8 us
    dot_general x12, matrix products, dot_nt(): lax.dot_general(a, b, (((1,), (1,)), ((), ())), preferred_element_type=F32)  60.7 us
    ppermute x4, waiting for transfers between devices, plane_gather(): two = jnp.stack([rows, lax.ppermute(rows, PLANE, first)])  56.1 us
    pallas_call x2, Pallas kernels, attend_back(): pl.pallas_call(functools.partial(attend_back_kernel, heads, 1.0 / math.sq...  55 us
  transfers between devices with their start and end apart: 70, of which 40 were waited for; matrix products, arithmetic and copies ran while one was open for 29% of the time, Pallas kernels for 8%

profile of v1, /device:TPU:0, one launch (start us, length us, event | category | flops | bytes accessed | tf_op | source)
XLA Modules:
  0.0 1131.5 jit_solution(5475961560884270553)
XLA Ops:
  18.4 10.9 collective-permute-done.15
  34.3 22.5 %collective-permute-done.16 = bf16[2,128,2048]{2,1,0:T(8,128)(2,1)} collective-permute-done((bf16[2,128,2048]{2,1,0:T(8,128)(2,1)}, bf16[2,128,2048]{2,1,0:T(8,128)(2,1)}, u32[]{:S(2)}, u32[]{:S(2)}) %collective-permute-start.16) | collective-permute-done | bytes 1048608 | tf_op jit(solution)/shard_map/ppermute | solution.py:343
  76.1 16.3 %collective-permute-done.1 = bf16[2,128,2048]{2,1,0:T(8,128)(2,1)} collective-permute-done((bf16[2,128,2048]{2,1,0:T(8,128)(2,1)}, bf16[2,128,2048]{2,1,0:T(8,128)(2,1)}, u32[]{:S(2)}, u32[]{:S(2)}) %collective-permute-start.1) | collective-permute-done | bytes 1048608 | tf_op jit(solution)/shard_map/ppermute | solution.py:343
  103.8 19.2 %shard_map.230 = (bf16[8,128,512]{2,1,0:T(8,128)(2,1)S(1)}, f32[8,512,128]{2,1,0:T(8,128)S(1)}) custom-call(s32[8]{0:T(128)S(1)} %add_add_fusion.order_ref, s32[8]{0:T(128)S(1)} %convert_reduce_fusion.low_ref, f32[8,128,768]{2,1,0:T(8,128)} %fusion.52.qkv_ref, f32[8,128,128]{2,1,0:T(8,128)S(1)} %copy-done.2, f32[8,128,128]{2,1,0:T(8,128)S(1)} %copy-done.4, ...), custom_call_target="tpu_custom_call" | custom-call | tf_op jit(solution)/shard_map/pallas_call | solution.py:257
  140.1 18.0 %shard_map.229 = (bf16[8,128,512]{2,1,0:T(8,128)(2,1)S(1)}, f32[8,512,128]{2,1,0:T(8,128)S(1)}) custom-call(s32[8]{0:T(128)S(1)} %add_add_fusion.1.order_ref, s32[8]{0:T(128)S(1)} %convert_reduce_fusion.1.low_ref, f32[8,128,768]{2,1,0:T(8,128)} %fusion.54.qkv_ref, f32[8,128,128]{2,1,0:T(8,128)S(1)} %copy-done.3, f32[8,128,128]{2,1,0:T(8,128)S(1)} %copy-done.5, ...), custom_call_target="tpu_custom_call" | custom-call | tf_op jit(solution)/shard_map/pallas_call | solution.py:257
  165.5 14.4 %collective-permute-done.6 = s32[128,8]{0,1:T(8,128)S(1)} collective-permute-done((s32[128,8]{0,1:T(8,128)S(1)}, s32[128,8]{0,1:T(8,128)S(1)}, u32[]{:S(2)}, u32[]{:S(2)}) %collective-permute-start.6) | collective-permute-done | bytes 4128 | tf_op jit(solution)/shard_map/ppermute | solution.py:311
  200.2 12.3 %collective-permute-done.19 = bf16[2,128,2048]{2,1,0:T(8,128)(2,1)S(1)} collective-permute-done((bf16[2,128,2048]{2,1,0:T(8,128)(2,1)S(1)}, bf16[2,128,2048]{2,1,0:T(8,128)(2,1)S(1)}, u32[]{:S(2)}, u32[]{:S(2)}) %collective-permute-start.19) | collective-permute-done | bytes 1048608 | tf_op jit(solution)/shard_map/ppermute | solution.py:362
  242.9 12.8 %collective-permute-done.9 = bf16[128,2176]{1,0:T(8,128)(2,1)S(1)} collective-permute-done((bf16[128,2176]{1,0:T(8,128)(2,1)}, bf16[128,2176]{1,0:T(8,128)(2,1)S(1)}, u32[]{:S(2)}, u32[]{:S(2)}) %collective-permute-start.9) | collective-permute-done | bytes 557088 | tf_op jit(solution)/shard_map/ppermute | solution.py:311
  258.0 12.7 %collective-permute-done.10 = bf16[128,2176]{1,0:T(8,128)(2,1)S(1)} collective-permute-done((bf16[128,2176]{1,0:T(8,128)(2,1)S(1)}, bf16[128,2176]{1,0:T(8,128)(2,1)S(1)}, u32[]{:S(2)}, u32[]{:S(2)}) %collective-permute-start.10) | collective-permute-done | bytes 557088 | tf_op jit(solution)/shard_map/ppermute | solution.py:311
  272.2 12.7 %collective-permute-done.11 = bf16[128,2176]{1,0:T(8,128)(2,1)S(1)} collective-permute-done((bf16[128,2176]{1,0:T(8,128)(2,1)S(1)}, bf16[128,2176]{1,0:T(8,128)(2,1)S(1)}, u32[]{:S(2)}, u32[]{:S(2)}) %collective-permute-start.11) | collective-permute-done | bytes 557088 | tf_op jit(solution)/shard_map/ppermute | solution.py:311
  301.1 15.3 %collective-permute-done.24 = bf16[128,2176]{1,0:T(8,128)(2,1)S(1)} collective-permute-done((bf16[128,2176]{1,0:T(8,128)(2,1)}, bf16[128,2176]{1,0:T(8,128)(2,1)S(1)}, u32[]{:S(2)}, u32[]{:S(2)}) %collective-permute-start.24) | collective-permute-done | bytes 557088 | tf_op jit(solution)/shard_map/ppermute | solution.py:311
  317.0 14.3 %collective-permute-done.25 = bf16[128,2176]{1,0:T(8,128)(2,1)S(1)} collective-permute-done((bf16[128,2176]{1,0:T(8,128)(2,1)S(1)}, bf16[128,2176]{1,0:T(8,128)(2,1)S(1)}, u32[]{:S(2)}, u32[]{:S(2)}) %collective-permute-start.25) | collective-permute-done | bytes 557088 | tf_op jit(solution)/shard_map/ppermute | solution.py:311
  332.1 13.6 %collective-permute-done.26 = bf16[128,2176]{1,0:T(8,128)(2,1)S(1)} collective-permute-done((bf16[128,2176]{1,0:T(8,128)(2,1)S(1)}, bf16[128,2176]{1,0:T(8,128)(2,1)S(1)}, u32[]{:S(2)}, u32[]{:S(2)}) %collective-permute-start.26) | collective-permute-done | bytes 557088 | tf_op jit(solution)/shard_map/ppermute | solution.py:311
  358.4 14.6 %collective-permute-done.42 = bf16[128,2048]{1,0:T(8,128)(2,1)S(1)} collective-permute-done((bf16[128,2048]{1,0:T(8,128)(2,1)}, bf16[128,2048]{1,0:T(8,128)(2,1)S(1)}, u32[]{:S(2)}, u32[]{:S(2)}) %collective-permute-start.42) | collective-permute-done | bytes 524320 | tf_op jit(solution)/shard_map/ppermute | solution.py:311
  374.4 13.8 %collective-permute-done.43 = bf16[128,2048]{1,0:T(8,128)(2,1)} collective-permute-done((bf16[128,2048]{1,0:T(8,128)(2,1)S(1)}, bf16[128,2048]{1,0:T(8,128)(2,1)}, u32[]{:S(2)}, u32[]{:S(2)}) %collective-permute-start.43) | collective-permute-done | bytes 524320 | tf_op jit(solution)/shard_map/ppermute | solution.py:311
  388.7 13.3 %collective-permute-done.44 = bf16[128,2048]{1,0:T(8,128)(2,1)} collective-permute-done((bf16[128,2048]{1,0:T(8,128)(2,1)}, bf16[128,2048]{1,0:T(8,128)(2,1)}, u32[]{:S(2)}, u32[]{:S(2)}) %collective-permute-start.44) | collective-permute-done | bytes 524320 | tf_op jit(solution)/shard_map/ppermute | solution.py:311
  433.3 9.6 fusion.20
  449.9 23.3 %all-to-all-done.6 = bf16[8,144,2048]{2,1,0:T(8,128)(2,1)} async-done(((bf16[8,144,2048]{2,1,0:T(8,128)(2,1)}), bf16[8,144,2048]{2,1,0:T(8,128)(2,1)}, u32[]{:S(2)}, u32[]{:S(2)}) %all-to-all-start.6) | async-done | bytes 4718624 | tf_op jit(solution)/shard_map/all_to_all | solution.py:368
  490.7 9.6 fusion.22
  507.4 24.7 %all-to-all-done.1 = bf16[8,144,2048]{2,1,0:T(8,128)(2,1)} async-done(((bf16[8,144,2048]{2,1,0:T(8,128)(2,1)}), bf16[8,144,2048]{2,1,0:T(8,128)(2,1)}, u32[]{:S(2)}, u32[]{:S(2)}) %all-to-all-start.1) | async-done | bytes 4718624 | tf_op jit(solution)/shard_map/all_to_all | solution.py:368
  552.4 38.5 %all-to-all-done.3 = bf16[8,144,2048]{2,1,0:T(8,128)(2,1)} async-done(((bf16[8,144,2048]{2,1,0:T(8,128)(2,1)}), bf16[8,144,2048]{2,1,0:T(8,128)(2,1)}, u32[]{:S(2)}, u32[]{:S(2)}) %all-to-all-start.3) | async-done | bytes 4718624 | tf_op jit(solution)/shard_map/all_to_all | solution.py:368
  610.2 42.5 %all-to-all-done.5 = bf16[8,144,2176]{2,1,0:T(8,128)(2,1)} async-done(((bf16[8,144,2176]{2,1,0:T(8,128)(2,1)}), bf16[8,144,2176]{2,1,0:T(8,128)(2,1)}, u32[]{:S(2)}, u32[]{:S(2)}) %all-to-all-start.5) | async-done | bytes 5013536 | tf_op jit(solution)/shard_map/all_to_all | solution.py:368
  681.4 33.1 %all-to-all-done.7 = bf16[8,144,2176]{2,1,0:T(8,128)(2,1)} async-done(((bf16[8,144,2176]{2,1,0:T(8,128)(2,1)}), bf16[8,144,2176]{2,1,0:T(8,128)(2,1)}, u32[]{:S(2)}, u32[]{:S(2)}) %all-to-all-start.7) | async-done | bytes 5013536 | tf_op jit(solution)/shard_map/all_to_all | solution.py:368
  785.0 31.9 %collective-permute-done.35 = bf16[128,2176]{1,0:T(8,128)(2,1)S(1)} collective-permute-done((bf16[128,2176]{1,0:T(8,128)(2,1)S(1)}, bf16[128,2176]{1,0:T(8,128)(2,1)S(1)}, u32[]{:S(2)}, u32[]{:S(2)}) %collective-permute-start.35) | collective-permute-done | bytes 557088 | tf_op jit(solution)/shard_map/ppermute | solution.py:321
  835.0 11.6 %collective-permute-done.36 = bf16[128,2048]{1,0:T(8,128)(2,1)S(1)} collective-permute-done((bf16[128,2048]{1,0:T(8,128)(2,1)S(1)}, bf16[128,2048]{1,0:T(8,128)(2,1)S(1)}, u32[]{:S(2)}, u32[]{:S(2)}) %collective-permute-start.36) | collective-permute-done | bytes 524320 | tf_op jit(solution)/shard_map/ppermute | solution.py:342
  855.2 27.2 %collective-permute-done.48 = bf16[128,2048]{1,0:T(8,128)(2,1)S(1)} collective-permute-done((bf16[128,2048]{1,0:T(8,128)(2,1)}, bf16[128,2048]{1,0:T(8,128)(2,1)S(1)}, u32[]{:S(2)}, u32[]{:S(2)}) %collective-permute-start.48) | collective-permute-done | bytes 524320 | tf_op jit(solution)/shard_map/ppermute | solution.py:342
  887.0 11.7 %fusion.15 = f32[1,2048,768]{2,1,0:T(8,128)} fusion(bf16[1152,2048]{1,0:T(8,128)(2,1)S(1)} %slice.348, bf16[1152,2048]{1,0:T(8,128)(2,1)S(1)} %slice.336, bf16[1152,768]{1,0:T(8,128)(2,1)} %get-tuple-element.112, bf16[1152,768]{1,0:T(8,128)(2,1)S(1)} %copy-done.107), kind=kOutput, calls=%fused_computation.44 | convolution fusion | flops 7273709568 | bytes 19267584 | tf_op jit(solution)/shard_map/dot_general | solution.py:31
  907.9 11.9 %fusion.14 = f32[1,2048,768]{2,1,0:T(8,128)} fusion(bf16[1152,2048]{1,0:T(8,128)(2,1)S(1)} %slice.348, bf16[1152,2048]{1,0:T(8,128)(2,1)S(1)} %slice.336, bf16[1152,768]{1,0:T(8,128)(2,1)} %get-tuple-element.110, bf16[1152,768]{1,0:T(8,128)(2,1)} %get-tuple-element.111), kind=kOutput, calls=%fused_computation.43 | convolution fusion | flops 7273709568 | bytes 19267584 | tf_op jit(solution)/shard_map/dot_general | solution.py:31
  936.5 28.2 %shard_map.232 = (bf16[8,128,768]{2,1,0:T(8,128)(2,1)}, f32[8,128]{1,0:T(8,128)}) custom-call(s32[8]{0:T(128)} %copy-done.19, s32[8]{0:T(128)} %copy-done.20, f32[8,128,768]{2,1,0:T(8,128)} %fusion.52.qkv_ref, f32[8,128,128]{2,1,0:T(8,128)} %get-tuple-element.167.cos_ref, f32[8,128,128]{2,1,0:T(8,128)} %get-tuple-element.168.sin_ref, f32[1,128]{1,0:T(1,128)} %bitcast.367, ...), custom_call_target="tpu_custom_call" | custom-call | tf_op jit(solution)/shard_map/pallas_call | solution.py:280
  977.4 26.8 %shard_map.231 = (bf16[8,128,768]{2,1,0:T(8,128)(2,1)}, f32[8,128]{1,0:T(8,128)}) custom-call(s32[8]{0:T(128)} %copy-done.21, s32[8]{0:T(128)} %copy-done.18, f32[8,128,768]{2,1,0:T(8,128)} %fusion.54.qkv_ref, f32[8,128,128]{2,1,0:T(8,128)} %get-tuple-element.167.cos_ref, f32[8,128,128]{2,1,0:T(8,128)} %get-tuple-element.168.sin_ref, f32[1,128]{1,0:T(1,128)} %bitcast.368, ...), custom_call_target="tpu_custom_call" | custom-call | tf_op jit(solution)/shard_map/pallas_call | solution.py:280
  1025.4 12.2 %fusion.16 = f32[1,768,2048]{2,1,0:T(8,128)} fusion(bf16[1152,2048]{1,0:T(8,128)(2,1)} %bitcast.67, bf16[1152,2048]{1,0:T(8,128)(2,1)} %bitcast.53, bf16[1152,768]{1,0:T(8,128)(2,1)S(1)} %copy-done.72, bf16[1152,768]{1,0:T(8,128)(2,1)S(1)} %copy-done.70), kind=kOutput, calls=%fused_computation.45 | convolution fusion | flops 7273709568 | bytes 19267584 | tf_op jit(solution)/shard_map/dot_general | solution.py:31
  1054.6 15.0 %collective-permute-done.52 = bf16[2,128,2048]{2,1,0:T(8,128)(2,1)} collective-permute-done((bf16[2,128,2048]{2,1,0:T(8,128)(2,1)}, bf16[2,128,2048]{2,1,0:T(8,128)(2,1)}, u32[]{:S(2)}, u32[]{:S(2)}) %collective-permute-start.52) | collective-permute-done | bytes 1048608 | tf_op jit(solution)/shard_map/ppermute | solution.py:362
  (527 shorter events, 520.7 us)
Async XLA Ops:
  7.2 88.1 %all-gather.3.cloned.1.call-start = ((), (), s32[]{:S(2)}) async-start(), calls=%async_computation.14 | async-start | bytes 3932160 | tf_op jit(solution)/shard_map/all_gather | solution.py:412
  10.5 114.8 %all-gather.5.cloned.1.call-start = ((), (), s32[]{:S(2)}) async-start(), calls=%async_computation.15 | async-start | bytes 2621440 | tf_op jit(solution)/shard_map/all_gather | solution.py:425
  32.1 34.3 %collective-permute-start = (bf16[128,2048]{1,0:T(8,128)(2,1)}, bf16[128,2048]{1,0:T(8,128)(2,1)}, u32[]{:S(2)}, u32[]{:S(2)}) collective-permute-start(bf16[128,2048]{1,0:T(8,128)(2,1)} %get-tuple-element.135), channel_id=1, source_target_pairs={{0,4},{1,5},{2,6},{3,7},{4,0},{5,1},{6,2},{7,3},{8,12},{9,13},{10,... | collective-permute-start | bytes 1572872 | tf_op jit(solution)/shard_map/ppermute | solution.py:342
  59.9 35.4 %collective-permute-start.17 = (bf16[4,128,2048]{2,1,0:T(8,128)(2,1)}, bf16[4,128,2048]{2,1,0:T(8,128)(2,1)}, u32[]{:S(2)}, u32[]{:S(2)}) collective-permute-start(bf16[4,128,2048]{2,1,0:T(8,128)(2,1)} %pad_maximum_fusion.14), channel_id=1, source_target_pairs={{0,2},{1,3},{2,0},{3,1},{4,6},{5,7},{6,4},{7,5},{8,10},{9,11},{10,... | collective-permute-start | bytes 6291464 | tf_op jit(solution)/shard_map/ppermute | solution.py:344
  95.2 37.4 %collective-permute-start.2 = (bf16[4,128,2048]{2,1,0:T(8,128)(2,1)}, bf16[4,128,2048]{2,1,0:T(8,128)(2,1)}, u32[]{:S(2)}, u32[]{:S(2)}) collective-permute-start(bf16[4,128,2048]{2,1,0:T(8,128)(2,1)} %pad_maximum_fusion.13), channel_id=1, source_target_pairs={{0,2},{1,3},{2,0},{3,1},{4,6},{5,7},{6,4},{7,5},{8,10},{9,11},{10,... | collective-permute-start | bytes 6291464 | tf_op jit(solution)/shard_map/ppermute | solution.py:344
  132.2 54.3 %collective-permute-start.18 = (bf16[4,128,2048]{2,1,0:T(8,128)(2,1)}, bf16[4,128,2048]{2,1,0:T(8,128)(2,1)}, u32[]{:S(2)}, u32[]{:S(2)}) collective-permute-start(bf16[4,128,2048]{2,1,0:T(8,128)(2,1)} %bitcast.38), channel_id=1, source_target_pairs={{0,2},{1,3},{2,0},{3,1},{4,6},{5,7},{6,4},{7,5},{8,10},{9,11},{10,... | collective-permute-start | bytes 6291464 | tf_op jit(solution)/shard_map/ppermute | solution.py:362
  226.8 64.5 %all-to-all-start.4 = ((bf16[8,144,2048]{2,1,0:T(8,128)(2,1)}), bf16[8,144,2048]{2,1,0:T(8,128)(2,1)}, u32[]{:S(2)}, u32[]{:S(2)}) async-start(bf16[8,144,2048]{2,1,0:T(8,128)(2,1)} %bitcast.386), calls=%async_computation.4 | async-start | bytes 9437184 | tf_op jit(solution)/shard_map/all_to_all | solution.py:368
  291.3 61.7 %all-to-all-start = ((bf16[8,144,2176]{2,1,0:T(8,128)(2,1)}), bf16[8,144,2176]{2,1,0:T(8,128)(2,1)}, u32[]{:S(2)}, u32[]{:S(2)}) async-start(bf16[8,144,2176]{2,1,0:T(8,128)(2,1)} %bitcast.384), calls=%async_computation | async-start | bytes 10027008 | tf_op jit(solution)/shard_map/all_to_all | solution.py:368
  353.0 61.7 %all-to-all-start.2 = ((bf16[8,144,2176]{2,1,0:T(8,128)(2,1)}), bf16[8,144,2176]{2,1,0:T(8,128)(2,1)}, u32[]{:S(2)}, u32[]{:S(2)}) async-start(bf16[8,144,2176]{2,1,0:T(8,128)(2,1)} %bitcast.385), calls=%async_computation.2 | async-start | bytes 10027008 | tf_op jit(solution)/shard_map/all_to_all | solution.py:368
  414.7 58.5 %all-to-all-start.6 = ((bf16[8,144,2048]{2,1,0:T(8,128)(2,1)}), bf16[8,144,2048]{2,1,0:T(8,128)(2,1)}, u32[]{:S(2)}, u32[]{:S(2)}) async-start(bf16[8,144,2048]{2,1,0:T(8,128)(2,1)} %bitcast.388), calls=%async_computation.6 | async-start | bytes 9437184 | tf_op jit(solution)/shard_map/all_to_all | solution.py:368
  473.2 58.9 %all-to-all-start.1 = ((bf16[8,144,2048]{2,1,0:T(8,128)(2,1)}), bf16[8,144,2048]{2,1,0:T(8,128)(2,1)}, u32[]{:S(2)}, u32[]{:S(2)}) async-start(bf16[8,144,2048]{2,1,0:T(8,128)(2,1)} %bitcast.389), calls=%async_computation.1 | async-start | bytes 9437184 | tf_op jit(solution)/shard_map/all_to_all | solution.py:368
  532.1 58.8 %all-to-all-start.3 = ((bf16[8,144,2048]{2,1,0:T(8,128)(2,1)}), bf16[8,144,2048]{2,1,0:T(8,128)(2,1)}, u32[]{:S(2)}, u32[]{:S(2)}) async-start(bf16[8,144,2048]{2,1,0:T(8,128)(2,1)} %bitcast.387), calls=%async_computation.3 | async-start | bytes 9437184 | tf_op jit(solution)/shard_map/all_to_all | solution.py:368
  590.9 61.8 %all-to-all-start.5 = ((bf16[8,144,2176]{2,1,0:T(8,128)(2,1)}), bf16[8,144,2176]{2,1,0:T(8,128)(2,1)}, u32[]{:S(2)}, u32[]{:S(2)}) async-start(bf16[8,144,2176]{2,1,0:T(8,128)(2,1)} %bitcast.376), calls=%async_computation.5 | async-start | bytes 10027008 | tf_op jit(solution)/shard_map/all_to_all | solution.py:368
  652.7 61.8 %all-to-all-start.7 = ((bf16[8,144,2176]{2,1,0:T(8,128)(2,1)}), bf16[8,144,2176]{2,1,0:T(8,128)(2,1)}, u32[]{:S(2)}, u32[]{:S(2)}) async-start(bf16[8,144,2176]{2,1,0:T(8,128)(2,1)} %bitcast.375), calls=%async_computation.7 | async-start | bytes 10027008 | tf_op jit(solution)/shard_map/all_to_all | solution.py:368
  657.5 433.8 %reduce-scatter.5.cloned.1.call-start = ((), (), s32[]{:S(2)}) async-start(), calls=%async_computation.17 | async-start | bytes 2621440 | tf_op jit(solution)/shard_map/reduce_scatter | solution.py:605
  664.0 58.0 %collective-permute-start.12 = (bf16[128,2048]{1,0:T(8,128)(2,1)}, bf16[128,2048]{1,0:T(8,128)(2,1)}, u32[]{:S(2)}, u32[]{:S(2)}) collective-permute-start(bf16[128,2048]{1,0:T(8,128)(2,1)} %slice.338), channel_id=1, source_target_pairs={{24,8},{16,24},{0,16},{8,0},{25,9},{17,25},{1,17},{9,1},{26,10},{1... | collective-permute-start | bytes 1572872 | tf_op jit(solution)/shard_map/ppermute | solution.py:321
  671.9 54.0 %collective-permute-start.27 = (bf16[128,2048]{1,0:T(8,128)(2,1)}, bf16[128,2048]{1,0:T(8,128)(2,1)}, u32[]{:S(2)}, u32[]{:S(2)}) collective-permute-start(bf16[128,2048]{1,0:T(8,128)(2,1)} %slice.350), channel_id=1, source_target_pairs={{24,8},{16,24},{0,16},{8,0},{25,9},{17,25},{1,17},{9,1},{26,10},{1... | collective-permute-start | bytes 1572872 | tf_op jit(solution)/shard_map/ppermute | solution.py:321
  681.4 45.7 %collective-permute-start.33 = (bf16[128,2176]{1,0:T(8,128)(2,1)}, bf16[128,2176]{1,0:T(8,128)(2,1)S(1)}, u32[]{:S(2)}, u32[]{:S(2)}) collective-permute-start(bf16[128,2176]{1,0:T(8,128)(2,1)} %slice.354), channel_id=1, source_target_pairs={{24,8},{16,24},{0,16},{8,0},{25,9},{17,25},{1,17},{9,1},{26,10},{1... | collective-permute-start | bytes 1671176 | tf_op jit(solution)/shard_map/ppermute | solution.py:321
  727.0 31.6 %collective-permute-start.28 = (bf16[128,2048]{1,0:T(8,128)(2,1)S(1)}, bf16[128,2048]{1,0:T(8,128)(2,1)S(1)}, u32[]{:S(2)}, u32[]{:S(2)}) collective-permute-start(bf16[128,2048]{1,0:T(8,128)(2,1)S(1)} %add_convert_fusion.17), channel_id=1, source_target_pairs={{24,8},{16,24},{0,16},{8,0},{25,9},{17,25},{1,17},{9,1},{26,10},{1... | collective-permute-start | bytes 1572872 | tf_op jit(solution)/shard_map/ppermute | solution.py:321
  727.2 43.3 %collective-permute-start.34 = (bf16[128,2176]{1,0:T(8,128)(2,1)S(1)}, bf16[128,2176]{1,0:T(8,128)(2,1)S(1)}, u32[]{:S(2)}, u32[]{:S(2)}) collective-permute-start(bf16[128,2176]{1,0:T(8,128)(2,1)S(1)} %add_convert_fusion.11), channel_id=1, source_target_pairs={{24,8},{16,24},{0,16},{8,0},{25,9},{17,25},{1,17},{9,1},{26,10},{1... | collective-permute-start | bytes 1671176 | tf_op jit(solution)/shard_map/ppermute | solution.py:321
  736.3 46.2 %collective-permute-start.46 = (bf16[128,2176]{1,0:T(8,128)(2,1)S(1)}, bf16[128,2176]{1,0:T(8,128)(2,1)S(1)}, u32[]{:S(2)}, u32[]{:S(2)}) collective-permute-start(bf16[128,2176]{1,0:T(8,128)(2,1)S(1)} %add_convert_fusion.8), channel_id=1, source_target_pairs={{24,8},{16,24},{0,16},{8,0},{25,9},{17,25},{1,17},{9,1},{26,10},{1... | collective-permute-start | bytes 1671176 | tf_op jit(solution)/shard_map/ppermute | solution.py:321
  747.5 81.4 %collective-permute-start.14 = (bf16[128,2048]{1,0:T(8,128)(2,1)S(1)}, bf16[128,2048]{1,0:T(8,128)(2,1)S(1)}, u32[]{:S(2)}, u32[]{:S(2)}) collective-permute-start(bf16[128,2048]{1,0:T(8,128)(2,1)S(1)} %add_convert_fusion.21), channel_id=1, source_target_pairs={{24,8},{16,24},{0,16},{8,0},{25,9},{17,25},{1,17},{9,1},{26,10},{1... | collective-permute-start | bytes 1572872 | tf_op jit(solution)/shard_map/ppermute | solution.py:321
  758.8 72.1 %collective-permute-start.29 = (bf16[128,2048]{1,0:T(8,128)(2,1)S(1)}, bf16[128,2048]{1,0:T(8,128)(2,1)S(1)}, u32[]{:S(2)}, u32[]{:S(2)}) collective-permute-start(bf16[128,2048]{1,0:T(8,128)(2,1)S(1)} %add_convert_fusion.16), channel_id=1, source_target_pairs={{24,8},{16,24},{0,16},{8,0},{25,9},{17,25},{1,17},{9,1},{26,10},{1... | collective-permute-start | bytes 1572872 | tf_op jit(solution)/shard_map/ppermute | solution.py:321
  770.7 46.2 %collective-permute-start.35 = (bf16[128,2176]{1,0:T(8,128)(2,1)S(1)}, bf16[128,2176]{1,0:T(8,128)(2,1)S(1)}, u32[]{:S(2)}, u32[]{:S(2)}) collective-permute-start(bf16[128,2176]{1,0:T(8,128)(2,1)S(1)} %add_convert_fusion.10), channel_id=1, source_target_pairs={{24,8},{16,24},{0,16},{8,0},{25,9},{17,25},{1,17},{9,1},{26,10},{1... | collective-permute-start | bytes 1671176 | tf_op jit(solution)/shard_map/ppermute | solution.py:321
  782.7 45.2 %collective-permute-start.47 = (bf16[128,2176]{1,0:T(8,128)(2,1)S(1)}, bf16[128,2176]{1,0:T(8,128)(2,1)S(1)}, u32[]{:S(2)}, u32[]{:S(2)}) collective-permute-start(bf16[128,2176]{1,0:T(8,128)(2,1)S(1)} %add_convert_fusion.7), channel_id=1, source_target_pairs={{24,8},{16,24},{0,16},{8,0},{25,9},{17,25},{1,17},{9,1},{26,10},{1... | collective-permute-start | bytes 1671176 | tf_op jit(solution)/shard_map/ppermute | solution.py:321
  847.7 37.8 %collective-permute-start.37 = (bf16[2,128,2048]{2,1,0:T(8,128)(2,1)}, bf16[2,128,2048]{2,1,0:T(8,128)(2,1)}, u32[]{:S(2)}, u32[]{:S(2)}) collective-permute-start(bf16[2,128,2048]{2,1,0:T(8,128)(2,1)} %pad_maximum_fusion.20), channel_id=1, source_target_pairs={{0,1},{1,0},{2,3},{3,2},{4,5},{5,4},{6,7},{7,6},{8,9},{9,8},{10,11... | collective-permute-start | bytes 3145736 | tf_op jit(solution)/shard_map/ppermute | solution.py:343
  848.4 34.1 %collective-permute-start.48 = (bf16[128,2048]{1,0:T(8,128)(2,1)}, bf16[128,2048]{1,0:T(8,128)(2,1)S(1)}, u32[]{:S(2)}, u32[]{:S(2)}) collective-permute-start(bf16[128,2048]{1,0:T(8,128)(2,1)} %get-tuple-element.124), channel_id=1, source_target_pairs={{0,1},{1,0},{2,3},{3,2},{4,5},{5,4},{6,7},{7,6},{8,9},{9,8},{10,11... | collective-permute-start | bytes 1572872 | tf_op jit(solution)/shard_map/ppermute | solution.py:342
  886.9 32.9 %collective-permute-start.38 = (bf16[4,128,2048]{2,1,0:T(8,128)(2,1)S(1)}, bf16[4,128,2048]{2,1,0:T(8,128)(2,1)S(1)}, u32[]{:S(2)}, u32[]{:S(2)}) collective-permute-start(bf16[4,128,2048]{2,1,0:T(8,128)(2,1)S(1)} %pad_maximum_fusion.15), channel_id=1, source_target_pairs={{0,2},{1,3},{2,0},{3,1},{4,6},{5,7},{6,4},{7,5},{8,10},{9,11},{10,... | collective-permute-start | bytes 6291464 | tf_op jit(solution)/shard_map/ppermute | solution.py:344
  930.4 173.9 %reduce-scatter.3.cloned.1.call-start = ((), (), s32[]{:S(2)}) async-start(), calls=%async_computation.16 | async-start | bytes 3932160 | tf_op jit(solution)/shard_map/reduce_scatter | solution.py:605
  972.4 65.4 %collective-permute-start.51 = (bf16[4,128,2048]{2,1,0:T(8,128)(2,1)}, bf16[4,128,2048]{2,1,0:T(8,128)(2,1)}, u32[]{:S(2)}, u32[]{:S(2)}) collective-permute-start(bf16[4,128,2048]{2,1,0:T(8,128)(2,1)} %bitcast.76), channel_id=1, source_target_pairs={{0,2},{1,3},{2,0},{3,1},{4,6},{5,7},{6,4},{7,5},{8,10},{9,11},{10,... | collective-permute-start | bytes 6291464 | tf_op jit(solution)/shard_map/ppermute | solution.py:362
  1041.3 28.3 %collective-permute-start.52 = (bf16[2,128,2048]{2,1,0:T(8,128)(2,1)}, bf16[2,128,2048]{2,1,0:T(8,128)(2,1)}, u32[]{:S(2)}, u32[]{:S(2)}) collective-permute-start(bf16[2,128,2048]{2,1,0:T(8,128)(2,1)} %slice.379), channel_id=1, source_target_pairs={{0,4},{1,5},{2,6},{3,7},{4,0},{5,1},{6,2},{7,3},{8,12},{9,13},{10,... | collective-permute-start | bytes 3145736 | tf_op jit(solution)/shard_map/ppermute | solution.py:362
  1046.5 28.7 %collective-permute-start.40 = (bf16[2,128,2048]{2,1,0:T(8,128)(2,1)}, bf16[2,128,2048]{2,1,0:T(8,128)(2,1)}, u32[]{:S(2)}, u32[]{:S(2)}) collective-permute-start(bf16[2,128,2048]{2,1,0:T(8,128)(2,1)} %slice.365), channel_id=1, source_target_pairs={{0,1},{1,0},{2,3},{3,2},{4,5},{5,4},{6,7},{7,6},{8,9},{9,8},{10,11... | collective-permute-start | bytes 3145736 | tf_op jit(solution)/shard_map/ppermute | solution.py:362
  (146 other events, 2816.6 us)
Sparse Core Ops, SparseCore 0:
  10.6 66.1 all-gather.2
  79.0 44.5 all-gather.4
  930.5 44.2 reduce-scatter.4
  1017.7 63.5 reduce-scatter.2

commit v2 on v1

--- a/solution.py
+++ b/solution.py
@@ -5,6 +5,7 @@
 import jax.numpy as jnp
 from jax import lax
 from jax.experimental import pallas as pl
+from jax.experimental.layout import Layout, with_layout_constraint
 from jax.experimental.pallas import tpu as pltpu
 from jax.sharding import PartitionSpec as P
 
@@ -13,6 +14,7 @@
 HEAD_DIM = 128
 EPSILON = 1e-06
 NEG_FILL = -1e30
+LOG2E = 1.4426950408889634
 PLANE = ("blk", "head")
 EVERY = ("dp", "blk", "head")
 F32 = jnp.float32
@@ -56,13 +58,16 @@
 
 def fill_keys(heads, order_ref, qkv_ref, cos_ref, sin_ref, k_gain_ref, k_scr, v_scr):
     start = heads * HEAD_DIM
+    if v_scr.shape[2] > HEAD_DIM:
+        v_scr[:, :, HEAD_DIM:] = jnp.ones_like(v_scr[:, :, HEAD_DIM:])
 
     def one(block, carry):
         place = order_ref[block]
         raw = qkv_ref[place, :, start : start + HEAD_DIM]
         turned, _, _ = head_forward(raw, k_gain_ref[...], cos_ref[block], sin_ref[block])
         k_scr[block] = turned.astype(BF16)
-        v_scr[block] = qkv_ref[place, :, start + HEAD_DIM : start + 2 * HEAD_DIM].astype(BF16)
+        values = qkv_ref[place, :, start + HEAD_DIM : start + 2 * HEAD_DIM].astype(BF16)
+        v_scr[block, :, :HEAD_DIM] = values
         return carry
 
     lax.fori_loop(0, qkv_ref.shape[0], one, 0)
@@ -110,32 +115,21 @@
     row_seg = seg_col_ref[block]
 
     def step(key_block, carry):
-        top, total, acc = carry
-        scores = dot_nt(queries, k_scr[key_block]) * score_scale
+        scores = dot_nt(queries, k_scr[key_block]) * (score_scale * LOG2E)
         scores = scores + allowed_keys(row_seg, seg_row_ref[key_block], block, key_block, heads)
-        new_top = jnp.maximum(top, jnp.max(scores, axis=1, keepdims=True))
-        shrink = jnp.exp(top - new_top)
-        weights = jnp.exp(scores - new_top)
-        total = total * shrink + jnp.sum(weights, axis=1, keepdims=True)
-        acc = acc * shrink + dot_nn(weights.astype(BF16), v_scr[key_block])
-        return new_top, total, acc
-
-    first = step(
-        block,
-        (
-            jnp.full((count, 1), NEG_FILL, F32),
-            jnp.zeros((count, 1), F32),
-            jnp.zeros((count, HEAD_DIM), F32),
-        ),
-    )
-    top, total, acc = lax.fori_loop(low_ref[block], block, step, first)
+        return carry + dot_nn(jnp.exp2(scores).astype(BF16), v_scr[key_block])
+
+    both = lax.fori_loop(
+        low_ref[block], block + 1, step, jnp.zeros((count, 2 * HEAD_DIM), F32)
+    )
+    acc, total = both[:, :HEAD_DIM], both[:, HEAD_DIM:]
     acc = acc / total
     size = attn_ref.shape[1]
     for h in range(heads):
         attn_ref[0, :, h * HEAD_DIM : (h + 1) * HEAD_DIM] = acc[h * size : (h + 1) * size].astype(
             BF16
         )
-    stat_ref[0] = jnp.broadcast_to(top + jnp.log(total), (count, HEAD_DIM))
+    stat_ref[0] = jnp.log2(total)
 
 
 def attend_back_kernel(
@@ -193,9 +187,9 @@
 
     def step(key_block, acc):
         keys, values = k_scr[key_block], v_scr[key_block]
-        scores = dot_nt(queries, keys) * score_scale
+        scores = dot_nt(queries, keys) * (score_scale * LOG2E)
         scores = scores + allowed_keys(row_seg, seg_row_ref[key_block], block, key_block, heads)
-        probs = jnp.exp(scores - stat)
+        probs = jnp.exp2(scores - stat)
         grad_probs = dot_nt(grad_rows, values)
         grad_scores = (probs * (grad_probs - delta)).astype(BF16)
         dk_scr[key_block] += dot_tn(grad_scores, queries)
@@ -264,13 +258,19 @@
                 row_block((1, size, heads * HEAD_DIM)),
                 row_block((1, heads * size, HEAD_DIM)),
             ],
-            scratch_shapes=[pltpu.VMEM((blocks, size, HEAD_DIM), BF16)] * 2,
+            scratch_shapes=[
+                pltpu.VMEM((blocks, size, HEAD_DIM), BF16),
+                pltpu.VMEM((blocks, size, 2 * HEAD_DIM), BF16),
+            ],
         ),
         out_shape=[
             jax.ShapeDtypeStruct((blocks, size, heads * HEAD_DIM), BF16),
             jax.ShapeDtypeStruct((blocks, heads * size, HEAD_DIM), F32),
         ],
         compiler_params=pltpu.CompilerParams(vmem_limit_bytes=48 * 2**20),
+        cost_estimate=pl.CostEstimate(
+            flops=2**24 * blocks * heads, bytes_accessed=qkv.size * 8, transcendentals=0
+        ),
     )(order, low, *arrays)
 
 
@@ -297,7 +297,100 @@
             jax.ShapeDtypeStruct((8, HEAD_DIM), F32),
         ],
         compiler_params=pltpu.CompilerParams(vmem_limit_bytes=56 * 2**20),
+        cost_estimate=pl.CostEstimate(
+            flops=2**24 * blocks * heads * 2, bytes_accessed=qkv.size * 12, transcendentals=0
+        ),
     )(order, low, *arrays, attn, grad, stat)
+
+
+def expert_kernel(
+    experts,
+    expert_ref,
+    rows_ref,
+    gates_ref,
+    cot_ref,
+    gate_w_ref,
+    up_w_ref,
+    down_w_ref,
+    gated_ref,
+    grad_gate_ref,
+    grad_up_ref,
+    back_ref,
+    out_ref,
+):
+    width = rows_ref.shape[1]
+    rows = rows_ref[...]
+    spots = lax.broadcasted_iota(jnp.int32, gates_ref.shape, 1)
+    coarse_spot = spots == expert_ref[0]
+    fine_spot = spots == expert_ref[0] + experts
+    gate = jnp.sum(
+        jnp.where(coarse_spot | fine_spot, gates_ref[...].astype(F32), 0.0), axis=1, keepdims=True
+    )
+    gate_pre = dot_nn(rows, gate_w_ref[...])
+    up_pre = dot_nn(rows, up_w_ref[...])
+    pulled = dot_nt(cot_ref[...], down_w_ref[...])
+    sigma = 1.0 / (1.0 + jnp.exp(-gate_pre))
+    swish = gate_pre * sigma
+    hidden = (swish * up_pre).astype(BF16).astype(F32)
+    gate_grad = jnp.sum(hidden * pulled, axis=1, keepdims=True)
+    gated = (hidden * gate).astype(BF16)
+    grad_hidden = pulled * gate
+    grad_gate = (grad_hidden * up_pre * (sigma + swish * (1.0 - sigma))).astype(BF16)
+    grad_up = (grad_hidden * swish).astype(BF16)
+    gated_ref[...] = gated
+    grad_gate_ref[...] = grad_gate
+    grad_up_ref[...] = grad_up
+    back_ref[:, :width] = (
+        dot_nt(grad_gate, gate_w_ref[...]) + dot_nt(grad_up, up_w_ref[...])
+    ).astype(BF16)
+    coarse = gate_grad.astype(BF16).astype(F32)
+    back_ref[:, width:] = jnp.where(
+        coarse_spot, coarse, jnp.where(fine_spot, gate_grad - coarse, 0.0)
+    ).astype(BF16)
+    out_ref[...] = dot_nn(gated, down_w_ref[...]).astype(BF16)
+
+
+def expert_pass(came, cot, gate_w, up_w, down_w, expert_id, experts):
+    count, full = came.shape
+    width, hidden = gate_w.shape
+    block = max(b for b in range(16, 385, 16) if count % b == 0)
+    extra = full - width
+
+    def rows_of(columns, place=0):
+        return pl.BlockSpec((block, columns), lambda i, e: (i, place))
+
+    def kept(shape):
+        return pl.BlockSpec(shape, lambda i, e: (0, 0), pipeline_mode=pl.Buffered(1))
+
+    return pl.pallas_call(
+        functools.partial(expert_kernel, experts),
+        grid_spec=pltpu.PrefetchScalarGridSpec(
+            num_scalar_prefetch=1,
+            grid=(count // block,),
+            in_specs=[
+                rows_of(width),
+                rows_of(extra, width // extra),
+                rows_of(width),
+                kept(gate_w.shape),
+                kept(up_w.shape),
+                kept(down_w.shape),
+            ],
+            out_specs=[rows_of(hidden)] * 3 + [rows_of(full), rows_of(width)],
+        ),
+        out_shape=[jax.ShapeDtypeStruct((count, hidden), BF16)] * 3
+        + [
+            jax.ShapeDtypeStruct((count, full), BF16),
+            jax.ShapeDtypeStruct((count, width), BF16),
+        ],
+        compiler_params=pltpu.CompilerParams(vmem_limit_bytes=58 * 2**20),
+        cost_estimate=pl.CostEstimate(
+            flops=count * width * hidden * 3, bytes_accessed=count * width * 4, transcendentals=0
+        ),
+    )(expert_id.reshape(1), came, came, cot, gate_w, up_w, down_w)
+
+
+def by_rows(array):
+    return with_layout_constraint(array, Layout(major_to_minor=tuple(range(array.ndim))))
 
 
 def ring_steps(ways):
@@ -313,14 +406,57 @@
     return jnp.concatenate(out, axis=0)
 
 
-def line_reduce(parts, ways):
+def ring_jumps(ways, count):
+    ring = [a for a, _ in ring_steps(ways)]
+    return [(ring[i], ring[(i + count) % ways]) for i in range(ways)]
+
+
+def line_spread(rows, ways):
+    blocks = [lax.ppermute(rows, "dp", ring_jumps(ways, k)) for k in range(1, ways)]
+    return jnp.concatenate([rows] + blocks, axis=0)
+
+
+def line_sum(parts, ways):
     size = parts.shape[0] // ways
+    total = parts[:size].astype(F32)
+    for k in range(1, ways):
+        part = parts[k * size : (k + 1) * size]
+        total = total + lax.ppermute(part, "dp", ring_jumps(ways, -k)).astype(F32)
+    return total
+
+
+def line_reduce(part, ways):
     back = [(b, a) for a, b in ring_steps(ways)]
-    acc = parts[(ways - 1) * size :]
+    acc = part(ways - 1)
     for k in range(ways - 2, -1, -1):
         acc = lax.ppermute(acc, "dp", back)
-        acc = (acc.astype(F32) + parts[k * size : (k + 1) * size].astype(F32)).astype(BF16)
-    return acc
+        acc = yield (acc.astype(F32) + part(k).astype(F32)).astype(BF16)
+
+
+def plane_gather_steps(rows, turn, pair):
+    if not pair:
+        yield lax.all_gather(rows, PLANE, axis=0, tiled=False)
+        return
+    first, second = plane_flips(turn)
+    two = yield jnp.stack([rows, lax.ppermute(rows, PLANE, first)])
+    four = yield jnp.concatenate([two, lax.ppermute(two, PLANE, second)])
+    yield jnp.concatenate([four, lax.ppermute(four, PLANE, flips(2))])
+
+
+def together(*moves):
+    held = [next(move) for move in moves]
+    while True:
+        if len(held) > 1:
+            held = [by_rows(h) for h in tie(*held)]
+        after = []
+        for move, value in zip(moves, held):
+            try:
+                after.append(move.send(value))
+            except StopIteration:
+                after.append(value)
+        if all(a is b for a, b in zip(after, held)):
+            return held
+        held = after
 
 
 def paired(blk_ways, head_ways):
@@ -333,15 +469,6 @@
 
 def plane_flips(turn):
     return (flips(4), flips(1)) if turn % 2 == 0 else (flips(1), flips(4))
-
-
-def plane_gather(rows, turn, pair):
-    if not pair:
-        return lax.all_gather(rows, PLANE, axis=0, tiled=False)
-    first, second = plane_flips(turn)
-    two = jnp.stack([rows, lax.ppermute(rows, PLANE, first)])
-    four = jnp.concatenate([two, lax.ppermute(two, PLANE, second)])
-    return jnp.concatenate([four, lax.ppermute(four, PLANE, flips(2))])
 
 
 def plane_order(plane_index, plane_ways, turn, pair):
@@ -354,14 +481,27 @@
     return (core * 4 + far * 2 + near).astype(jnp.int32)
 
 
-def plane_reduce(parts, turn, pair):
+def plane_reduce(product, turn, pair):
     if not pair:
-        return lax.psum_scatter(parts, PLANE, scatter_dimension=0, tiled=False)
+        yield lax.psum_scatter(product(0, None), PLANE, scatter_dimension=0, tiled=False)
+        return
     first, second = plane_flips(turn)
-    for half, move in ((4, flips(2)), (2, second), (1, first)):
+    away = lax.ppermute(product(4, 8), PLANE, flips(2))
+    parts = yield (product(0, 4).astype(F32) + away.astype(F32)).astype(BF16)
+    for half, move in ((2, second), (1, first)):
         came = lax.ppermute(parts[half:], PLANE, move)
         parts = (parts[:half].astype(F32) + came.astype(F32)).astype(BF16)
-    return parts[0]
+        if half > 1:
+            parts = yield parts
+    yield parts[0]
+
+
+def tie(*arrays):
+    return lax.optimization_barrier(arrays)
+
+
+def every_exchange(rows):
+    return lax.all_to_all(rows, EVERY, split_axis=0, concat_axis=0, tiled=True)
 
 
 def plane_exchange(rows):
@@ -443,25 +583,46 @@
     ).astype(BF16)
     slot_ids = jnp.arange(dp_ways * capacity, dtype=jnp.int32)
 
-    def picks_of(route):
-        line_routes = line_gather(route, dp_ways)
-        chosen = jnp.any(line_routes[:, :, None] == expert_ids[None, None, :], axis=1)
+    spots = jnp.array([[a for a, _ in ring_steps(dp_ways)].index(i) for i in range(dp_ways)], jnp.int32)
+    ring_slots = (spots[dp_index] - spots) % dp_ways
+    ring = jnp.array([a for a, _ in ring_steps(dp_ways)], jnp.int32)
+    dp_index_of_slot = ring[(spots[dp_index] - jnp.arange(dp_ways)) % dp_ways]
+    line_routes = line_gather(routes.reshape(1, seqs * size, top_count), dp_ways)
+    line_routes = line_routes.reshape(dp_ways, seqs, size, top_count)
+
+    def picks_of(s):
+        seen = line_routes[:, s].reshape(dp_ways * size, top_count)
+        chosen = jnp.any(seen[:, :, None] == expert_ids[None, None, :], axis=1)
         chosen = chosen.reshape(dp_ways, size, plane_ways)
         ranks = jnp.einsum(
             "ij,zje->zie", before, chosen.astype(BF16), preferred_element_type=F32
         ).astype(jnp.int32)
         ranks = ranks + jnp.arange(dp_ways, dtype=jnp.int32)[:, None, None] * capacity
-        keys = jnp.where(chosen, ranks, -1).reshape(dp_ways * size, plane_ways).T
-        picks = (keys[:, None, :] == slot_ids[None, :, None]).astype(BF16)
-        return picks.reshape(plane_ways * dp_ways * capacity, dp_ways * size)
-
-    picks = [picks_of(routes[s]) for s in range(seqs)]
-
-    def dispatch(rows, s):
-        return plane_exchange(dot_nn(picks[s], line_gather(rows, dp_ways)).astype(BF16))
-
-    def collect(rows, s):
-        return line_reduce(dot_tn(picks[s], plane_exchange(rows)).astype(BF16), dp_ways)
+        keys = jnp.where(chosen, ranks, -1)
+
+        def table(keys):
+            keys = keys.reshape(dp_ways * size, plane_ways).T
+            picks = (keys[:, None, :] == slot_ids[None, :, None]).astype(BF16)
+            return picks.reshape(plane_ways * dp_ways * capacity, dp_ways * size)
+
+        return table(keys), table(jnp.take(keys, ring_slots, axis=0))
+
+    picks, straight_picks = zip(*[picks_of(s) for s in range(seqs)])
+
+    last = []
+
+    def exchange(rows, move=plane_exchange):
+        if last:
+            rows, _ = tie(rows, last.pop())
+        out = move(rows)
+        last.append(out)
+        return out
+
+    def pack(line_rows, table):
+        return dot_nn(table, line_rows).astype(BF16)
+
+    def unpack(rows, s):
+        return dot_tn(picks[s], rows).astype(BF16)
 
     orders, lows = [], []
     for s in range(seqs):
@@ -480,23 +641,40 @@
         inputs.append(rows)
         units.append(unit)
         scales.append(scale)
-        spread.append(plane_gather((unit * attn_gain_row).astype(BF16), s, pair))
-    cot_rows = [dispatch(cotangent[s], s) for s in range(seqs)]
-    projected, attended, stats, middles = [], [], [], []
+        spread.append(plane_gather_steps((unit * attn_gain_row).astype(BF16), s, pair))
+    *spread, qkv_local = tie(*together(*spread), qkv_local)
+    spread = [by_rows(rows) for rows in spread]
+
+    def times(left, right):
+        def product(start, stop):
+            rows = left[start:stop]
+            count = rows.shape[0]
+            out = dot_nt(rows.reshape(count * size, -1), right).astype(BF16)
+            return out.reshape(count, size, width)
+
+        return product
+
+    lines, held = [], out_local
+    for s in range(seqs):
+        rows, held = tie(cotangent[s], held)
+        held = line_spread(rows, dp_ways)
+        lines.append(pack(held, picks[s]))
+    projected, attended, stats, mixes = [], [], [], []
     for s in range(seqs):
         qkv = dot_nn(spread[s].reshape(seq_total, width), qkv_local)
         qkv = qkv.reshape(plane_ways, size, local_dim + 2 * HEAD_DIM)
         attn, stat = attend(qkv, tables, gains, segments[s], orders[s], lows[s], heads)
-        mixed = dot_nt(attn.reshape(seq_total, local_dim), out_local).astype(BF16)
-        mixed = plane_reduce(mixed.reshape(plane_ways, size, width), s, pair)
         projected.append(qkv)
         attended.append(attn)
         stats.append(stat)
-        middles.append(inputs[s] + mixed.astype(F32))
-
-    normed2s, mid_units, mid_scales, gate_tables, came = [], [], [], [], []
-    for s in range(seqs):
-        unit, scale = rms_parts(middles[s])
+        mixes.append(together(plane_reduce(times(attn, out_local), s, pair))[0])
+    lines[0], *mixes = tie(lines[0], *mixes)
+    cot_rows = [exchange(rows) for rows in lines]
+
+    middles, normed2s, mid_units, mid_scales, gate_tables, came = [], [], [], [], [], []
+    for s in range(seqs):
+        middle = inputs[s] + mixes[s].astype(F32)
+        unit, scale = rms_parts(middle)
         normed2 = (unit * ffn_gain_row).astype(BF16)
         logits = dot_nn(normed2, router_weight)
         chosen = jnp.any(
@@ -510,67 +688,71 @@
         payload = [normed2, coarse, fine]
         if extra > 2 * experts:
             payload.append(jnp.zeros((size, extra - 2 * experts), BF16))
+        middles.append(middle)
         normed2s.append(normed2)
         mid_units.append(unit)
         mid_scales.append(scale)
         gate_tables.append(gates)
-        came.append(dispatch(jnp.concatenate(payload, axis=1), s))
+        came.append(
+            exchange(pack(line_gather(jnp.concatenate(payload, axis=1), dp_ways), picks[s]))
+        )
 
     gate_w, up_w, down_w = gate_weight[0], up_weight[0], down_weight[0]
-    expert_id = dp_index * plane_ways + plane_index
-    extra_ids = jnp.arange(extra, dtype=jnp.int32)
-    mine_coarse = (extra_ids == expert_id).astype(F32)[None, :]
-    mine_fine = (extra_ids == experts + expert_id).astype(F32)[None, :]
-    mine = mine_coarse + mine_fine
-    kept = []
-    grad_backs, out_backs = [], []
-    for s in range(seqs):
-        rows = came[s][:, :width]
-        gate = jnp.sum(came[s][:, width:].astype(F32) * mine, axis=1, keepdims=True)
-        gate_pre = dot_nn(rows, gate_w)
-        up_pre = dot_nn(rows, up_w)
-        pulled = dot_nt(cot_rows[s], down_w)
-        sigma = 1.0 / (1.0 + jnp.exp(-gate_pre))
-        hidden = (gate_pre * sigma * up_pre).astype(BF16).astype(F32)
-        gate_grad_rows = jnp.sum(hidden * pulled, axis=1, keepdims=True)
-        gated = (hidden * gate).astype(BF16)
-        grad_hidden = pulled * gate
-        grad_gate = (grad_hidden * up_pre * sigma * (1.0 + gate_pre * (1.0 - sigma))).astype(BF16)
-        grad_up = (grad_hidden * gate_pre * sigma).astype(BF16)
-        grad_rows = (dot_nt(grad_gate, gate_w) + dot_nt(grad_up, up_w)).astype(BF16)
-        coarse = gate_grad_rows.astype(BF16)
-        fine = gate_grad_rows - coarse.astype(F32)
-        tail = (coarse.astype(F32) * mine_coarse + fine * mine_fine).astype(BF16)
-        grad_backs.append(collect(jnp.concatenate([grad_rows, tail], axis=1), s))
-        kept.append((rows, gated, cot_rows[s], grad_gate, grad_up))
-    for s in range(seqs):
-        out_backs.append(collect(dot_nn(kept[s][1], down_w).astype(BF16), s))
-    layer_out = jnp.stack(
-        [(middles[s] + out_backs[s].astype(F32)).astype(BF16) for s in range(seqs)]
-    )
-    every = [jnp.concatenate([kept[s][i] for s in range(seqs)], axis=0) for i in range(5)]
-    gate_grad = dot_tn(every[0], every[3])
-    up_grad = dot_tn(every[0], every[4])
-    down_grad = dot_tn(every[1], every[2])
-
-    grad_mids, grad_spread = [], []
+    expert_id = (dp_index * plane_ways + plane_index).astype(jnp.int32)
+    kept, grad_lines, produced = [], [], []
+    for s in range(seqs):
+        gated, grad_gate, grad_up, back, out = expert_pass(
+            came[s], cot_rows[s], gate_w, up_w, down_w, expert_id, experts
+        )
+        if s:
+            back, grad_lines[-1] = tie(back, grad_lines[-1])
+        grad_lines.append(exchange(back))
+        produced.append(out)
+        kept.append((came[s][:, :width], gated, cot_rows[s], grad_gate, grad_up))
+    out_lines, grad_mids, reduced = [], [], []
     router_grad = jnp.zeros((width, experts), F32)
     ffn_sum = jnp.zeros((width,), F32)
     for s in range(seqs):
-        tail = grad_backs[s][:, width:].astype(F32)
+        back = unpack(grad_lines[s], s)
+        if s == 0:
+            back, kept = tie(back, kept)
+        reduced.append(line_sum(back, dp_ways))
+    out_lines.append(exchange(produced[0]))
+    for s in range(seqs):
+        tail = reduced[s][:, width:]
         gates = gate_tables[s]
         grad_gates = tail[:, :experts] + tail[:, experts : 2 * experts]
         grad_logits = (
             gates * (grad_gates - jnp.sum(gates * grad_gates, axis=1, keepdims=True))
         ).astype(BF16)
         router_grad = router_grad + dot_tn(normed2s[s], grad_logits)
-        grad_normed2 = grad_backs[s][:, :width].astype(F32) + dot_nt(grad_logits, router_weight)
+        grad_normed2 = reduced[s][:, :width] + dot_nt(grad_logits, router_weight)
         ffn_sum = ffn_sum + jnp.sum(grad_normed2 * mid_units[s], axis=0)
-        grad_mid = cotangent[s].astype(F32) + rms_back(
-            grad_normed2, mid_units[s], mid_scales[s], ffn_gain_row
+        grad_mids.append(
+            cotangent[s].astype(F32)
+            + rms_back(grad_normed2, mid_units[s], mid_scales[s], ffn_gain_row)
         )
-        grad_mids.append(grad_mid)
-        grad_spread.append(plane_gather(grad_mid.astype(BF16), s, pair))
+
+    gate_grad = sum(dot_tn(rows, grad) for rows, _, _, grad, _ in kept)
+    up_grad = sum(dot_tn(rows, grad) for rows, _, _, _, grad in kept)
+    down_grad = sum(dot_tn(gated, cot) for _, gated, cot, _, _ in kept)
+    *grad_mids, out_lines[0], gate_grad, up_grad, down_grad = tie(
+        *grad_mids, out_lines[0], gate_grad, up_grad, down_grad
+    )
+    grad_spread = together(
+        *[plane_gather_steps(grad_mids[s].astype(BF16), s, pair) for s in range(seqs)]
+    )
+    devices = dp_ways * plane_ways
+
+    def outcome(s):
+        back = dot_tn(straight_picks[s], out_lines[s]).astype(BF16)
+        back = lax.psum_scatter(back, "dp", scatter_dimension=0, tiled=True)
+        return (middles[s] + back.astype(F32)).astype(BF16)
+
+    for s in range(1, seqs):
+        rows, *grad_spread = tie(produced[s], *grad_spread)
+        grad_spread = [by_rows(g) for g in grad_spread]
+        out_lines.append(exchange(rows))
     grad_qkvs, grad_ins = [], []
     head_sums = jnp.zeros((2, HEAD_DIM), F32)
     for s in range(seqs):
@@ -589,27 +771,54 @@
             stats[s],
         )
         head_sums = head_sums + sums[:2]
-        grad_qkv = grad_qkv.reshape(seq_total, local_dim + 2 * HEAD_DIM)
         grad_qkvs.append(grad_qkv)
-        grad_normed = dot_nt(grad_qkv, qkv_local).astype(BF16)
-        grad_normed = plane_reduce(grad_normed.reshape(plane_ways, size, width), s, pair)
-        grad_in = rms_back(grad_normed.astype(F32), units[s], scales[s], attn_gain_row)
-        grad_ins.append((grad_mids[s] + grad_in).astype(BF16))
-    input_grad = jnp.stack(grad_ins)
-
-    def shared_grad(lefts, rights):
-        total = sum(
+    *grad_qkvs, out_lines[-1] = tie(*grad_qkvs, out_lines[-1])
+    small = exchange(
+        jnp.concatenate(
+            [
+                router_grad.reshape(devices, -1),
+                ffn_sum.reshape(devices, -1),
+                head_sums[0].reshape(devices, -1),
+                head_sums[1].reshape(devices, -1),
+            ],
+            axis=1,
+        ),
+        every_exchange,
+    )
+
+    def total_over(lefts, rights):
+        return sum(
             dot_tn(a.reshape(seq_total, -1), b.reshape(seq_total, -1))
             for a, b in zip(lefts, rights)
         ).astype(BF16)
-        total = lax.psum_scatter(total, "dp", scatter_dimension=0, tiled=True)
+
+    total = total_over(spread, grad_qkvs)
+    *grad_normeds, qkv_rows = together(
+        *[plane_reduce(times(grad_qkvs[s], qkv_local), s, pair) for s in range(seqs)],
+        line_reduce(
+            lambda k: lax.dynamic_slice_in_dim(
+                total, dp_index_of_slot[k] * weight_rows, weight_rows
+            ),
+            dp_ways,
+        ),
+    )
+    for s in range(seqs):
+        grad_in = rms_back(grad_normeds[s].astype(F32), units[s], scales[s], attn_gain_row)
+        grad_ins.append((grad_mids[s] + grad_in).astype(BF16))
+    input_grad = jnp.stack(grad_ins)
+    layer_out = jnp.stack([outcome(s) for s in range(seqs)])
+
+    def rows_of_plane(total):
         return plane_exchange(total).reshape(plane_ways, weight_rows // plane_ways, -1)
 
     def side_by_side(pieces):
         return pieces.transpose(1, 0, 2).reshape(pieces.shape[1], -1)
 
-    out_grad = side_by_side(shared_grad(grad_spread, attended)).astype(F32)
-    pieces = shared_grad(spread, grad_qkvs).astype(F32)
+    out_total = lax.psum_scatter(
+        total_over(grad_spread, attended), "dp", scatter_dimension=0, tiled=True
+    )
+    out_grad = side_by_side(rows_of_plane(out_total)).astype(F32)
+    pieces = rows_of_plane(qkv_rows).astype(F32)
     row_count = pieces.shape[1]
 
     def kv_columns(start):
@@ -632,21 +841,8 @@
     )
     attn_gain_grad = jnp.sum(own_rows.astype(F32) * qkv_grad, axis=1) / own_gain
 
-    def every_reduce(parts):
-        return jnp.sum(
-            lax.all_to_all(parts, EVERY, split_axis=0, concat_axis=0, tiled=True), axis=0
-        )
-
-    devices = dp_ways * plane_ways
-    small = every_reduce(
-        jnp.concatenate(
-            [router_grad.reshape(devices, -1), ffn_sum.reshape(devices, -1)], axis=1
-        )
-    )
-    head_small = every_reduce(
-        head_sums.reshape(2, devices, -1).transpose(1, 0, 2).reshape(devices, -1)
-    )
-    head_small = head_small.reshape(2, -1)
+    small = jnp.sum(small, axis=0)
+    head_small = small[-2 * (HEAD_DIM // devices) :].reshape(2, -1)
     cut = row_count * experts
     return (
         layer_out,
@@ -656,7 +852,7 @@
         head_small[0],
         head_small[1],
         out_grad,
-        small[cut:],
+        small[cut : cut + row_count],
         small[:cut].reshape(row_count, experts),
         gate_grad[None],
         up_grad[None],

time: 1140 us -> 950 us (0.83)
  waiting for transfers between devices: 550 us -> 401 us
  matrix products: 226 us -> 150 us
  Pallas kernels: 92.2 us -> 151 us
  other arithmetic: 80.5 us -> 67.5 us
    all_to_all x10, waiting for transfers between devices: 182 us -> 74.4 us  [plane_exchange(): return lax.all_to_all(rows, PLANE, split_axis=0, concat_axis=0, tiled=True)]
    ppermute x12 -> x28, waiting for transfers between devices: 102 us -> 182 us  [the longest x6 78.9 us: line_spread(): lax.ppermute(rows, 'dp', ring_jumps(ways, k))]
    ppermute x12 -> x3, waiting for transfers between devices: 86 us -> 19.6 us  [line_reduce(): acc = lax.ppermute(acc, 'dp', back)]
    pallas_call x0 -> x2, Pallas kernels: none -> 60.2 us  [expert_pass(): pl.pallas_call(functools.partial(expert_kernel, experts), grid_spec=pltpu...]
    ppermute x18 -> x9, waiting for transfers between devices: 143 us -> 95.1 us  [line_gather(): held = lax.ppermute(held, 'dp', ring_steps(ways))]
    dot_general x12 -> x10, matrix products: 60.7 us -> 18.1 us  [dot_nt(): lax.dot_general(a, b, (((1,), (1,)), ((), ())), preferred_element_type=F32)]
    dot_general x16 -> x10, matrix products: 84.9 us -> 47.6 us  [dot_nn(): return jnp.dot(a, b, preferred_element_type=F32)]
    ppermute x12 -> x8, waiting for transfers between devices: 32.6 us -> 17 us  [plane_reduce(): came = lax.ppermute(parts[half:], PLANE, move)]
  transfers between devices with their start and end apart: 70 -> 64, of which waited for: 40 -> 39; matrix products, arithmetic and copies ran while one was open for 29% -> 25% of each run, Pallas kernels for 8% -> 16%
where the time goes in v2:
time: 950 us; the launch traced here: 943 us
  waiting for transfers between devices  401 us (42%)
  Pallas kernels  151 us (16%)
  matrix products  150 us (16%)
  starting transfers between devices  109 us (11%)
  other arithmetic  67.5 us (7%)
  local copies, waits for them, and re-layouts  45.9 us (5%)
  between operations  18.6 us (2%)
    ppermute x9, waiting for transfers between devices, line_gather(): held = lax.ppermute(held, 'dp', ring_steps(ways))  95.1 us
    dot_general x16, matrix products, dot_tn(): lax.dot_general(a, b, (((0,), (0,)), ((), ())), preferred_element_type=F32)  84.2 us
    ppermute x6, waiting for transfers between devices, line_spread(): lax.ppermute(rows, 'dp', ring_jumps(ways, k))  78.9 us
    all_to_all x10, waiting for transfers between devices, plane_exchange(): return lax.all_to_all(rows, PLANE, split_axis=0, concat_axis=0, tiled=True)  74.4 us
    pallas_call x2, Pallas kernels, expert_pass(): pl.pallas_call(functools.partial(expert_kernel, experts), grid_spec=pltpu...  60.2 us
    pallas_call x2, Pallas kernels, attend_back(): pl.pallas_call(functools.partial(attend_back_kernel, heads, 1.0 / math.sq...  55.1 us
    dot_general x10, matrix products, dot_nn(): return jnp.dot(a, b, preferred_element_type=F32)  47.6 us
    all_to_all x10, starting transfers between devices, plane_exchange(): return lax.all_to_all(rows, PLANE, split_axis=0, concat_axis=0, tiled=True)  46.6 us
  transfers between devices with their start and end apart: 64, of which 39 were waited for; matrix products, arithmetic and copies ran while one was open for 25% of the time, Pallas kernels for 16%

profile of v2, /device:TPU:0, one launch (start us, length us, event | category | flops | bytes accessed | tf_op | source)
XLA Modules:
  0.0 943.5 jit_solution(11954984488585269588)
XLA Ops:
  17.6 8.5 collective-permute-done.7
  34.8 17.8 %collective-permute-done.8 = bf16[2,128,2048]{2,1,0:T(8,128)(2,1)S(1)} collective-permute-done((bf16[2,128,2048]{2,1,0:T(8,128)(2,1)S(1)}, bf16[2,128,2048]{2,1,0:T(8,128)(2,1)S(1)}, u32[]{:S(2)}, u32[]{:S(2)}) %collective-permute-start.8) | collective-permute-done | bytes 1048608 | tf_op jit(solution)/shard_map/ppermute | solution.py:442
  81.1 8.4 fusion.7.qkv_ref
  89.6 17.5 %shard_map.248 = (bf16[8,128,512]{2,1,0:T(8,128)(2,1)S(1)}, f32[8,512,128]{2,1,0:T(8,128)S(1)}) custom-call(s32[8]{0:T(128)S(1)} %get-tuple-element.307.order_ref, s32[8]{0:T(128)S(1)} %convert_reduce_fusion.low_ref, f32[8,128,768]{2,1,0:T(8,128)} %fusion.7.qkv_ref, f32[8,128,128]{2,1,0:T(8,128)S(1)} %get-tuple-element.311.cos_ref, ...), custom_call_target="tpu_custom_call" | custom-call | flops 536870912 | bytes 6291456 | tf_op jit(solution)/shard_map/pallas_call | solution.py:251
  114.2 9.7 %all-gather.3.cloned.1.call-done = bf16[2048,512]{1,0:T(8,128)(2,1)} async-done(((bf16[512,512]{1,0:T(8,128)(2,1)}), bf16[2048,512]{1,0:T(8,128)(2,1)}) %all-gather.3.cloned.1.call-update) | async-done | bytes 2097168 | tf_op jit(solution)/shard_map/all_gather | solution.py:565
  128.1 18.1 %shard_map.247 = (bf16[8,128,512]{2,1,0:T(8,128)(2,1)S(1)}, f32[8,512,128]{2,1,0:T(8,128)S(1)}) custom-call(s32[8]{0:T(128)S(1)} %get-tuple-element.308.order_ref, s32[8]{0:T(128)S(1)} %convert_reduce_fusion.1.low_ref, f32[8,128,768]{2,1,0:T(8,128)} %fusion.9.qkv_ref, f32[8,128,128]{2,1,0:T(8,128)S(1)} %get-tuple-element.311.cos_ref, ...), custom_call_target="tpu_custom_call" | custom-call | flops 536870912 | bytes 6291456 | tf_op jit(solution)/shard_map/pallas_call | solution.py:251
  166.8 33.7 %collective-permute-done.3 = bf16[128,2048]{1,0:T(8,128)(2,1)S(1)} collective-permute-done((bf16[128,2048]{1,0:T(8,128)(2,1)S(1)}, bf16[128,2048]{1,0:T(8,128)(2,1)S(1)}, u32[]{:S(2)}, u32[]{:S(2)}) %collective-permute-start.3) | collective-permute-done | bytes 524320 | tf_op jit(solution)/shard_map/ppermute | solution.py:415
  225.6 10.5 %collective-permute-done.26 = bf16[128,2048]{1,0:T(8,128)(2,1)S(1)} collective-permute-done((bf16[128,2048]{1,0:T(8,128)(2,1)}, bf16[128,2048]{1,0:T(8,128)(2,1)S(1)}, u32[]{:S(2)}, u32[]{:S(2)}) %collective-permute-start.26) | collective-permute-done | bytes 524320 | tf_op jit(solution)/shard_map/ppermute | solution.py:415
  236.1 12.5 %collective-permute-done.25 = bf16[128,2048]{1,0:T(8,128)(2,1)S(1)} collective-permute-done((bf16[128,2048]{1,0:T(8,128)(2,1)}, bf16[128,2048]{1,0:T(8,128)(2,1)S(1)}, u32[]{:S(2)}, u32[]{:S(2)}) %collective-permute-start.25) | collective-permute-done | bytes 524320 | tf_op jit(solution)/shard_map/ppermute | solution.py:415
  248.6 22.2 %collective-permute-done.24 = bf16[128,2048]{1,0:T(8,128)(2,1)S(1)} collective-permute-done((bf16[128,2048]{1,0:T(8,128)(2,1)}, bf16[128,2048]{1,0:T(8,128)(2,1)S(1)}, u32[]{:S(2)}, u32[]{:S(2)}) %collective-permute-start.24) | collective-permute-done | bytes 524320 | tf_op jit(solution)/shard_map/ppermute | solution.py:415
  286.8 16.0 %collective-permute-done.21 = bf16[128,2176]{1,0:T(8,128)(2,1)S(1)} collective-permute-done((bf16[128,2176]{1,0:T(8,128)(2,1)}, bf16[128,2176]{1,0:T(8,128)(2,1)S(1)}, u32[]{:S(2)}, u32[]{:S(2)}) %collective-permute-start.21) | collective-permute-done | bytes 557088 | tf_op jit(solution)/shard_map/ppermute | solution.py:404
  302.8 15.0 %collective-permute-done.22 = bf16[128,2176]{1,0:T(8,128)(2,1)S(1)} collective-permute-done((bf16[128,2176]{1,0:T(8,128)(2,1)S(1)}, bf16[128,2176]{1,0:T(8,128)(2,1)S(1)}, u32[]{:S(2)}, u32[]{:S(2)}) %collective-permute-start.22) | collective-permute-done | bytes 557088 | tf_op jit(solution)/shard_map/ppermute | solution.py:404
  318.0 14.2 %collective-permute-done.23 = bf16[128,2176]{1,0:T(8,128)(2,1)S(1)} collective-permute-done((bf16[128,2176]{1,0:T(8,128)(2,1)S(1)}, bf16[128,2176]{1,0:T(8,128)(2,1)S(1)}, u32[]{:S(2)}, u32[]{:S(2)}) %collective-permute-start.23) | collective-permute-done | bytes 557088 | tf_op jit(solution)/shard_map/ppermute | solution.py:404
  347.6 16.0 %collective-permute-done.18 = bf16[128,2176]{1,0:T(8,128)(2,1)S(1)} collective-permute-done((bf16[128,2176]{1,0:T(8,128)(2,1)}, bf16[128,2176]{1,0:T(8,128)(2,1)S(1)}, u32[]{:S(2)}, u32[]{:S(2)}) %collective-permute-start.18) | collective-permute-done | bytes 557088 | tf_op jit(solution)/shard_map/ppermute | solution.py:404
  363.6 15.0 %collective-permute-done.19 = bf16[128,2176]{1,0:T(8,128)(2,1)S(1)} collective-permute-done((bf16[128,2176]{1,0:T(8,128)(2,1)S(1)}, bf16[128,2176]{1,0:T(8,128)(2,1)S(1)}, u32[]{:S(2)}, u32[]{:S(2)}) %collective-permute-start.19) | collective-permute-done | bytes 557088 | tf_op jit(solution)/shard_map/ppermute | solution.py:404
  378.6 14.2 %collective-permute-done.20 = bf16[128,2176]{1,0:T(8,128)(2,1)S(1)} collective-permute-done((bf16[128,2176]{1,0:T(8,128)(2,1)S(1)}, bf16[128,2176]{1,0:T(8,128)(2,1)S(1)}, u32[]{:S(2)}, u32[]{:S(2)}) %collective-permute-start.20) | collective-permute-done | bytes 557088 | tf_op jit(solution)/shard_map/ppermute | solution.py:404
  404.9 30.2 %shard_map.250 = (bf16[1152,768]{1,0:T(8,128)(2,1)}, bf16[1152,768]{1,0:T(8,128)(2,1)}, bf16[1152,768]{1,0:T(8,128)(2,1)}, bf16[1152,2176]{1,0:T(8,128)(2,1)}, bf16[1152,2048]{1,0:T(8,128)(2,1)}) custom-call(s32[1]{0:T(128)} %bitcast.44.expert_ref, bf16[1152,2176]{1,0:T(8,128)(2,1)} %bitcast.59.rows_ref.gates_ref, ...), custom_call_target="tpu_custom_call" | custom-call | flops 5435817984 | bytes 9437184 | tf_op jit(solution)/shard_map/pallas_call | solution.py:365
  435.1 26.9 %all-to-all-done.3 = bf16[8,144,2176]{2,1,0:T(8,128)(2,1)} async-done(((bf16[8,144,2176]{2,1,0:T(8,128)(2,1)}), bf16[8,144,2176]{2,1,0:T(8,128)(2,1)}, u32[]{:S(2)}, u32[]{:S(2)}) %all-to-all-start.3) | async-done | bytes 5013536 | tf_op jit(solution)/shard_map/all_to_all | solution.py:508
  477.5 30.1 %shard_map.249 = (bf16[1152,768]{1,0:T(8,128)(2,1)}, bf16[1152,768]{1,0:T(8,128)(2,1)}, bf16[1152,768]{1,0:T(8,128)(2,1)}, bf16[1152,2176]{1,0:T(8,128)(2,1)}, bf16[1152,2048]{1,0:T(8,128)(2,1)}) custom-call(s32[1]{0:T(128)} %bitcast.44.expert_ref, bf16[1152,2176]{1,0:T(8,128)(2,1)} %bitcast.61.rows_ref.gates_ref, ...), custom_call_target="tpu_custom_call" | custom-call | flops 5435817984 | bytes 9437184 | tf_op jit(solution)/shard_map/pallas_call | solution.py:365
  507.6 16.5 %all-to-all-done.4 = bf16[8,144,2176]{2,1,0:T(8,128)(2,1)} async-done(((bf16[8,144,2176]{2,1,0:T(8,128)(2,1)}), bf16[8,144,2176]{2,1,0:T(8,128)(2,1)}, u32[]{:S(2)}, u32[]{:S(2)}) %all-to-all-start.4) | async-done | bytes 5013536 | tf_op jit(solution)/shard_map/all_to_all | solution.py:508
  539.6 6.7 fusion.112
  557.4 6.5 convolution_add_fusion.2
  570.5 8.7 convolution_add_fusion
  602.6 21.1 %collective-permute-done.30 = bf16[128,2176]{1,0:T(8,128)(2,1)S(1)} collective-permute-done((bf16[128,2176]{1,0:T(8,128)(2,1)S(1)}, bf16[128,2176]{1,0:T(8,128)(2,1)S(1)}, u32[]{:S(2)}, u32[]{:S(2)}) %collective-permute-start.30) | collective-permute-done | bytes 557088 | tf_op jit(solution)/shard_map/ppermute | solution.py:424
  623.7 11.5 %collective-permute-done.31 = bf16[128,2176]{1,0:T(8,128)(2,1)S(1)} collective-permute-done((bf16[128,2176]{1,0:T(8,128)(2,1)S(1)}, bf16[128,2176]{1,0:T(8,128)(2,1)S(1)}, u32[]{:S(2)}, u32[]{:S(2)}) %collective-permute-start.31) | collective-permute-done | bytes 557088 | tf_op jit(solution)/shard_map/ppermute | solution.py:424
  647.0 11.2 %collective-permute-done.34 = bf16[128,2048]{1,0:T(8,128)(2,1)S(1)} collective-permute-done((bf16[128,2048]{1,0:T(8,128)(2,1)S(1)}, bf16[128,2048]{1,0:T(8,128)(2,1)S(1)}, u32[]{:S(2)}, u32[]{:S(2)}) %collective-permute-start.34) | collective-permute-done | bytes 524320 | tf_op jit(solution)/shard_map/ppermute | solution.py:441
  661.7 21.7 %collective-permute-done.35 = bf16[2,128,2048]{2,1,0:T(8,128)(2,1)S(1)} collective-permute-done((bf16[2,128,2048]{2,1,0:T(8,128)(2,1)S(1)}, bf16[2,128,2048]{2,1,0:T(8,128)(2,1)S(1)}, u32[]{:S(2)}, u32[]{:S(2)}) %collective-permute-start.35) | collective-permute-done | bytes 1048608 | tf_op jit(solution)/shard_map/ppermute | solution.py:442
  722.0 28.3 %shard_map.251 = (bf16[8,128,768]{2,1,0:T(8,128)(2,1)}, f32[8,128]{1,0:T(8,128)}) custom-call(s32[8]{0:T(128)} %copy-done.18, s32[8]{0:T(128)} %copy-done.16, f32[8,128,768]{2,1,0:T(8,128)} %fusion.9.qkv_ref, f32[8,128,128]{2,1,0:T(8,128)} %copy-done.2, f32[8,128,128]{2,1,0:T(8,128)} %copy-done.3, f32[1,128]{1,0:T(1,128)} %bitcast.354, f32[1,128]{1,0:T(1,128)} %bitcast.358, ...), custom_call_target="tpu_custom_call" | custom-call | flops 1073741824 | bytes 9437184 | tf_op jit(solution)/shard_map/pallas_call | solution.py:280
  753.7 26.8 %shard_map.252 = (bf16[8,128,768]{2,1,0:T(8,128)(2,1)}, f32[8,128]{1,0:T(8,128)}) custom-call(s32[8]{0:T(128)} %copy-done.17, s32[8]{0:T(128)} %copy-done.15, f32[8,128,768]{2,1,0:T(8,128)} %fusion.7.qkv_ref, f32[8,128,128]{2,1,0:T(8,128)} %copy-done.2, f32[8,128,128]{2,1,0:T(8,128)} %copy-done.3, f32[1,128]{1,0:T(1,128)} %bitcast.355, f32[1,128]{1,0:T(1,128)} %bitcast.359, ...), custom_call_target="tpu_custom_call" | custom-call | flops 1073741824 | bytes 9437184 | tf_op jit(solution)/shard_map/pallas_call | solution.py:280
  796.5 10.2 %collective-permute-start.41 = (bf16[512,768]{1,0:T(8,128)(2,1)S(1)}, bf16[512,768]{1,0:T(8,128)(2,1)S(1)}, u32[]{:S(2)}, u32[]{:S(2)}) collective-permute-start(bf16[512,768]{1,0:T(8,128)(2,1)S(1)} %constant_dynamic-slice_fusion), channel_id=1, source_target_pairs={{24,8},{16,24},{0,16},{8,0},{25,9},{17,25},{1,17},{9,1},{26,10},{1... | collective-permute-start | bytes 2359304 | tf_op jit(solution)/shard_map/ppermute | solution.py:432
  810.3 13.6 %collective-permute-done.41 = bf16[512,768]{1,0:T(8,128)(2,1)S(1)} collective-permute-done((bf16[512,768]{1,0:T(8,128)(2,1)S(1)}, bf16[512,768]{1,0:T(8,128)(2,1)S(1)}, u32[]{:S(2)}, u32[]{:S(2)}) %collective-permute-start.41) | collective-permute-done | bytes 786464 | tf_op jit(solution)/shard_map/ppermute | solution.py:432
  861.1 15.2 %all-to-all-done.10 = bf16[8,64,512]{2,1,0:T(8,128)(2,1)} async-done(((bf16[8,64,512]{2,1,0:T(8,128)(2,1)}), bf16[8,64,512]{2,1,0:T(8,128)(2,1)}, u32[]{:S(2)}, u32[]{:S(2)}) %all-to-all-start.10) | async-done | bytes 524320 | tf_op jit(solution)/shard_map/all_to_all | solution.py:508
  (471 shorter events, 390.4 us)
Async XLA Ops:
  7.2 73.9 %all-gather.5.cloned.1.call-start = ((), (), s32[]{:S(2)}) async-start(), calls=%async_computation.15 | async-start | bytes 3932160 | tf_op jit(solution)/shard_map/all_gather | solution.py:552
  10.4 113.4 %all-gather.3.cloned.1.call-start = ((), (), s32[]{:S(2)}) async-start(), calls=%async_computation.14 | async-start | bytes 2621440 | tf_op jit(solution)/shard_map/all_gather | solution.py:565
  14.2 48.0 %collective-permute-start = (s32[1,256,8]{1,2,0:T(8,128)S(1)}, s32[1,256,8]{1,2,0:T(8,128)S(1)}, u32[]{:S(2)}, u32[]{:S(2)}) collective-permute-start(s32[1,256,8]{1,2,0:T(8,128)S(1)} %bitcast.413), channel_id=1, source_target_pairs={{8,24},{24,16},{16,0},{0,8},{9,25},{25,17},{17,1},{1,9},{10,26},{2... | collective-permute-start | bytes 24584 | tf_op jit(solution)/shard_map/ppermute | solution.py:404
  128.1 30.7 %collective-permute-start.15 = (bf16[4,128,2048]{2,1,0:T(8,128)(2,1)}, bf16[4,128,2048]{2,1,0:T(8,128)(2,1)}, u32[]{:S(2)}, u32[]{:S(2)}) collective-permute-start(bf16[4,128,2048]{2,1,0:T(8,128)(2,1)} %bitcast.38), channel_id=1, source_target_pairs={{0,2},{1,3},{2,0},{3,1},{4,6},{5,7},{6,4},{7,5},{8,10},{9,11},{10,... | collective-permute-start | bytes 6291464 | tf_op jit(solution)/shard_map/ppermute | solution.py:489
  153.6 47.0 %collective-permute-start.5 = (bf16[128,2048]{1,0:T(8,128)(2,1)S(1)}, bf16[128,2048]{1,0:T(8,128)(2,1)S(1)}, u32[]{:S(2)}, u32[]{:S(2)}) collective-permute-start(bf16[128,2048]{1,0:T(8,128)(2,1)S(1)} %copy-done.47), channel_id=1, source_target_pairs={{8,0},{24,8},{16,24},{0,16},{9,1},{25,9},{17,25},{1,17},{10,2},{26... | collective-permute-start | bytes 1572872 | tf_op jit(solution)/shard_map/ppermute | solution.py:415
  153.8 46.8 %collective-permute-start.4 = (bf16[128,2048]{1,0:T(8,128)(2,1)S(1)}, bf16[128,2048]{1,0:T(8,128)(2,1)S(1)}, u32[]{:S(2)}, u32[]{:S(2)}) collective-permute-start(bf16[128,2048]{1,0:T(8,128)(2,1)S(1)} %copy-done.47), channel_id=1, source_target_pairs={{8,16},{24,0},{16,8},{0,24},{9,17},{25,1},{17,9},{1,25},{10,18},{2... | collective-permute-start | bytes 1572872 | tf_op jit(solution)/shard_map/ppermute | solution.py:415
  155.0 45.5 %collective-permute-start.3 = (bf16[128,2048]{1,0:T(8,128)(2,1)S(1)}, bf16[128,2048]{1,0:T(8,128)(2,1)S(1)}, u32[]{:S(2)}, u32[]{:S(2)}) collective-permute-start(bf16[128,2048]{1,0:T(8,128)(2,1)S(1)} %copy-done.47), channel_id=1, source_target_pairs={{8,24},{24,16},{16,0},{0,8},{9,25},{25,17},{17,1},{1,9},{10,26},{2... | collective-permute-start | bytes 1572872 | tf_op jit(solution)/shard_map/ppermute | solution.py:415
  161.2 39.4 %collective-permute-start.16 = (bf16[2,128,2048]{2,1,0:T(8,128)(2,1)S(1)}, bf16[2,128,2048]{2,1,0:T(8,128)(2,1)S(1)}, u32[]{:S(2)}, u32[]{:S(2)}) collective-permute-start(bf16[2,128,2048]{2,1,0:T(8,128)(2,1)S(1)} %slice.305), channel_id=1, source_target_pairs={{0,4},{1,5},{2,6},{3,7},{4,0},{5,1},{6,2},{7,3},{8,12},{9,13},{10,... | collective-permute-start | bytes 3145736 | tf_op jit(solution)/shard_map/ppermute | solution.py:492
  165.3 37.4 %collective-permute-start.13 = (bf16[2,128,2048]{2,1,0:T(8,128)(2,1)S(1)}, bf16[2,128,2048]{2,1,0:T(8,128)(2,1)S(1)}, u32[]{:S(2)}, u32[]{:S(2)}) collective-permute-start(bf16[2,128,2048]{2,1,0:T(8,128)(2,1)S(1)} %slice.301), channel_id=1, source_target_pairs={{0,1},{1,0},{2,3},{3,2},{4,5},{5,4},{6,7},{7,6},{8,9},{9,8},{10,11... | collective-permute-start | bytes 3145736 | tf_op jit(solution)/shard_map/ppermute | solution.py:492
  216.9 59.7 %all-to-all-start = ((bf16[8,144,2048]{2,1,0:T(8,128)(2,1)}), bf16[8,144,2048]{2,1,0:T(8,128)(2,1)}, u32[]{:S(2)}, u32[]{:S(2)}) async-start(bf16[8,144,2048]{2,1,0:T(8,128)(2,1)} %bitcast.381), calls=%async_computation | async-start | bytes 9437184 | tf_op jit(solution)/shard_map/all_to_all | solution.py:508
  224.5 46.3 %collective-permute-start.24 = (bf16[128,2048]{1,0:T(8,128)(2,1)}, bf16[128,2048]{1,0:T(8,128)(2,1)S(1)}, u32[]{:S(2)}, u32[]{:S(2)}) collective-permute-start(bf16[128,2048]{1,0:T(8,128)(2,1)} %get-tuple-element.106), channel_id=1, source_target_pairs={{8,24},{24,16},{16,0},{0,8},{9,25},{25,17},{17,1},{1,9},{10,26},{2... | collective-permute-start | bytes 1572872 | tf_op jit(solution)/shard_map/ppermute | solution.py:415
  276.6 61.9 %all-to-all-start.1 = ((bf16[8,144,2048]{2,1,0:T(8,128)(2,1)}), bf16[8,144,2048]{2,1,0:T(8,128)(2,1)}, u32[]{:S(2)}, u32[]{:S(2)}) async-start(bf16[8,144,2048]{2,1,0:T(8,128)(2,1)} %bitcast.378), calls=%async_computation.1 | async-start | bytes 9437184 | tf_op jit(solution)/shard_map/all_to_all | solution.py:508
  338.6 61.7 %all-to-all-start.2 = ((bf16[8,144,2176]{2,1,0:T(8,128)(2,1)}), bf16[8,144,2176]{2,1,0:T(8,128)(2,1)}, u32[]{:S(2)}, u32[]{:S(2)}) async-start(bf16[8,144,2176]{2,1,0:T(8,128)(2,1)} %bitcast.369), calls=%async_computation.2 | async-start | bytes 10027008 | tf_op jit(solution)/shard_map/all_to_all | solution.py:508
  400.2 61.7 %all-to-all-start.3 = ((bf16[8,144,2176]{2,1,0:T(8,128)(2,1)}), bf16[8,144,2176]{2,1,0:T(8,128)(2,1)}, u32[]{:S(2)}, u32[]{:S(2)}) async-start(bf16[8,144,2176]{2,1,0:T(8,128)(2,1)} %bitcast.372), calls=%async_computation.3 | async-start | bytes 10027008 | tf_op jit(solution)/shard_map/all_to_all | solution.py:508
  461.9 62.1 %all-to-all-start.4 = ((bf16[8,144,2176]{2,1,0:T(8,128)(2,1)}), bf16[8,144,2176]{2,1,0:T(8,128)(2,1)}, u32[]{:S(2)}, u32[]{:S(2)}) async-start(bf16[8,144,2176]{2,1,0:T(8,128)(2,1)} %bitcast.371), calls=%async_computation.4 | async-start | bytes 10027008 | tf_op jit(solution)/shard_map/all_to_all | solution.py:508
  524.0 61.7 %all-to-all-start.5 = ((bf16[8,144,2176]{2,1,0:T(8,128)(2,1)}), bf16[8,144,2176]{2,1,0:T(8,128)(2,1)}, u32[]{:S(2)}, u32[]{:S(2)}) async-start(bf16[8,144,2176]{2,1,0:T(8,128)(2,1)} %bitcast.370), calls=%async_computation.5 | async-start | bytes 10027008 | tf_op jit(solution)/shard_map/all_to_all | solution.py:508
  535.7 63.2 %collective-permute-start.27 = (bf16[128,2176]{1,0:T(8,128)(2,1)}, bf16[128,2176]{1,0:T(8,128)(2,1)}, u32[]{:S(2)}, u32[]{:S(2)}) collective-permute-start(bf16[128,2176]{1,0:T(8,128)(2,1)} %get-tuple-element.250), channel_id=1, source_target_pairs={{8,0},{24,8},{16,24},{0,16},{9,1},{25,9},{17,25},{1,17},{10,2},{26... | collective-permute-start | bytes 1671176 | tf_op jit(solution)/shard_map/ppermute | solution.py:424
  536.5 64.1 %collective-permute-start.29 = (bf16[128,2176]{1,0:T(8,128)(2,1)}, bf16[128,2176]{1,0:T(8,128)(2,1)}, u32[]{:S(2)}, u32[]{:S(2)}) collective-permute-start(bf16[128,2176]{1,0:T(8,128)(2,1)} %get-tuple-element.251), channel_id=1, source_target_pairs={{8,24},{24,16},{16,0},{0,8},{9,25},{25,17},{17,1},{1,9},{10,26},{2... | collective-permute-start | bytes 1671176 | tf_op jit(solution)/shard_map/ppermute | solution.py:424
  538.0 62.6 %collective-permute-start.28 = (bf16[128,2176]{1,0:T(8,128)(2,1)}, bf16[128,2176]{1,0:T(8,128)(2,1)}, u32[]{:S(2)}, u32[]{:S(2)}) collective-permute-start(bf16[128,2176]{1,0:T(8,128)(2,1)} %get-tuple-element.252), channel_id=1, source_target_pairs={{8,16},{24,0},{16,8},{0,24},{9,17},{25,1},{17,9},{1,25},{10,18},{2... | collective-permute-start | bytes 1671176 | tf_op jit(solution)/shard_map/ppermute | solution.py:424
  585.7 58.5 %all-to-all-start.6 = ((bf16[8,144,2048]{2,1,0:T(8,128)(2,1)}), bf16[8,144,2048]{2,1,0:T(8,128)(2,1)}, u32[]{:S(2)}, u32[]{:S(2)}) async-start(bf16[8,144,2048]{2,1,0:T(8,128)(2,1)} %bitcast.377), calls=%async_computation.6 | async-start | bytes 9437184 | tf_op jit(solution)/shard_map/all_to_all | solution.py:508
  590.4 261.4 %reduce-scatter.8.cloned.1.call-start = ((), (), s32[]{:S(2)}) async-start(), calls=%async_computation.18 | async-start | bytes 2621440 | tf_op jit(solution)/shard_map/reduce_scatter | solution.py:817
  596.5 27.3 %collective-permute-start.30 = (bf16[128,2176]{1,0:T(8,128)(2,1)S(1)}, bf16[128,2176]{1,0:T(8,128)(2,1)S(1)}, u32[]{:S(2)}, u32[]{:S(2)}) collective-permute-start(bf16[128,2176]{1,0:T(8,128)(2,1)S(1)} %get-tuple-element.247), channel_id=1, source_target_pairs={{8,0},{24,8},{16,24},{0,16},{9,1},{25,9},{17,25},{1,17},{10,2},{26... | collective-permute-start | bytes 1671176 | tf_op jit(solution)/shard_map/ppermute | solution.py:424
  598.9 36.3 %collective-permute-start.31 = (bf16[128,2176]{1,0:T(8,128)(2,1)S(1)}, bf16[128,2176]{1,0:T(8,128)(2,1)S(1)}, u32[]{:S(2)}, u32[]{:S(2)}) collective-permute-start(bf16[128,2176]{1,0:T(8,128)(2,1)S(1)} %get-tuple-element.249), channel_id=1, source_target_pairs={{8,16},{24,0},{16,8},{0,24},{9,17},{25,1},{17,9},{1,25},{10,18},{2... | collective-permute-start | bytes 1671176 | tf_op jit(solution)/shard_map/ppermute | solution.py:424
  698.3 82.1 %all-to-all-start.7 = ((bf16[8,144,2048]{2,1,0:T(8,128)(2,1)}), bf16[8,144,2048]{2,1,0:T(8,128)(2,1)}, u32[]{:S(2)}, u32[]{:S(2)}) async-start(bf16[8,144,2048]{2,1,0:T(8,128)(2,1)} %bitcast.376), calls=%async_computation.8 | async-start | bytes 9437184 | tf_op jit(solution)/shard_map/all_to_all | solution.py:508
  703.1 219.6 %reduce-scatter.4.cloned.1.call-start = ((), (), s32[]{:S(2)}) async-start(), calls=%async_computation.16 | async-start | bytes 2621440 | tf_op jit(solution)/shard_map/reduce_scatter | solution.py:749
  715.6 207.1 %reduce-scatter.6.cloned.1.call-start = ((), (), s32[]{:S(2)}) async-start(), calls=%async_computation.17 | async-start | bytes 2621440 | tf_op jit(solution)/shard_map/reduce_scatter | solution.py:749
  791.8 33.3 %collective-permute-start.39 = (bf16[4,128,2048]{2,1,0:T(8,128)(2,1)S(1)}, bf16[4,128,2048]{2,1,0:T(8,128)(2,1)S(1)}, u32[]{:S(2)}, u32[]{:S(2)}) collective-permute-start(bf16[4,128,2048]{2,1,0:T(8,128)(2,1)S(1)} %bitcast.423), channel_id=1, source_target_pairs={{0,2},{1,3},{2,0},{3,1},{4,6},{5,7},{6,4},{7,5},{8,10},{9,11},{10,... | collective-permute-start | bytes 6291464 | tf_op jit(solution)/shard_map/ppermute | solution.py:489
  792.2 33.7 %collective-permute-start.40 = (bf16[4,128,2048]{2,1,0:T(8,128)(2,1)S(1)}, bf16[4,128,2048]{2,1,0:T(8,128)(2,1)S(1)}, u32[]{:S(2)}, u32[]{:S(2)}) collective-permute-start(bf16[4,128,2048]{2,1,0:T(8,128)(2,1)S(1)} %bitcast.422), channel_id=1, source_target_pairs={{0,2},{1,3},{2,0},{3,1},{4,6},{5,7},{6,4},{7,5},{8,10},{9,11},{10,... | collective-permute-start | bytes 6291464 | tf_op jit(solution)/shard_map/ppermute | solution.py:489
  796.5 27.5 %collective-permute-start.41 = (bf16[512,768]{1,0:T(8,128)(2,1)S(1)}, bf16[512,768]{1,0:T(8,128)(2,1)S(1)}, u32[]{:S(2)}, u32[]{:S(2)}) collective-permute-start(bf16[512,768]{1,0:T(8,128)(2,1)S(1)} %constant_dynamic-slice_fusion), channel_id=1, source_target_pairs={{24,8},{16,24},{0,16},{8,0},{25,9},{17,25},{1,17},{9,1},{26,10},{1... | collective-permute-start | bytes 2359304 | tf_op jit(solution)/shard_map/ppermute | solution.py:432
  826.7 29.3 %collective-permute-start.44 = (bf16[512,768]{1,0:T(8,128)(2,1)}, bf16[512,768]{1,0:T(8,128)(2,1)}, u32[]{:S(2)}, u32[]{:S(2)}) collective-permute-start(bf16[512,768]{1,0:T(8,128)(2,1)} %add_convert_fusion.6), channel_id=1, source_target_pairs={{24,8},{16,24},{0,16},{8,0},{25,9},{17,25},{1,17},{9,1},{26,10},{1... | collective-permute-start | bytes 2359304 | tf_op jit(solution)/shard_map/ppermute | solution.py:432
  831.1 27.4 %collective-permute-start.43 = (bf16[2,128,2048]{2,1,0:T(8,128)(2,1)}, bf16[2,128,2048]{2,1,0:T(8,128)(2,1)}, u32[]{:S(2)}, u32[]{:S(2)}) collective-permute-start(bf16[2,128,2048]{2,1,0:T(8,128)(2,1)} %slice.275), channel_id=1, source_target_pairs={{0,4},{1,5},{2,6},{3,7},{4,0},{5,1},{6,2},{7,3},{8,12},{9,13},{10,... | collective-permute-start | bytes 3145736 | tf_op jit(solution)/shard_map/ppermute | solution.py:492
  847.3 32.5 %collective-permute-start.42 = (bf16[2,128,2048]{2,1,0:T(8,128)(2,1)}, bf16[2,128,2048]{2,1,0:T(8,128)(2,1)}, u32[]{:S(2)}, u32[]{:S(2)}) collective-permute-start(bf16[2,128,2048]{2,1,0:T(8,128)(2,1)} %slice.273), channel_id=1, source_target_pairs={{0,1},{1,0},{2,3},{3,2},{4,5},{5,4},{6,7},{7,6},{8,9},{9,8},{10,11... | collective-permute-start | bytes 3145736 | tf_op jit(solution)/shard_map/ppermute | solution.py:492
  (118 other events, 3504.1 us)
Sparse Core Ops, SparseCore 0:
  10.6 66.4 all-gather.4
  79.2 44.5 all-gather.2
  698.4 51.4 reduce-scatter.7
  752.1 43.1 reduce-scatter.3
  839.4 42.6 reduce-scatter.5

commit v3 on v2

--- a/solution.py
+++ b/solution.py
@@ -15,6 +15,7 @@
 EPSILON = 1e-06
 NEG_FILL = -1e30
 LOG2E = 1.4426950408889634
+SCORE_SCALE = LOG2E / math.sqrt(HEAD_DIM)
 PLANE = ("blk", "head")
 EVERY = ("dp", "blk", "head")
 F32 = jnp.float32
@@ -43,6 +44,23 @@
     return scale * (scaled - unit * jnp.mean(scaled * unit, axis=-1, keepdims=True))
 
 
+def lane_sum(values):
+    ones = jnp.ones((HEAD_DIM, HEAD_DIM), BF16)
+    coarse = values.astype(BF16)
+    fine = (values - coarse.astype(F32)).astype(BF16)
+    return dot_nn(coarse, ones) + dot_nn(fine, ones)
+
+
+def head_parts(values):
+    scale = lax.rsqrt(lane_sum(values * values) * (1.0 / HEAD_DIM) + EPSILON)
+    return values * scale, scale
+
+
+def head_back(grad, unit, scale, gain_vec):
+    scaled = grad * gain_vec
+    return scale * (scaled - unit * (lane_sum(scaled * unit) * (1.0 / HEAD_DIM)))
+
+
 def turn_head(unit, cosines, sines):
     return unit * cosines + pltpu.roll(unit, HEAD_DIM // 2, 1) * sines
 
@@ -51,42 +69,39 @@
     return grad * cosines + pltpu.roll(grad * sines, HEAD_DIM // 2, 1)
 
 
-def head_forward(raw, gain_row, cosines, sines):
-    unit, scale = rms_parts(raw)
-    return turn_head(unit * gain_row, cosines, sines), unit, scale
-
-
-def fill_keys(heads, order_ref, qkv_ref, cos_ref, sin_ref, k_gain_ref, k_scr, v_scr):
-    start = heads * HEAD_DIM
-    if v_scr.shape[2] > HEAD_DIM:
-        v_scr[:, :, HEAD_DIM:] = jnp.ones_like(v_scr[:, :, HEAD_DIM:])
-
-    def one(block, carry):
-        place = order_ref[block]
-        raw = qkv_ref[place, :, start : start + HEAD_DIM]
-        turned, _, _ = head_forward(raw, k_gain_ref[...], cos_ref[block], sin_ref[block])
-        k_scr[block] = turned.astype(BF16)
-        values = qkv_ref[place, :, start + HEAD_DIM : start + 2 * HEAD_DIM].astype(BF16)
-        v_scr[block, :, :HEAD_DIM] = values
-        return carry
-
-    lax.fori_loop(0, qkv_ref.shape[0], one, 0)
-
-
-def allowed_keys(row_seg, key_seg, row_block, key_block, heads):
-    rows = lax.broadcasted_iota(jnp.int32, (row_seg.shape[0], key_seg.shape[1]), 0)
-    cols = lax.broadcasted_iota(jnp.int32, (row_seg.shape[0], key_seg.shape[1]), 1)
-    rows = rows + (row_block - key_block) * row_seg.shape[0]
-    keep = jnp.where((row_seg == key_seg) & (cols <= rows), 0.0, NEG_FILL)
-    return jnp.concatenate([keep] * heads, axis=0)
+def pair_of(refs, start):
+    return jnp.concatenate([ref[0, :, start : start + HEAD_DIM] for ref in refs], axis=0)
+
+
+def put_pair(ref, order_ref, pair, start, values):
+    size = values.shape[0] // 2
+    for i in range(2):
+        ref[order_ref[2 * pair + i], :, start : start + HEAD_DIM] = values[
+            i * size : (i + 1) * size
+        ].astype(ref.dtype)
+
+
+def add_keys(start, pair, qkv_refs, cosines, sines, k_gain_ref, k_scr, v_scr):
+    raw = pair_of(qkv_refs, start)
+    unit, _ = head_parts(raw)
+    k_scr[pair] = turn_head(unit * k_gain_ref[...], cosines, sines).astype(BF16)
+    v_scr[pair, :, :HEAD_DIM] = pair_of(qkv_refs, start + HEAD_DIM).astype(BF16)
+    return raw
+
+
+def hidden_keys(row_seg, key_seg, row_pair, key_pair):
+    shape = (row_seg.shape[0], key_seg.shape[1])
+    rows = lax.broadcasted_iota(jnp.int32, shape, 0) + (row_pair - key_pair) * shape[0]
+    cols = lax.broadcasted_iota(jnp.int32, shape, 1)
+    return jnp.where((row_seg == key_seg) & (cols <= rows), 0.0, NEG_FILL)
 
 
 def attend_kernel(
     heads,
-    score_scale,
     order_ref,
     low_ref,
-    qkv_ref,
+    qkv_even_ref,
+    qkv_odd_ref,
     cos_ref,
     sin_ref,
     q_gain_ref,
@@ -97,55 +112,57 @@
     stat_ref,
     k_scr,
     v_scr,
+    q_scr,
+    acc_scr,
 ):
-    block = pl.program_id(0)
-
-    @pl.when(block == 0)
+    pair = pl.program_id(0)
+
+    qkv_refs = (qkv_even_ref, qkv_odd_ref)
+
+    @pl.when(pair == 0)
     def _():
-        fill_keys(heads, order_ref, qkv_ref, cos_ref, sin_ref, k_gain_ref, k_scr, v_scr)
-
-    place = order_ref[block]
-    cosines, sines = cos_ref[block], sin_ref[block]
-    rows = []
+        v_scr[:, :, HEAD_DIM:] = jnp.ones_like(v_scr[:, :, HEAD_DIM:])
+
+    cosines, sines = cos_ref[0], sin_ref[0]
+    add_keys(heads * HEAD_DIM, pair, qkv_refs, cosines, sines, k_gain_ref, k_scr, v_scr)
     for h in range(heads):
-        raw = qkv_ref[place, :, h * HEAD_DIM : (h + 1) * HEAD_DIM]
-        rows.append(head_forward(raw, q_gain_ref[...], cosines, sines)[0].astype(BF16))
-    queries = jnp.concatenate(rows, axis=0)
-    count = queries.shape[0]
-    row_seg = seg_col_ref[block]
-
-    def step(key_block, carry):
-        scores = dot_nt(queries, k_scr[key_block]) * (score_scale * LOG2E)
-        scores = scores + allowed_keys(row_seg, seg_row_ref[key_block], block, key_block, heads)
-        return carry + dot_nn(jnp.exp2(scores).astype(BF16), v_scr[key_block])
-
-    both = lax.fori_loop(
-        low_ref[block], block + 1, step, jnp.zeros((count, 2 * HEAD_DIM), F32)
-    )
-    acc, total = both[:, :HEAD_DIM], both[:, HEAD_DIM:]
-    acc = acc / total
-    size = attn_ref.shape[1]
+        unit, _ = head_parts(pair_of(qkv_refs, h * HEAD_DIM))
+        turned = turn_head(unit * q_gain_ref[...], cosines, sines)
+        q_scr[h] = (turned * SCORE_SCALE).astype(BF16)
+    acc_scr[...] = jnp.zeros_like(acc_scr)
+    row_seg = seg_col_ref[0]
+
+    def step(key_pair, carry):
+        hide = hidden_keys(row_seg, seg_row_ref[key_pair], pair, key_pair)
+        keys, values = k_scr[key_pair], v_scr[key_pair]
+        for h in range(heads):
+            weights = jnp.exp2(dot_nt(q_scr[h], keys) + hide).astype(BF16)
+            acc_scr[h] += dot_nn(weights, values)
+        return carry
+
+    lax.fori_loop(low_ref[pair], pair + 1, step, 0)
     for h in range(heads):
-        attn_ref[0, :, h * HEAD_DIM : (h + 1) * HEAD_DIM] = acc[h * size : (h + 1) * size].astype(
-            BF16
-        )
-    stat_ref[0] = jnp.log2(total)
+        total = acc_scr[h, :, HEAD_DIM:]
+        put_pair(attn_ref, order_ref, pair, h * HEAD_DIM, acc_scr[h, :, :HEAD_DIM] / total)
+        stat_ref[0, h] = jnp.log2(total)
 
 
 def attend_back_kernel(
     heads,
-    score_scale,
     order_ref,
     low_ref,
-    qkv_ref,
+    qkv_even_ref,
+    qkv_odd_ref,
     cos_ref,
     sin_ref,
     q_gain_ref,
     k_gain_ref,
     seg_row_ref,
     seg_col_ref,
-    attn_ref,
-    grad_ref,
+    attn_even_ref,
+    attn_odd_ref,
+    grad_even_ref,
+    grad_odd_ref,
     stat_ref,
     out_ref,
     gain_ref,
@@ -153,119 +170,141 @@
     v_scr,
     dk_scr,
     dv_scr,
+    q_scr,
+    dq_scr,
+    delta_scr,
+    grad_scr,
+    raw_scr,
+    turn_scr,
 ):
-    block = pl.program_id(0)
-    blocks = pl.num_programs(0)
+    pair = pl.program_id(0)
+    pairs = pl.num_programs(0)
     start = heads * HEAD_DIM
 
-    @pl.when(block == 0)
+    @pl.when(pair == 0)
     def _():
-        fill_keys(heads, order_ref, qkv_ref, cos_ref, sin_ref, k_gain_ref, k_scr, v_scr)
         dk_scr[...] = jnp.zeros_like(dk_scr)
         dv_scr[...] = jnp.zeros_like(dv_scr)
         gain_ref[...] = jnp.zeros_like(gain_ref)
 
-    place = order_ref[block]
-    cosines, sines = cos_ref[block], sin_ref[block]
-    rows, units, scales, grads, deltas = [], [], [], [], []
+    qkv_refs = (qkv_even_ref, qkv_odd_ref)
+    cosines, sines = cos_ref[0], sin_ref[0]
+    raw_scr[pair] = add_keys(start, pair, qkv_refs, cosines, sines, k_gain_ref, k_scr, v_scr)
+    turn_scr[0, pair] = cosines
+    turn_scr[1, pair] = sines
     for h in range(heads):
-        raw = qkv_ref[place, :, h * HEAD_DIM : (h + 1) * HEAD_DIM]
-        turned, unit, scale = head_forward(raw, q_gain_ref[...], cosines, sines)
-        rows.append(turned.astype(BF16))
-        units.append(unit)
-        scales.append(scale)
-        grad = grad_ref[0, :, h * HEAD_DIM : (h + 1) * HEAD_DIM]
-        grads.append(grad)
-        attn = attn_ref[0, :, h * HEAD_DIM : (h + 1) * HEAD_DIM]
-        deltas.append(jnp.sum(grad.astype(F32) * attn.astype(F32), axis=1, keepdims=True))
-    queries = jnp.concatenate(rows, axis=0)
-    grad_rows = jnp.concatenate(grads, axis=0)
-    delta = jnp.concatenate(deltas, axis=0)
-    stat = stat_ref[0]
-    row_seg = seg_col_ref[block]
-    count = queries.shape[0]
-
-    def step(key_block, acc):
-        keys, values = k_scr[key_block], v_scr[key_block]
-        scores = dot_nt(queries, keys) * (score_scale * LOG2E)
-        scores = scores + allowed_keys(row_seg, seg_row_ref[key_block], block, key_block, heads)
-        probs = jnp.exp2(scores - stat)
-        grad_probs = dot_nt(grad_rows, values)
-        grad_scores = (probs * (grad_probs - delta)).astype(BF16)
-        dk_scr[key_block] += dot_tn(grad_scores, queries)
-        dv_scr[key_block] += dot_tn(probs.astype(BF16), grad_rows)
-        return acc + dot_nn(grad_scores, keys)
-
-    acc = lax.fori_loop(
-        low_ref[block], block + 1, step, jnp.zeros((count, HEAD_DIM), F32)
-    )
-    acc = acc * score_scale
-    size = grad_ref.shape[1]
+        unit, _ = head_parts(pair_of(qkv_refs, h * HEAD_DIM))
+        turned = turn_head(unit * q_gain_ref[...], cosines, sines)
+        q_scr[h] = (turned * SCORE_SCALE).astype(BF16)
+        grad = pair_of((grad_even_ref, grad_odd_ref), h * HEAD_DIM)
+        attn = pair_of((attn_even_ref, attn_odd_ref), h * HEAD_DIM)
+        grad_scr[h] = grad
+        delta_scr[h] = lane_sum(grad.astype(F32) * attn.astype(F32))
+    dq_scr[...] = jnp.zeros_like(dq_scr)
+    row_seg = seg_col_ref[0]
+
+    def step(key_pair, carry):
+        hide = hidden_keys(row_seg, seg_row_ref[key_pair], pair, key_pair)
+        keys, values = k_scr[key_pair], v_scr[key_pair]
+        dk, dv = dk_scr[key_pair], dv_scr[key_pair]
+        for h in range(heads):
+            grad_rows = grad_scr[h]
+            stat = jnp.concatenate([stat_ref[0, h]] * 2, axis=1)
+            delta = jnp.concatenate([delta_scr[h]] * 2, axis=1)
+            probs = jnp.exp2(dot_nt(q_scr[h], keys) + (hide - stat))
+            grad_scores = (probs * (dot_nt(grad_rows, values) - delta)).astype(BF16)
+            dk = dk + dot_tn(grad_scores, q_scr[h])
+            dv = dv + dot_tn(probs.astype(BF16), grad_rows)
+            dq_scr[h] += dot_nn(grad_scores, keys)
+        dk_scr[key_pair] = dk
+        dv_scr[key_pair] = dv
+        return carry
+
+    lax.fori_loop(low_ref[pair], pair + 1, step, 0)
     gain_sum = jnp.zeros((1, HEAD_DIM), F32)
     for h in range(heads):
-        grad = turn_back(acc[h * size : (h + 1) * size], cosines, sines)
-        gain_sum = gain_sum + jnp.sum(grad * units[h], axis=0, keepdims=True)
-        out_ref[place, :, h * HEAD_DIM : (h + 1) * HEAD_DIM] = rms_back(
-            grad, units[h], scales[h], q_gain_ref[...]
-        ).astype(BF16)
+        unit, scale = head_parts(pair_of(qkv_refs, h * HEAD_DIM))
+        grad = turn_back(dq_scr[h] * (SCORE_SCALE / LOG2E), cosines, sines)
+        gain_sum = gain_sum + jnp.sum(grad * unit, axis=0, keepdims=True)
+        put_pair(
+            out_ref, order_ref, pair, h * HEAD_DIM, head_back(grad, unit, scale, q_gain_ref[...])
+        )
     gain_ref[0:1, :] += gain_sum
 
-    @pl.when(block == blocks - 1)
+    @pl.when(pair == pairs - 1)
     def _():
-        def one(key_block, carry):
-            spot = order_ref[key_block]
-            raw = qkv_ref[spot, :, start : start + HEAD_DIM]
-            unit, scale = rms_parts(raw)
-            grad = turn_back(dk_scr[key_block] * score_scale, cos_ref[key_block], sin_ref[key_block])
-            out_ref[spot, :, start : start + HEAD_DIM] = rms_back(
-                grad, unit, scale, k_gain_ref[...]
-            ).astype(BF16)
-            out_ref[spot, :, start + HEAD_DIM : start + 2 * HEAD_DIM] = dv_scr[key_block].astype(
-                BF16
+        def one(key_pair, carry):
+            unit, scale = head_parts(raw_scr[key_pair])
+            grad = turn_back(
+                dk_scr[key_pair] * (1.0 / LOG2E), turn_scr[0, key_pair], turn_scr[1, key_pair]
             )
+            put_pair(
+                out_ref, order_ref, key_pair, start, head_back(grad, unit, scale, k_gain_ref[...])
+            )
+            put_pair(out_ref, order_ref, key_pair, start + HEAD_DIM, dv_scr[key_pair])
             return carry + jnp.sum(grad * unit, axis=0, keepdims=True)
 
-        gain_ref[1:2, :] += lax.fori_loop(0, blocks, one, jnp.zeros((1, HEAD_DIM), F32))
+        gain_ref[1:2, :] += lax.fori_loop(0, pairs, one, jnp.zeros((1, HEAD_DIM), F32))
 
 
 def whole_block(shape):
     zeros = (0,) * len(shape)
-    return pl.BlockSpec(shape, lambda block, order, low: zeros)
-
-
-def row_block(shape):
-    return pl.BlockSpec(shape, lambda block, order, low: (order[block], 0, 0))
+    return pl.BlockSpec(shape, lambda pair, order, low: zeros)
+
+
+def stat_block(heads, rows):
+    return pl.BlockSpec((1, heads, rows, HEAD_DIM), lambda pair, order, low: (pair, 0, 0, 0))
+
+
+def pair_block(shape):
+    return pl.BlockSpec((1, *shape), lambda pair, order, low: (pair, 0, 0))
+
+
+def ordered_blocks(shape):
+    return [
+        pl.BlockSpec((1, *shape), lambda pair, order, low, i=i: (order[2 * pair + i], 0, 0))
+        for i in range(2)
+    ]
 
 
 def attention_inputs(qkv, tables, gains, segment):
-    blocks, size, _ = qkv.shape
-    rows = segment.reshape(blocks, 1, size)
-    cols = segment.reshape(blocks, size, 1)
-    arrays = (qkv, *tables, *gains, rows, cols)
-    return arrays, [whole_block(a.shape) for a in arrays]
+    blocks, size, width = qkv.shape
+    tables = [table.reshape(blocks // 2, 2 * size, HEAD_DIM) for table in tables]
+    rows = segment.reshape(blocks // 2, 1, 2 * size)
+    cols = segment.reshape(blocks // 2, 2 * size, 1)
+    specs = (
+        ordered_blocks((size, width))
+        + [pair_block((2 * size, HEAD_DIM))] * 2
+        + [whole_block(gain.shape) for gain in gains]
+        + [whole_block(rows.shape), pair_block((2 * size, 1))]
+    )
+    return (qkv, qkv, *tables, *gains, rows, cols), specs
 
 
 def attend(qkv, tables, gains, segment, order, low, heads):
     blocks, size, _ = qkv.shape
+    pairs, rows = blocks // 2, 2 * size
     arrays, specs = attention_inputs(qkv, tables, gains, segment)
     return pl.pallas_call(
-        functools.partial(attend_kernel, heads, 1.0 / math.sqrt(HEAD_DIM)),
+        functools.partial(attend_kernel, heads),
         grid_spec=pltpu.PrefetchScalarGridSpec(
             num_scalar_prefetch=2,
-            grid=(blocks,),
+            grid=(pairs,),
             in_specs=specs,
             out_specs=[
-                row_block((1, size, heads * HEAD_DIM)),
-                row_block((1, heads * size, HEAD_DIM)),
+                whole_block((blocks, size, heads * HEAD_DIM)),
+                stat_block(heads, rows),
             ],
             scratch_shapes=[
-                pltpu.VMEM((blocks, size, HEAD_DIM), BF16),
-                pltpu.VMEM((blocks, size, 2 * HEAD_DIM), BF16),
+                pltpu.VMEM((pairs, rows, HEAD_DIM), BF16),
+                pltpu.VMEM((pairs, rows, 2 * HEAD_DIM), BF16),
+                pltpu.VMEM((heads, rows, HEAD_DIM), BF16),
+                pltpu.VMEM((heads, rows, 2 * HEAD_DIM), F32),
             ],
         ),
         out_shape=[
             jax.ShapeDtypeStruct((blocks, size, heads * HEAD_DIM), BF16),
-            jax.ShapeDtypeStruct((blocks, heads * size, HEAD_DIM), F32),
+            jax.ShapeDtypeStruct((pairs, heads, rows, HEAD_DIM), F32),
         ],
         compiler_params=pltpu.CompilerParams(vmem_limit_bytes=48 * 2**20),
         cost_estimate=pl.CostEstimate(
@@ -276,21 +315,27 @@
 
 def attend_back(qkv, tables, gains, segment, order, low, heads, attn, grad, stat):
     blocks, size, width = qkv.shape
+    pairs, rows = blocks // 2, 2 * size
     arrays, specs = attention_inputs(qkv, tables, gains, segment)
     return pl.pallas_call(
-        functools.partial(attend_back_kernel, heads, 1.0 / math.sqrt(HEAD_DIM)),
+        functools.partial(attend_back_kernel, heads),
         grid_spec=pltpu.PrefetchScalarGridSpec(
             num_scalar_prefetch=2,
-            grid=(blocks,),
+            grid=(pairs,),
             in_specs=specs
+            + ordered_blocks((size, heads * HEAD_DIM)) * 2
+            + [stat_block(heads, rows)],
+            out_specs=[whole_block((blocks, size, width)), whole_block((8, HEAD_DIM))],
+            scratch_shapes=[pltpu.VMEM((pairs, rows, HEAD_DIM), BF16)] * 2
+            + [pltpu.VMEM((pairs, rows, HEAD_DIM), F32)] * 2
             + [
-                row_block((1, size, heads * HEAD_DIM)),
-                row_block((1, size, heads * HEAD_DIM)),
-                row_block((1, heads * size, HEAD_DIM)),
+                pltpu.VMEM((heads, rows, HEAD_DIM), BF16),
+                pltpu.VMEM((heads, rows, HEAD_DIM), F32),
+                pltpu.VMEM((heads, rows, HEAD_DIM), F32),
+                pltpu.VMEM((heads, rows, HEAD_DIM), BF16),
+                pltpu.VMEM((pairs, rows, HEAD_DIM), F32),
+                pltpu.VMEM((2, pairs, rows, HEAD_DIM), F32),
             ],
-            out_specs=[whole_block((blocks, size, width)), whole_block((8, HEAD_DIM))],
-            scratch_shapes=[pltpu.VMEM((blocks, size, HEAD_DIM), BF16)] * 2
-            + [pltpu.VMEM((blocks, size, HEAD_DIM), F32)] * 2,
         ),
         out_shape=[
             jax.ShapeDtypeStruct((blocks, size, width), BF16),
@@ -300,7 +345,56 @@
         cost_estimate=pl.CostEstimate(
             flops=2**24 * blocks * heads * 2, bytes_accessed=qkv.size * 12, transcendentals=0
         ),
-    )(order, low, *arrays, attn, grad, stat)
+    )(order, low, *arrays, attn, attn, grad, grad, stat)
+
+
+def project_kernel(counts, normed, *refs):
+    pieces, (gain_ref, weight_ref, out_ref, rows_ref) = refs[: len(counts)], refs[len(counts) :]
+    block = pl.program_id(0)
+    rows = pieces[-1][0]
+    place = sum(counts) - counts[-1]
+    for ref, count in zip(pieces[-2::-1], counts[-2::-1]):
+        rows = jnp.where(block < place, ref[0], rows)
+        place = place - count
+    if normed:
+        unit, _ = rms_parts(rows.astype(F32))
+        rows = (unit * gain_ref[...]).astype(BF16)
+    rows_ref[0] = rows
+    out_ref[0] = dot_nn(rows, weight_ref[...]).astype(out_ref.dtype)
+
+
+def project(pieces, gain, weight, normed, out_type):
+    counts = [piece.shape[0] for piece in pieces]
+    _, size, width = pieces[0].shape
+    blocks, columns = sum(counts), weight.shape[1]
+
+    def piece_spec(first, count):
+        return pl.BlockSpec(
+            (1, size, width), lambda i: (jnp.clip(i - first, 0, count - 1), 0, 0)
+        )
+
+    firsts = [sum(counts[:i]) for i in range(len(counts))]
+    return pl.pallas_call(
+        functools.partial(project_kernel, counts, normed),
+        grid=(blocks,),
+        in_specs=[piece_spec(first, count) for first, count in zip(firsts, counts)]
+        + [
+            pl.BlockSpec(gain.shape, lambda i: (0, 0)),
+            pl.BlockSpec(weight.shape, lambda i: (0, 0), pipeline_mode=pl.Buffered(1)),
+        ],
+        out_specs=[
+            pl.BlockSpec((1, size, columns), lambda i: (i, 0, 0)),
+            pl.BlockSpec((1, size, width), lambda i: (i, 0, 0)),
+        ],
+        out_shape=[
+            jax.ShapeDtypeStruct((blocks, size, columns), out_type),
+            jax.ShapeDtypeStruct((blocks, size, width), BF16),
+        ],
+        compiler_params=pltpu.CompilerParams(vmem_limit_bytes=32 * 2**20),
+        cost_estimate=pl.CostEstimate(
+            flops=blocks * size * width * columns, bytes_accessed=weight.size, transcendentals=0
+        ),
+    )(*pieces, gain, weight)
 
 
 def expert_kernel(
@@ -435,28 +529,27 @@
 
 def plane_gather_steps(rows, turn, pair):
     if not pair:
-        yield lax.all_gather(rows, PLANE, axis=0, tiled=False)
+        yield [lax.all_gather(rows, PLANE, axis=0, tiled=False)]
         return
     first, second = plane_flips(turn)
     two = yield jnp.stack([rows, lax.ppermute(rows, PLANE, first)])
     four = yield jnp.concatenate([two, lax.ppermute(two, PLANE, second)])
-    yield jnp.concatenate([four, lax.ppermute(four, PLANE, flips(2))])
+    yield [four, lax.ppermute(four, PLANE, flips(2))]
 
 
 def together(*moves):
-    held = [next(move) for move in moves]
-    while True:
+    held, going = [next(move) for move in moves], True
+    while going:
         if len(held) > 1:
-            held = [by_rows(h) for h in tie(*held)]
-        after = []
-        for move, value in zip(moves, held):
+            held = jax.tree.map(by_rows, list(tie(*held)))
+        going = False
+        for i, move in enumerate(moves):
             try:
-                after.append(move.send(value))
+                held[i] = move.send(held[i])
+                going = True
             except StopIteration:
-                after.append(value)
-        if all(a is b for a, b in zip(after, held)):
-            return held
-        held = after
+                continue
+    return held
 
 
 def paired(blk_ways, head_ways):
@@ -562,9 +655,6 @@
         axis=0,
         tiled=True,
     )
-    out_local = lax.all_gather(
-        columns(out_weight, plane_index * local_dim, local_dim), "dp", axis=0, tiled=True
-    )
 
     half = HEAD_DIM // 2
     frequency = 1000000.0 ** (-2.0 * jnp.arange(half, dtype=F32) / HEAD_DIM)
@@ -587,11 +677,15 @@
     ring_slots = (spots[dp_index] - spots) % dp_ways
     ring = jnp.array([a for a, _ in ring_steps(dp_ways)], jnp.int32)
     dp_index_of_slot = ring[(spots[dp_index] - jnp.arange(dp_ways)) % dp_ways]
-    line_routes = line_gather(routes.reshape(1, seqs * size, top_count), dp_ways)
-    line_routes = line_routes.reshape(dp_ways, seqs, size, top_count)
+    def route_steps():
+        yield lows[0]
+        yield line_routes
+
+    line_routes = line_spread(routes.reshape(1, seqs * size, top_count), dp_ways)
 
     def picks_of(s):
-        seen = line_routes[:, s].reshape(dp_ways * size, top_count)
+        seen = line_routes.reshape(dp_ways, seqs, size, top_count)[:, s]
+        seen = seen.reshape(dp_ways * size, top_count)
         chosen = jnp.any(seen[:, :, None] == expert_ids[None, None, :], axis=1)
         chosen = chosen.reshape(dp_ways, size, plane_ways)
         ranks = jnp.einsum(
@@ -607,7 +701,6 @@
 
         return table(keys), table(jnp.take(keys, ring_slots, axis=0))
 
-    picks, straight_picks = zip(*[picks_of(s) for s in range(seqs)])
 
     last = []
 
@@ -626,24 +719,31 @@
 
     orders, lows = [], []
     for s in range(seqs):
-        blocks = segments[s].reshape(plane_ways, size)
+        blocks = segments[s].reshape(plane_ways // 2, 2 * size)
         lows.append(
             jnp.sum(
-                (blocks[None, :, size - 1] < blocks[:, None, 0]).astype(jnp.int32), axis=1
+                (blocks[None, :, -1] < blocks[:, None, 0]).astype(jnp.int32), axis=1
             ).astype(jnp.int32)
         )
         orders.append(plane_order(plane_index, plane_ways, s, pair))
 
-    inputs, units, scales, spread = [], [], [], []
+    inputs, units, scales = [], [], []
+    moves = []
     for s in range(seqs):
         rows = tokens[s].astype(F32)
         unit, scale = rms_parts(rows)
         inputs.append(rows)
         units.append(unit)
         scales.append(scale)
-        spread.append(plane_gather_steps((unit * attn_gain_row).astype(BF16), s, pair))
-    *spread, qkv_local = tie(*together(*spread), qkv_local)
-    spread = [by_rows(rows) for rows in spread]
+        moves.append(plane_gather_steps(tokens[s], s, pair))
+    *pieces, line_routes = together(*moves, route_steps())
+    picks, straight_picks = zip(*[picks_of(s) for s in range(seqs)])
+    pieces, qkv_local = tie(pieces, qkv_local)
+    out_columns, qkv_local = tie(
+        columns(out_weight, plane_index * local_dim, local_dim), qkv_local
+    )
+    out_local = lax.all_gather(out_columns, "dp", axis=0, tiled=True)
+    pieces = jax.tree.map(by_rows, pieces)
 
     def times(left, right):
         def product(start, stop):
@@ -658,18 +758,26 @@
     for s in range(seqs):
         rows, held = tie(cotangent[s], held)
         held = line_spread(rows, dp_ways)
-        lines.append(pack(held, picks[s]))
-    projected, attended, stats, mixes = [], [], [], []
+        lines.append(held)
+    projected, attended, stats, mixes, spread = [], [], [], [], []
     for s in range(seqs):
-        qkv = dot_nn(spread[s].reshape(seq_total, width), qkv_local)
-        qkv = qkv.reshape(plane_ways, size, local_dim + 2 * HEAD_DIM)
+        qkv, rows = project(pieces[s], attn_gain_row, qkv_local, True, F32)
+        spread.append(rows)
         attn, stat = attend(qkv, tables, gains, segments[s], orders[s], lows[s], heads)
         projected.append(qkv)
         attended.append(attn)
         stats.append(stat)
-        mixes.append(together(plane_reduce(times(attn, out_local), s, pair))[0])
-    lines[0], *mixes = tie(lines[0], *mixes)
-    cot_rows = [exchange(rows) for rows in lines]
+        mixes.append(plane_reduce(times(attn, out_local), s, pair))
+
+    def pack_steps():
+        mark = yield lows[0]
+        mark = yield mark
+        rows, _ = tie(lines[0], mark)
+        yield pack(rows, picks[0])
+
+    *mixes, packed = together(*mixes, pack_steps())
+    packed, *mixes = tie(packed, *mixes)
+    cot_rows = [exchange(packed)]
 
     middles, normed2s, mid_units, mid_scales, gate_tables, came = [], [], [], [], [], []
     for s in range(seqs):
@@ -693,9 +801,10 @@
         mid_units.append(unit)
         mid_scales.append(scale)
         gate_tables.append(gates)
-        came.append(
-            exchange(pack(line_gather(jnp.concatenate(payload, axis=1), dp_ways), picks[s]))
-        )
+        line = line_gather(jnp.concatenate(payload, axis=1), dp_ways)
+        if s:
+            cot_rows.append(exchange(pack(lines[s], picks[s])))
+        came.append(exchange(pack(line, picks[s])))
 
     gate_w, up_w, down_w = gate_weight[0], up_weight[0], down_weight[0]
     expert_id = (dp_index * plane_ways + plane_index).astype(jnp.int32)
@@ -739,25 +848,46 @@
     *grad_mids, out_lines[0], gate_grad, up_grad, down_grad = tie(
         *grad_mids, out_lines[0], gate_grad, up_grad, down_grad
     )
-    grad_spread = together(
-        *[plane_gather_steps(grad_mids[s].astype(BF16), s, pair) for s in range(seqs)]
-    )
     devices = dp_ways * plane_ways
 
+    def small_steps():
+        rows = yield jnp.concatenate(
+            [router_grad.reshape(devices, -1), ffn_sum.reshape(devices, -1)], axis=1
+        )
+        yield exchange(rows, every_exchange)
+
+    outcome_lines = []
+
+    def outcome_steps():
+        rows = yield out_lines[0]
+        outcome_lines.append(dot_tn(straight_picks[0], rows).astype(BF16))
+        yield outcome_lines[0]
+
+    *pieces, small, _ = together(
+        *[plane_gather_steps(grad_mids[s].astype(BF16), s, pair) for s in range(seqs)],
+        small_steps(),
+        outcome_steps(),
+    )
+    pieces, small = tie(pieces, small)
+    pieces = jax.tree.map(by_rows, pieces)
+
     def outcome(s):
-        back = dot_tn(straight_picks[s], out_lines[s]).astype(BF16)
+        if s == len(outcome_lines):
+            outcome_lines.append(dot_tn(straight_picks[s], out_lines[s]).astype(BF16))
+        back = outcome_lines[s]
         back = lax.psum_scatter(back, "dp", scatter_dimension=0, tiled=True)
         return (middles[s] + back.astype(F32)).astype(BF16)
 
     for s in range(1, seqs):
-        rows, *grad_spread = tie(produced[s], *grad_spread)
-        grad_spread = [by_rows(g) for g in grad_spread]
+        rows, pieces = tie(produced[s], pieces)
+        pieces = jax.tree.map(by_rows, pieces)
         out_lines.append(exchange(rows))
+    grad_spread = []
     grad_qkvs, grad_ins = [], []
     head_sums = jnp.zeros((2, HEAD_DIM), F32)
     for s in range(seqs):
-        flat = grad_spread[s].reshape(seq_total, width)
-        grad_attn = dot_nn(flat, out_local).astype(BF16).reshape(plane_ways, size, local_dim)
+        grad_attn, rows = project(pieces[s], ffn_gain_row, out_local, False, BF16)
+        grad_spread.append(rows)
         grad_qkv, sums = attend_back(
             projected[s],
             tables,
@@ -773,15 +903,9 @@
         head_sums = head_sums + sums[:2]
         grad_qkvs.append(grad_qkv)
     *grad_qkvs, out_lines[-1] = tie(*grad_qkvs, out_lines[-1])
-    small = exchange(
+    head_small = exchange(
         jnp.concatenate(
-            [
-                router_grad.reshape(devices, -1),
-                ffn_sum.reshape(devices, -1),
-                head_sums[0].reshape(devices, -1),
-                head_sums[1].reshape(devices, -1),
-            ],
-            axis=1,
+            [head_sums[0].reshape(devices, -1), head_sums[1].reshape(devices, -1)], axis=1
         ),
         every_exchange,
     )
@@ -793,31 +917,41 @@
         ).astype(BF16)
 
     total = total_over(spread, grad_qkvs)
-    *grad_normeds, qkv_rows = together(
-        *[plane_reduce(times(grad_qkvs[s], qkv_local), s, pair) for s in range(seqs)],
-        line_reduce(
-            lambda k: lax.dynamic_slice_in_dim(
-                total, dp_index_of_slot[k] * weight_rows, weight_rows
-            ),
-            dp_ways,
+    def rows_of_plane(total):
+        return plane_exchange(total).reshape(plane_ways, weight_rows // plane_ways, -1)
+
+    out_total = lax.psum_scatter(
+        total_over(grad_spread, attended), "dp", scatter_dimension=0, tiled=True
+    )
+    out_rows = rows_of_plane(out_total)
+    sums = [plane_reduce(times(grad_qkvs[s], qkv_local), s, pair) for s in range(seqs)]
+    ring_sum = line_reduce(
+        lambda k: lax.dynamic_slice_in_dim(
+            total, dp_index_of_slot[k] * weight_rows, weight_rows
         ),
-    )
+        dp_ways,
+    )
+    held, qkv_rows = [next(move) for move in sums], next(ring_sum)
+    qkv_rows, head_small = tie(qkv_rows, head_small)
+    for turn in range(dp_ways - 1):
+        qkv_rows = ring_sum.send(qkv_rows) if turn else qkv_rows
+        if pair and turn:
+            qkv_rows, *held = tie(qkv_rows, *held)
+            held = [move.send(by_rows(h)) for move, h in zip(sums, held)]
+        if turn == 1:
+            qkv_rows, out_rows = tie(qkv_rows, out_rows)
+    grad_normeds = held
+
     for s in range(seqs):
         grad_in = rms_back(grad_normeds[s].astype(F32), units[s], scales[s], attn_gain_row)
         grad_ins.append((grad_mids[s] + grad_in).astype(BF16))
     input_grad = jnp.stack(grad_ins)
     layer_out = jnp.stack([outcome(s) for s in range(seqs)])
 
-    def rows_of_plane(total):
-        return plane_exchange(total).reshape(plane_ways, weight_rows // plane_ways, -1)
-
     def side_by_side(pieces):
         return pieces.transpose(1, 0, 2).reshape(pieces.shape[1], -1)
 
-    out_total = lax.psum_scatter(
-        total_over(grad_spread, attended), "dp", scatter_dimension=0, tiled=True
-    )
-    out_grad = side_by_side(rows_of_plane(out_total)).astype(F32)
+    out_grad = side_by_side(out_rows).astype(F32)
     pieces = rows_of_plane(qkv_rows).astype(F32)
     row_count = pieces.shape[1]
 
@@ -842,7 +976,7 @@
     attn_gain_grad = jnp.sum(own_rows.astype(F32) * qkv_grad, axis=1) / own_gain
 
     small = jnp.sum(small, axis=0)
-    head_small = small[-2 * (HEAD_DIM // devices) :].reshape(2, -1)
+    head_small = jnp.sum(head_small, axis=0).reshape(2, -1)
     cut = row_count * experts
     return (
         layer_out,

time: 950 us -> 948 us (level)
  waiting for transfers between devices: 401 us -> 372 us
  local copies, waits for them, and re-layouts: 45.9 us -> 65.3 us
  matrix products: 150 us -> 134 us
  starting transfers between devices: 109 us -> 124 us
    ppermute x4, waiting for transfers between devices: 41 us -> 12.4 us  [plane_gather_steps(): four = (yield jnp.concatenate([two, lax.ppermute(two, PLANE, second)]))]
    dot_general x10 -> x6, matrix products: 47.6 us -> 24.8 us  [dot_nn(): return jnp.dot(a, b, preferred_element_type=F32)]
    ppermute x6 -> x9, waiting for transfers between devices: 78.9 us -> 57.8 us  [line_spread(): lax.ppermute(rows, 'dp', ring_jumps(ways, k))]
    all_gather x1, waiting for transfers between devices: 0.01 us -> 16.9 us  [body(): lax.all_gather(jnp.concatenate([columns(qkv_weight, plane_index * local_d...]
    unnamed x183 -> x202, local copies, waits for them, and re-layouts: 6.31 us -> 18.4 us
    ppermute x3, waiting for transfers between devices: 19.6 us -> 31 us  [line_reduce(): acc = lax.ppermute(acc, 'dp', back)]
    all_to_all x1 -> x2, starting transfers between devices: 3.49 us -> 13.7 us  [every_exchange(): return lax.all_to_all(rows, EVERY, split_axis=0, concat_axis=0, tiled=True)]
    concatenate x5 -> x3, other arithmetic: 9.79 us -> 0.03 us  [the longest x1 0.02 us: small_steps(): jnp.concatenate([router_grad.reshape(devices, -1), ffn_sum.reshape(device...]
  transfers between devices with their start and end apart: 64 -> 65, of which waited for: 39 -> 41; matrix products, arithmetic and copies ran while one was open for 25% -> 25% of each run, Pallas kernels for 16% -> 15%
where the time goes in v3:
time: 948 us; the launch traced here: 936 us
  waiting for transfers between devices  372 us (39%)
  Pallas kernels  150 us (16%)
  matrix products  134 us (14%)
  starting transfers between devices  124 us (13%)
  other arithmetic  73.2 us (8%)
  local copies, waits for them, and re-layouts  65.3 us (7%)
  between operations  18.3 us (2%)
    ppermute x6, waiting for transfers between devices, line_gather(): held = lax.ppermute(held, 'dp', ring_steps(ways))  88.5 us
    dot_general x16, matrix products, dot_tn(): lax.dot_general(a, b, (((0,), (0,)), ((), ())), preferred_element_type=F32)  83.7 us
    all_to_all x10, waiting for transfers between devices, plane_exchange(): return lax.all_to_all(rows, PLANE, split_axis=0, concat_axis=0, tiled=True)  65.9 us
    pallas_call x2, Pallas kernels, expert_pass(): pl.pallas_call(functools.partial(expert_kernel, experts), grid_spec=pltpu...  60.3 us
    ppermute x9, waiting for transfers between devices, line_spread(): lax.ppermute(rows, 'dp', ring_jumps(ways, k))  57.8 us
    pallas_call x2, Pallas kernels, attend_back(): pl.pallas_call(functools.partial(attend_back_kernel, heads), grid_spec=pl...  47.2 us
    all_to_all x10, starting transfers between devices, plane_exchange(): return lax.all_to_all(rows, PLANE, split_axis=0, concat_axis=0, tiled=True)  45.4 us
    ppermute x6, waiting for transfers between devices, line_sum(): total = total + lax.ppermute(part, 'dp', ring_jumps(ways, -k)).astype(F32)  32.3 us
  transfers between devices with their start and end apart: 65, of which 41 were waited for; matrix products, arithmetic and copies ran while one was open for 25% of the time, Pallas kernels for 15%

profile of v3, /device:TPU:0, one launch (start us, length us, event | category | flops | bytes accessed | tf_op | source)
XLA Modules:
  0.0 936.4 jit_solution(13226330762381602604)
XLA Ops:
  15.8 10.0 %collective-permute-done.1 = bf16[128,2048]{1,0:T(8,128)(2,1)} collective-permute-done((bf16[128,2048]{1,0:T(8,128)(2,1)S(1)}, bf16[128,2048]{1,0:T(8,128)(2,1)}, u32[]{:S(2)}, u32[]{:S(2)}) %collective-permute-start.1) | collective-permute-done | bytes 524320 | tf_op jit(solution)/shard_map/ppermute | solution.py:535
  39.1 12.4 %collective-permute-done.2 = bf16[2,128,2048]{2,1,0:T(8,128)(2,1)S(1)} collective-permute-done((bf16[2,128,2048]{2,1,0:T(8,128)(2,1)S(1)}, bf16[2,128,2048]{2,1,0:T(8,128)(2,1)S(1)}, u32[]{:S(2)}, u32[]{:S(2)}) %collective-permute-start.2) | collective-permute-done | bytes 1048608 | tf_op jit(solution)/shard_map/ppermute | solution.py:536
  60.5 16.9 %all-gather.3.cloned.1.call-done.refs_3_ = bf16[2048,768]{1,0:T(8,128)(2,1)} async-done(((bf16[512,768]{1,0:T(8,128)(2,1)}), bf16[2048,768]{1,0:T(8,128)(2,1)}) %all-gather.3.cloned.1.call-update) | async-done | bytes 3145744 | tf_op jit(solution)/shard_map/all_gather | solution.py:645
  86.3 8.5 shard_map.247
  96.5 9.6 %shard_map.248 = (bf16[8,128,512]{2,1,0:T(8,128)(2,1)S(1)}, f32[4,4,256,128]{3,2,1,0:T(8,128)S(1)}) custom-call(s32[8]{0:T(128)S(1)} %get-tuple-element.384.order_ref, s32[4]{0:T(128)S(1)} %convert_reduce_fusion.1.low_ref, f32[8,128,768]{2,1,0:T(8,128)} %copy-done.2, f32[8,128,768]{2,1,0:T(8,128)} %copy-done.2, ...), custom_call_target="tpu_custom_call" | custom-call | flops 536870912 | bytes 6291456 | tf_op jit(solution)/shard_map/pallas_call | solution.py:288
  106.1 8.4 shard_map.249
  118.2 8.9 shard_map.250
  162.0 8.5 collective-permute-done.16
  211.6 10.1 %collective-permute-start.24 = (bf16[128,2176]{1,0:T(8,128)(2,1)}, bf16[128,2176]{1,0:T(8,128)(2,1)S(1)}, u32[]{:S(2)}, u32[]{:S(2)}) collective-permute-start(bf16[128,2176]{1,0:T(8,128)(2,1)} %concatenate.63), channel_id=1, source_target_pairs={{8,24},{24,16},{16,0},{0,8},{9,25},{25,17},{17,1},{1,9},{10,26},{2... | collective-permute-start | bytes 1671176 | tf_op jit(solution)/shard_map/ppermute | solution.py:498
  221.7 14.3 %collective-permute-done.24 = bf16[128,2176]{1,0:T(8,128)(2,1)S(1)} collective-permute-done((bf16[128,2176]{1,0:T(8,128)(2,1)}, bf16[128,2176]{1,0:T(8,128)(2,1)S(1)}, u32[]{:S(2)}, u32[]{:S(2)}) %collective-permute-start.24) | collective-permute-done | bytes 557088 | tf_op jit(solution)/shard_map/ppermute | solution.py:498
  236.8 14.5 %collective-permute-done.25 = bf16[128,2176]{1,0:T(8,128)(2,1)S(1)} collective-permute-done((bf16[128,2176]{1,0:T(8,128)(2,1)S(1)}, bf16[128,2176]{1,0:T(8,128)(2,1)S(1)}, u32[]{:S(2)}, u32[]{:S(2)}) %collective-permute-start.25) | collective-permute-done | bytes 557088 | tf_op jit(solution)/shard_map/ppermute | solution.py:498
  251.7 14.4 %collective-permute-done.26 = bf16[128,2176]{1,0:T(8,128)(2,1)S(1)} collective-permute-done((bf16[128,2176]{1,0:T(8,128)(2,1)S(1)}, bf16[128,2176]{1,0:T(8,128)(2,1)S(1)}, u32[]{:S(2)}, u32[]{:S(2)}) %collective-permute-start.26) | collective-permute-done | bytes 557088 | tf_op jit(solution)/shard_map/ppermute | solution.py:498
  279.8 22.7 %collective-permute-done.23 = bf16[128,2048]{1,0:T(8,128)(2,1)S(1)} collective-permute-done((bf16[128,2048]{1,0:T(8,128)(2,1)}, bf16[128,2048]{1,0:T(8,128)(2,1)S(1)}, u32[]{:S(2)}, u32[]{:S(2)}) %collective-permute-start.23) | collective-permute-done | bytes 524320 | tf_op jit(solution)/shard_map/ppermute | solution.py:509
  303.3 21.8 %collective-permute-done.21 = bf16[128,2048]{1,0:T(8,128)(2,1)S(1)} collective-permute-done((bf16[128,2048]{1,0:T(8,128)(2,1)}, bf16[128,2048]{1,0:T(8,128)(2,1)S(1)}, u32[]{:S(2)}, u32[]{:S(2)}) %collective-permute-start.21) | collective-permute-done | bytes 524320 | tf_op jit(solution)/shard_map/ppermute | solution.py:509
  343.3 16.0 %collective-permute-done.18 = bf16[128,2176]{1,0:T(8,128)(2,1)S(1)} collective-permute-done((bf16[128,2176]{1,0:T(8,128)(2,1)}, bf16[128,2176]{1,0:T(8,128)(2,1)S(1)}, u32[]{:S(2)}, u32[]{:S(2)}) %collective-permute-start.18) | collective-permute-done | bytes 557088 | tf_op jit(solution)/shard_map/ppermute | solution.py:498
  359.3 15.0 %collective-permute-done.19 = bf16[128,2176]{1,0:T(8,128)(2,1)S(1)} collective-permute-done((bf16[128,2176]{1,0:T(8,128)(2,1)S(1)}, bf16[128,2176]{1,0:T(8,128)(2,1)S(1)}, u32[]{:S(2)}, u32[]{:S(2)}) %collective-permute-start.19) | collective-permute-done | bytes 557088 | tf_op jit(solution)/shard_map/ppermute | solution.py:498
  374.3 14.2 %collective-permute-done.20 = bf16[128,2176]{1,0:T(8,128)(2,1)S(1)} collective-permute-done((bf16[128,2176]{1,0:T(8,128)(2,1)S(1)}, bf16[128,2176]{1,0:T(8,128)(2,1)S(1)}, u32[]{:S(2)}, u32[]{:S(2)}) %collective-permute-start.20) | collective-permute-done | bytes 557088 | tf_op jit(solution)/shard_map/ppermute | solution.py:498
  399.7 30.2 %shard_map.252 = (bf16[1152,768]{1,0:T(8,128)(2,1)}, bf16[1152,768]{1,0:T(8,128)(2,1)}, bf16[1152,768]{1,0:T(8,128)(2,1)}, bf16[1152,2176]{1,0:T(8,128)(2,1)}, bf16[1152,2048]{1,0:T(8,128)(2,1)}) custom-call(s32[1]{0:T(128)} %bitcast.37.expert_ref, bf16[1152,2176]{1,0:T(8,128)(2,1)} %bitcast.50.rows_ref.gates_ref, ...), custom_call_target="tpu_custom_call" | custom-call | flops 5435817984 | bytes 9437184 | tf_op jit(solution)/shard_map/pallas_call | solution.py:459
  429.9 26.8 %all-to-all-done.3 = bf16[8,144,2176]{2,1,0:T(8,128)(2,1)} async-done(((bf16[8,144,2176]{2,1,0:T(8,128)(2,1)}), bf16[8,144,2176]{2,1,0:T(8,128)(2,1)}, u32[]{:S(2)}, u32[]{:S(2)}) %all-to-all-start.3) | async-done | bytes 5013536 | tf_op jit(solution)/shard_map/all_to_all | solution.py:601
  472.1 30.1 %shard_map.251 = (bf16[1152,768]{1,0:T(8,128)(2,1)}, bf16[1152,768]{1,0:T(8,128)(2,1)}, bf16[1152,768]{1,0:T(8,128)(2,1)}, bf16[1152,2176]{1,0:T(8,128)(2,1)}, bf16[1152,2048]{1,0:T(8,128)(2,1)}) custom-call(s32[1]{0:T(128)} %bitcast.37.expert_ref, bf16[1152,2176]{1,0:T(8,128)(2,1)} %bitcast.54.rows_ref.gates_ref, ...), custom_call_target="tpu_custom_call" | custom-call | flops 5435817984 | bytes 9437184 | tf_op jit(solution)/shard_map/pallas_call | solution.py:459
  502.2 16.4 %all-to-all-done.4 = bf16[8,144,2176]{2,1,0:T(8,128)(2,1)} async-done(((bf16[8,144,2176]{2,1,0:T(8,128)(2,1)}), bf16[8,144,2176]{2,1,0:T(8,128)(2,1)}, u32[]{:S(2)}, u32[]{:S(2)}) %all-to-all-start.4) | async-done | bytes 5013536 | tf_op jit(solution)/shard_map/all_to_all | solution.py:601
  534.2 6.9 fusion.96
  565.5 8.7 convolution_add_fusion
  597.5 32.3 %collective-permute-done.30 = bf16[128,2176]{1,0:T(8,128)(2,1)S(1)} collective-permute-done((bf16[128,2176]{1,0:T(8,128)(2,1)S(1)}, bf16[128,2176]{1,0:T(8,128)(2,1)S(1)}, u32[]{:S(2)}, u32[]{:S(2)}) %collective-permute-start.30) | collective-permute-done | bytes 557088 | tf_op jit(solution)/shard_map/ppermute | solution.py:518
  650.7 8.3 collective-permute-done.34
  667.9 10.9 %all-to-all-start.7 = ((f32[32,1,2112]{2,1,0:T(1,128)}), f32[32,1,2112]{2,1,0:T(1,128)}, u32[]{:S(2)}, u32[]{:S(2)}) async-start(f32[32,1,2112]{2,1,0:T(1,128)} %copy.141), calls=%async_computation.8 | async-start | bytes 557056 | tf_op jit(solution)/shard_map/all_to_all | solution.py:597
  728.8 23.6 %shard_map.256 = (bf16[8,128,768]{2,1,0:T(8,128)(2,1)}, f32[8,128]{1,0:T(8,128)}) custom-call(s32[8]{0:T(128)} %copy-done.28, s32[4]{0:T(128)} %copy-done.29, f32[8,128,768]{2,1,0:T(8,128)} %copy-done.3, f32[8,128,768]{2,1,0:T(8,128)} %copy-done.3, f32[4,256,128]{2,1,0:T(8,128)} %copy-done.4, f32[4,256,128]{2,1,0:T(8,128)} %copy-done.5, f32[1,128]{1,0:T(1,128)} %bitcast.287, ...), custom_call_target="tpu_custom_call" | custom-call | flops 1073741824 | bytes 9437184 | tf_op jit(solution)/shard_map/pallas_call | solution.py:320
  752.4 23.6 %shard_map.254 = (bf16[8,128,768]{2,1,0:T(8,128)(2,1)}, f32[8,128]{1,0:T(8,128)}) custom-call(s32[8]{0:T(128)} %copy-done.27, s32[4]{0:T(128)} %copy-done.26, f32[8,128,768]{2,1,0:T(8,128)} %copy-done.2, f32[8,128,768]{2,1,0:T(8,128)} %copy-done.2, f32[4,256,128]{2,1,0:T(8,128)} %copy-done.4, f32[4,256,128]{2,1,0:T(8,128)} %copy-done.5, f32[1,128]{1,0:T(1,128)} %bitcast.288, ...), custom_call_target="tpu_custom_call" | custom-call | flops 1073741824 | bytes 9437184 | tf_op jit(solution)/shard_map/pallas_call | solution.py:320
  791.4 10.3 %collective-permute-start.39 = (bf16[512,768]{1,0:T(8,128)(2,1)}, bf16[512,768]{1,0:T(8,128)(2,1)}, u32[]{:S(2)}, u32[]{:S(2)}) collective-permute-start(bf16[512,768]{1,0:T(8,128)(2,1)} %constant_dynamic-slice_fusion), channel_id=1, source_target_pairs={{24,8},{16,24},{0,16},{8,0},{25,9},{17,25},{1,17},{9,1},{26,10},{1... | collective-permute-start | bytes 2359304 | tf_op jit(solution)/shard_map/ppermute | solution.py:526
  813.0 18.1 %collective-permute-done.39 = bf16[512,768]{1,0:T(8,128)(2,1)} collective-permute-done((bf16[512,768]{1,0:T(8,128)(2,1)}, bf16[512,768]{1,0:T(8,128)(2,1)}, u32[]{:S(2)}, u32[]{:S(2)}) %collective-permute-start.39) | collective-permute-done | bytes 786464 | tf_op jit(solution)/shard_map/ppermute | solution.py:526
  846.8 7.9 collective-permute-done.40
  910.8 8.5 all-to-all-done.11
  (494 shorter events, 429.4 us)
Async XLA Ops:
  7.2 70.2 %all-gather.3.cloned.1.call-start = ((), (), s32[]{:S(2)}) async-start(), calls=%async_computation.15 | async-start | bytes 3932160 | tf_op jit(solution)/shard_map/all_gather | solution.py:645
  10.4 119.8 %all-gather.5.cloned.1.call-start = ((), (), s32[]{:S(2)}) async-start(), calls=%async_computation.16 | async-start | bytes 2621440 | tf_op jit(solution)/shard_map/all_gather | solution.py:745
  150.8 25.9 %collective-permute-start.12 = (bf16[2,128,2048]{2,1,0:T(8,128)(2,1)}, bf16[2,128,2048]{2,1,0:T(8,128)(2,1)}, u32[]{:S(2)}, u32[]{:S(2)}) collective-permute-start(bf16[2,128,2048]{2,1,0:T(8,128)(2,1)} %slice.246), channel_id=1, source_target_pairs={{0,4},{1,5},{2,6},{3,7},{4,0},{5,1},{6,2},{7,3},{8,12},{9,13},{10,... | collective-permute-start | bytes 3145736 | tf_op jit(solution)/shard_map/ppermute | solution.py:585
  157.4 28.7 %collective-permute-start.17 = (bf16[128,2048]{1,0:T(8,128)(2,1)}, bf16[128,2048]{1,0:T(8,128)(2,1)S(1)}, u32[]{:S(2)}, u32[]{:S(2)}) collective-permute-start(bf16[128,2048]{1,0:T(8,128)(2,1)} %get-tuple-element.155), channel_id=1, source_target_pairs={{8,0},{24,8},{16,24},{0,16},{9,1},{25,9},{17,25},{1,17},{10,2},{26... | collective-permute-start | bytes 1572872 | tf_op jit(solution)/shard_map/ppermute | solution.py:509
  159.2 24.8 %collective-permute-start.11 = (bf16[2,128,2048]{2,1,0:T(8,128)(2,1)S(1)}, bf16[2,128,2048]{2,1,0:T(8,128)(2,1)S(1)}, u32[]{:S(2)}, u32[]{:S(2)}) collective-permute-start(bf16[2,128,2048]{2,1,0:T(8,128)(2,1)S(1)} %slice.244), channel_id=1, source_target_pairs={{0,1},{1,0},{2,3},{3,2},{4,5},{5,4},{6,7},{7,6},{8,9},{9,8},{10,11... | collective-permute-start | bytes 3145736 | tf_op jit(solution)/shard_map/ppermute | solution.py:585
  199.5 73.1 %all-to-all-start = ((bf16[8,144,2048]{2,1,0:T(8,128)(2,1)}), bf16[8,144,2048]{2,1,0:T(8,128)(2,1)}, u32[]{:S(2)}, u32[]{:S(2)}) async-start(bf16[8,144,2048]{2,1,0:T(8,128)(2,1)} %bitcast.311), calls=%async_computation | async-start | bytes 9437184 | tf_op jit(solution)/shard_map/all_to_all | solution.py:601
  211.6 24.3 %collective-permute-start.24 = (bf16[128,2176]{1,0:T(8,128)(2,1)}, bf16[128,2176]{1,0:T(8,128)(2,1)S(1)}, u32[]{:S(2)}, u32[]{:S(2)}) collective-permute-start(bf16[128,2176]{1,0:T(8,128)(2,1)} %concatenate.63), channel_id=1, source_target_pairs={{8,24},{24,16},{16,0},{0,8},{9,25},{25,17},{17,1},{1,9},{10,26},{2... | collective-permute-start | bytes 1671176 | tf_op jit(solution)/shard_map/ppermute | solution.py:498
  272.6 61.7 %all-to-all-start.1 = ((bf16[8,144,2176]{2,1,0:T(8,128)(2,1)}), bf16[8,144,2176]{2,1,0:T(8,128)(2,1)}, u32[]{:S(2)}, u32[]{:S(2)}) async-start(bf16[8,144,2176]{2,1,0:T(8,128)(2,1)} %bitcast.303), calls=%async_computation.1 | async-start | bytes 10027008 | tf_op jit(solution)/shard_map/all_to_all | solution.py:601
  277.2 25.3 %collective-permute-start.23 = (bf16[128,2048]{1,0:T(8,128)(2,1)}, bf16[128,2048]{1,0:T(8,128)(2,1)S(1)}, u32[]{:S(2)}, u32[]{:S(2)}) collective-permute-start(bf16[128,2048]{1,0:T(8,128)(2,1)} %get-tuple-element.161), channel_id=1, source_target_pairs={{8,0},{24,8},{16,24},{0,16},{9,1},{25,9},{17,25},{1,17},{10,2},{26... | collective-permute-start | bytes 1572872 | tf_op jit(solution)/shard_map/ppermute | solution.py:509
  277.3 26.0 %collective-permute-start.22 = (bf16[128,2048]{1,0:T(8,128)(2,1)}, bf16[128,2048]{1,0:T(8,128)(2,1)S(1)}, u32[]{:S(2)}, u32[]{:S(2)}) collective-permute-start(bf16[128,2048]{1,0:T(8,128)(2,1)} %get-tuple-element.161), channel_id=1, source_target_pairs={{8,16},{24,0},{16,8},{0,24},{9,17},{25,1},{17,9},{1,25},{10,18},{2... | collective-permute-start | bytes 1572872 | tf_op jit(solution)/shard_map/ppermute | solution.py:509
  279.0 46.1 %collective-permute-start.21 = (bf16[128,2048]{1,0:T(8,128)(2,1)}, bf16[128,2048]{1,0:T(8,128)(2,1)S(1)}, u32[]{:S(2)}, u32[]{:S(2)}) collective-permute-start(bf16[128,2048]{1,0:T(8,128)(2,1)} %get-tuple-element.161), channel_id=1, source_target_pairs={{8,24},{24,16},{16,0},{0,8},{9,25},{25,17},{17,1},{1,9},{10,26},{2... | collective-permute-start | bytes 1572872 | tf_op jit(solution)/shard_map/ppermute | solution.py:509
  334.3 60.6 %all-to-all-start.2 = ((bf16[8,144,2048]{2,1,0:T(8,128)(2,1)}), bf16[8,144,2048]{2,1,0:T(8,128)(2,1)}, u32[]{:S(2)}, u32[]{:S(2)}) async-start(bf16[8,144,2048]{2,1,0:T(8,128)(2,1)} %bitcast.312), calls=%async_computation.2 | async-start | bytes 9437184 | tf_op jit(solution)/shard_map/all_to_all | solution.py:601
  394.9 61.8 %all-to-all-start.3 = ((bf16[8,144,2176]{2,1,0:T(8,128)(2,1)}), bf16[8,144,2176]{2,1,0:T(8,128)(2,1)}, u32[]{:S(2)}, u32[]{:S(2)}) async-start(bf16[8,144,2176]{2,1,0:T(8,128)(2,1)} %bitcast.305), calls=%async_computation.3 | async-start | bytes 10027008 | tf_op jit(solution)/shard_map/all_to_all | solution.py:601
  456.7 61.9 %all-to-all-start.4 = ((bf16[8,144,2176]{2,1,0:T(8,128)(2,1)}), bf16[8,144,2176]{2,1,0:T(8,128)(2,1)}, u32[]{:S(2)}, u32[]{:S(2)}) async-start(bf16[8,144,2176]{2,1,0:T(8,128)(2,1)} %bitcast.304), calls=%async_computation.4 | async-start | bytes 10027008 | tf_op jit(solution)/shard_map/all_to_all | solution.py:601
  518.6 61.7 %all-to-all-start.5 = ((bf16[8,144,2176]{2,1,0:T(8,128)(2,1)}), bf16[8,144,2176]{2,1,0:T(8,128)(2,1)}, u32[]{:S(2)}, u32[]{:S(2)}) async-start(bf16[8,144,2176]{2,1,0:T(8,128)(2,1)} %bitcast.302), calls=%async_computation.5 | async-start | bytes 10027008 | tf_op jit(solution)/shard_map/all_to_all | solution.py:601
  530.3 62.7 %collective-permute-start.27 = (bf16[128,2176]{1,0:T(8,128)(2,1)}, bf16[128,2176]{1,0:T(8,128)(2,1)}, u32[]{:S(2)}, u32[]{:S(2)}) collective-permute-start(bf16[128,2176]{1,0:T(8,128)(2,1)} %get-tuple-element.328), channel_id=1, source_target_pairs={{8,0},{24,8},{16,24},{0,16},{9,1},{25,9},{17,25},{1,17},{10,2},{26... | collective-permute-start | bytes 1671176 | tf_op jit(solution)/shard_map/ppermute | solution.py:518
  531.1 63.4 %collective-permute-start.29 = (bf16[128,2176]{1,0:T(8,128)(2,1)}, bf16[128,2176]{1,0:T(8,128)(2,1)}, u32[]{:S(2)}, u32[]{:S(2)}) collective-permute-start(bf16[128,2176]{1,0:T(8,128)(2,1)} %get-tuple-element.329), channel_id=1, source_target_pairs={{8,24},{24,16},{16,0},{0,8},{9,25},{25,17},{17,1},{1,9},{10,26},{2... | collective-permute-start | bytes 1671176 | tf_op jit(solution)/shard_map/ppermute | solution.py:518
  532.8 61.7 %collective-permute-start.28 = (bf16[128,2176]{1,0:T(8,128)(2,1)}, bf16[128,2176]{1,0:T(8,128)(2,1)}, u32[]{:S(2)}, u32[]{:S(2)}) collective-permute-start(bf16[128,2176]{1,0:T(8,128)(2,1)} %get-tuple-element.330), channel_id=1, source_target_pairs={{8,16},{24,0},{16,8},{0,24},{9,17},{25,1},{17,9},{1,25},{10,18},{2... | collective-permute-start | bytes 1671176 | tf_op jit(solution)/shard_map/ppermute | solution.py:518
  580.3 58.5 %all-to-all-start.6 = ((bf16[8,144,2048]{2,1,0:T(8,128)(2,1)}), bf16[8,144,2048]{2,1,0:T(8,128)(2,1)}, u32[]{:S(2)}, u32[]{:S(2)}) async-start(bf16[8,144,2048]{2,1,0:T(8,128)(2,1)} %bitcast.310), calls=%async_computation.6 | async-start | bytes 9437184 | tf_op jit(solution)/shard_map/all_to_all | solution.py:601
  591.0 38.8 %collective-permute-start.30 = (bf16[128,2176]{1,0:T(8,128)(2,1)S(1)}, bf16[128,2176]{1,0:T(8,128)(2,1)S(1)}, u32[]{:S(2)}, u32[]{:S(2)}) collective-permute-start(bf16[128,2176]{1,0:T(8,128)(2,1)S(1)} %get-tuple-element.325), channel_id=1, source_target_pairs={{8,0},{24,8},{16,24},{0,16},{9,1},{25,9},{17,25},{1,17},{10,2},{26... | collective-permute-start | bytes 1671176 | tf_op jit(solution)/shard_map/ppermute | solution.py:518
  591.0 38.8 %collective-permute-start.32 = (bf16[128,2176]{1,0:T(8,128)(2,1)S(1)}, bf16[128,2176]{1,0:T(8,128)(2,1)S(1)}, u32[]{:S(2)}, u32[]{:S(2)}) collective-permute-start(bf16[128,2176]{1,0:T(8,128)(2,1)S(1)} %get-tuple-element.326), channel_id=1, source_target_pairs={{8,24},{24,16},{16,0},{0,8},{9,25},{25,17},{17,1},{1,9},{10,26},{2... | collective-permute-start | bytes 1671176 | tf_op jit(solution)/shard_map/ppermute | solution.py:518
  593.1 36.7 %collective-permute-start.31 = (bf16[128,2176]{1,0:T(8,128)(2,1)S(1)}, bf16[128,2176]{1,0:T(8,128)(2,1)S(1)}, u32[]{:S(2)}, u32[]{:S(2)}) collective-permute-start(bf16[128,2176]{1,0:T(8,128)(2,1)S(1)} %get-tuple-element.327), channel_id=1, source_target_pairs={{8,16},{24,0},{16,8},{0,24},{9,17},{25,1},{17,9},{1,25},{10,18},{2... | collective-permute-start | bytes 1671176 | tf_op jit(solution)/shard_map/ppermute | solution.py:518
  664.6 29.3 %collective-permute-start.35 = (bf16[2,128,2048]{2,1,0:T(8,128)(2,1)}, bf16[2,128,2048]{2,1,0:T(8,128)(2,1)}, u32[]{:S(2)}, u32[]{:S(2)}) collective-permute-start(bf16[2,128,2048]{2,1,0:T(8,128)(2,1)} %pad_maximum_fusion.6), channel_id=1, source_target_pairs={{0,1},{1,0},{2,3},{3,2},{4,5},{5,4},{6,7},{7,6},{8,9},{9,8},{10,11... | collective-permute-start | bytes 3145736 | tf_op jit(solution)/shard_map/ppermute | solution.py:536
  665.5 30.1 %collective-permute-start.36 = (bf16[2,128,2048]{2,1,0:T(8,128)(2,1)S(1)}, bf16[2,128,2048]{2,1,0:T(8,128)(2,1)}, u32[]{:S(2)}, u32[]{:S(2)}) collective-permute-start(bf16[2,128,2048]{2,1,0:T(8,128)(2,1)S(1)} %pad_maximum_fusion.7), channel_id=1, source_target_pairs={{0,4},{1,5},{2,6},{3,7},{4,0},{5,1},{6,2},{7,3},{8,12},{9,13},{10,... | collective-permute-start | bytes 3145736 | tf_op jit(solution)/shard_map/ppermute | solution.py:536
  678.8 164.4 %reduce-scatter.8.cloned.1.call-start = ((), (), s32[]{:S(2)}) async-start(), calls=%async_computation.19 | async-start | bytes 2621440 | tf_op jit(solution)/shard_map/reduce_scatter | solution.py:923
  719.7 58.5 %all-to-all-start.8 = ((bf16[8,144,2048]{2,1,0:T(8,128)(2,1)}), bf16[8,144,2048]{2,1,0:T(8,128)(2,1)}, u32[]{:S(2)}, u32[]{:S(2)}) async-start(bf16[8,144,2048]{2,1,0:T(8,128)(2,1)} %bitcast.309), calls=%async_computation.9 | async-start | bytes 9437184 | tf_op jit(solution)/shard_map/all_to_all | solution.py:601
  724.3 199.6 %reduce-scatter.4.cloned.1.call-start = ((), (), s32[]{:S(2)}) async-start(), calls=%async_computation.17 | async-start | bytes 2621440 | tf_op jit(solution)/shard_map/reduce_scatter | solution.py:878
  791.4 39.8 %collective-permute-start.39 = (bf16[512,768]{1,0:T(8,128)(2,1)}, bf16[512,768]{1,0:T(8,128)(2,1)}, u32[]{:S(2)}, u32[]{:S(2)}) collective-permute-start(bf16[512,768]{1,0:T(8,128)(2,1)} %constant_dynamic-slice_fusion), channel_id=1, source_target_pairs={{24,8},{16,24},{0,16},{8,0},{25,9},{17,25},{1,17},{9,1},{26,10},{1... | collective-permute-start | bytes 2359304 | tf_op jit(solution)/shard_map/ppermute | solution.py:526
  804.9 51.4 %collective-permute-start.41 = (bf16[4,128,2048]{2,1,0:T(8,128)(2,1)}, bf16[4,128,2048]{2,1,0:T(8,128)(2,1)}, u32[]{:S(2)}, u32[]{:S(2)}) collective-permute-start(bf16[4,128,2048]{2,1,0:T(8,128)(2,1)} %bitcast.88), channel_id=1, source_target_pairs={{0,2},{1,3},{2,0},{3,1},{4,6},{5,7},{6,4},{7,5},{8,10},{9,11},{10,... | collective-permute-start | bytes 6291464 | tf_op jit(solution)/shard_map/ppermute | solution.py:582
  809.0 49.8 %collective-permute-start.42 = (bf16[4,128,2048]{2,1,0:T(8,128)(2,1)}, bf16[4,128,2048]{2,1,0:T(8,128)(2,1)}, u32[]{:S(2)}, u32[]{:S(2)}) collective-permute-start(bf16[4,128,2048]{2,1,0:T(8,128)(2,1)} %bitcast.92), channel_id=1, source_target_pairs={{0,2},{1,3},{2,0},{3,1},{4,6},{5,7},{6,4},{7,5},{8,10},{9,11},{10,... | collective-permute-start | bytes 6291464 | tf_op jit(solution)/shard_map/ppermute | solution.py:582
  810.2 24.9 %all-to-all-start.9 = ((f32[32,1,8]{2,1,0:T(1,128)}), f32[32,1,8]{2,1,0:T(1,128)S(1)}, u32[]{:S(2)}, u32[]{:S(2)}) async-start(f32[32,1,8]{2,1,0:T(1,128)} %bitcast.82), calls=%async_computation.11 | async-start | bytes 32768 | tf_op jit(solution)/shard_map/all_to_all | solution.py:597
  846.7 77.3 %reduce-scatter.6.cloned.1.call-start = ((), (), s32[]{:S(2)}) async-start(), calls=%async_computation.18 | async-start | bytes 2621440 | tf_op jit(solution)/shard_map/reduce_scatter | solution.py:878
  (128 other events, 1760.1 us)
Sparse Core Ops, SparseCore 0:
  10.5 66.8 all-gather.2
  79.6 44.5 all-gather.4
  719.8 50.9 reduce-scatter.7
  773.1 53.6 reduce-scatter.3
  876.4 43.1 reduce-scatter.5

commit v4 on v3

--- a/solution.py
+++ b/solution.py
@@ -859,8 +859,7 @@
     outcome_lines = []
 
     def outcome_steps():
-        rows = yield out_lines[0]
-        outcome_lines.append(dot_tn(straight_picks[0], rows).astype(BF16))
+        outcome_lines.append(dot_tn(straight_picks[0], out_lines[0]).astype(BF16))
         yield outcome_lines[0]
 
     *pieces, small, _ = together(
@@ -882,11 +881,13 @@
         rows, pieces = tie(produced[s], pieces)
         pieces = jax.tree.map(by_rows, pieces)
         out_lines.append(exchange(rows))
-    grad_spread = []
+    grad_spread, layer_outs = [], [outcome(0)]
     grad_qkvs, grad_ins = [], []
     head_sums = jnp.zeros((2, HEAD_DIM), F32)
     for s in range(seqs):
         grad_attn, rows = project(pieces[s], ffn_gain_row, out_local, False, BF16)
+        if s == 0:
+            grad_attn, layer_outs[0] = tie(grad_attn, layer_outs[0])
         grad_spread.append(rows)
         grad_qkv, sums = attend_back(
             projected[s],
@@ -946,7 +947,7 @@
         grad_in = rms_back(grad_normeds[s].astype(F32), units[s], scales[s], attn_gain_row)
         grad_ins.append((grad_mids[s] + grad_in).astype(BF16))
     input_grad = jnp.stack(grad_ins)
-    layer_out = jnp.stack([outcome(s) for s in range(seqs)])
+    layer_out = jnp.stack(layer_outs + [outcome(s) for s in range(1, seqs)])
 
     def side_by_side(pieces):
         return pieces.transpose(1, 0, 2).reshape(pieces.shape[1], -1)

time: 948 us -> 934 us (0.985)
  waiting for transfers between devices: 372 us -> 341 us
  blocking collectives: 0 us -> 26.2 us
  starting transfers between devices: 124 us -> 111 us
    all_to_all x0 -> x1, blocking collectives: none -> 26.2 us  [every_exchange(): return lax.all_to_all(rows, EVERY, split_axis=0, concat_axis=0, tiled=True)]
    ppermute x3, waiting for transfers between devices: 31 us -> 18.2 us  [line_reduce(): acc = lax.ppermute(acc, 'dp', back)]
    ppermute x4, waiting for transfers between devices: 21.8 us -> 10.2 us  [plane_gather_steps(): two = (yield jnp.stack([rows, lax.ppermute(rows, PLANE, first)]))]
  transfers between devices with their start and end apart: 65 -> 64, of which waited for: 41 -> 37; matrix products, arithmetic and copies ran while one was open for 25% -> 26% of each run, Pallas kernels for 15% -> 17%
where the time goes in v4:
time: 934 us; the launch traced here: 921 us
  waiting for transfers between devices  341 us (37%)
  Pallas kernels  153 us (16%)
  matrix products  135 us (14%)
  starting transfers between devices  111 us (12%)
  other arithmetic  74.7 us (8%)
  local copies, waits for them, and re-layouts  63.3 us (7%)
  blocking collectives  26.2 us (3%)
  between operations  18.4 us (2%)
    ppermute x6, waiting for transfers between devices, line_gather(): held = lax.ppermute(held, 'dp', ring_steps(ways))  88.6 us
    dot_general x16, matrix products, dot_tn(): lax.dot_general(a, b, (((0,), (0,)), ((), ())), preferred_element_type=F32)  84.3 us
    all_to_all x10, waiting for transfers between devices, plane_exchange(): return lax.all_to_all(rows, PLANE, split_axis=0, concat_axis=0, tiled=True)  63.9 us
    pallas_call x2, Pallas kernels, expert_pass(): pl.pallas_call(functools.partial(expert_kernel, experts), grid_spec=pltpu...  60.3 us
    ppermute x9, waiting for transfers between devices, line_spread(): lax.ppermute(rows, 'dp', ring_jumps(ways, k))  57.8 us
    all_to_all x10, starting transfers between devices, plane_exchange(): return lax.all_to_all(rows, PLANE, split_axis=0, concat_axis=0, tiled=True)  45.2 us
    pallas_call x2, Pallas kernels, attend_back(): pl.pallas_call(functools.partial(attend_back_kernel, heads), grid_spec=pl...  44 us
    ppermute x6, waiting for transfers between devices, line_sum(): total = total + lax.ppermute(part, 'dp', ring_jumps(ways, -k)).astype(F32)  32.3 us
  transfers between devices with their start and end apart: 64, of which 37 were waited for; matrix products, arithmetic and copies ran while one was open for 26% of the time, Pallas kernels for 17%

profile of v4, /device:TPU:0, one launch (start us, length us, event | category | flops | bytes accessed | tf_op | source)
XLA Modules:
  0.0 921.4 jit_solution(15867900987259687920)
XLA Ops:
  15.8 10.0 %collective-permute-done.1 = bf16[128,2048]{1,0:T(8,128)(2,1)} collective-permute-done((bf16[128,2048]{1,0:T(8,128)(2,1)S(1)}, bf16[128,2048]{1,0:T(8,128)(2,1)}, u32[]{:S(2)}, u32[]{:S(2)}) %collective-permute-start.1) | collective-permute-done | bytes 524320 | tf_op jit(solution)/shard_map/ppermute | solution.py:535
  39.1 12.4 %collective-permute-done.2 = bf16[2,128,2048]{2,1,0:T(8,128)(2,1)S(1)} collective-permute-done((bf16[2,128,2048]{2,1,0:T(8,128)(2,1)S(1)}, bf16[2,128,2048]{2,1,0:T(8,128)(2,1)S(1)}, u32[]{:S(2)}, u32[]{:S(2)}) %collective-permute-start.2) | collective-permute-done | bytes 1048608 | tf_op jit(solution)/shard_map/ppermute | solution.py:536
  60.5 16.9 %all-gather.3.cloned.1.call-done.refs_3_ = bf16[2048,768]{1,0:T(8,128)(2,1)} async-done(((bf16[512,768]{1,0:T(8,128)(2,1)}), bf16[2048,768]{1,0:T(8,128)(2,1)}) %all-gather.3.cloned.1.call-update) | async-done | bytes 3145744 | tf_op jit(solution)/shard_map/all_gather | solution.py:645
  86.3 8.4 shard_map.247
  98.5 9.0 shard_map.248
  107.5 8.4 shard_map.249
  117.6 8.4 shard_map.250
  161.0 8.5 collective-permute-done.16
  210.5 10.0 %collective-permute-start.24 = (bf16[128,2176]{1,0:T(8,128)(2,1)}, bf16[128,2176]{1,0:T(8,128)(2,1)S(1)}, u32[]{:S(2)}, u32[]{:S(2)}) collective-permute-start(bf16[128,2176]{1,0:T(8,128)(2,1)} %concatenate.63), channel_id=1, source_target_pairs={{8,24},{24,16},{16,0},{0,8},{9,25},{25,17},{17,1},{1,9},{10,26},{2... | collective-permute-start | bytes 1671176 | tf_op jit(solution)/shard_map/ppermute | solution.py:498
  220.5 14.4 %collective-permute-done.24 = bf16[128,2176]{1,0:T(8,128)(2,1)S(1)} collective-permute-done((bf16[128,2176]{1,0:T(8,128)(2,1)}, bf16[128,2176]{1,0:T(8,128)(2,1)S(1)}, u32[]{:S(2)}, u32[]{:S(2)}) %collective-permute-start.24) | collective-permute-done | bytes 557088 | tf_op jit(solution)/shard_map/ppermute | solution.py:498
  235.6 14.6 %collective-permute-done.25 = bf16[128,2176]{1,0:T(8,128)(2,1)S(1)} collective-permute-done((bf16[128,2176]{1,0:T(8,128)(2,1)S(1)}, bf16[128,2176]{1,0:T(8,128)(2,1)S(1)}, u32[]{:S(2)}, u32[]{:S(2)}) %collective-permute-start.25) | collective-permute-done | bytes 557088 | tf_op jit(solution)/shard_map/ppermute | solution.py:498
  250.6 14.4 %collective-permute-done.26 = bf16[128,2176]{1,0:T(8,128)(2,1)S(1)} collective-permute-done((bf16[128,2176]{1,0:T(8,128)(2,1)S(1)}, bf16[128,2176]{1,0:T(8,128)(2,1)S(1)}, u32[]{:S(2)}, u32[]{:S(2)}) %collective-permute-start.26) | collective-permute-done | bytes 557088 | tf_op jit(solution)/shard_map/ppermute | solution.py:498
  278.7 22.7 %collective-permute-done.23 = bf16[128,2048]{1,0:T(8,128)(2,1)S(1)} collective-permute-done((bf16[128,2048]{1,0:T(8,128)(2,1)}, bf16[128,2048]{1,0:T(8,128)(2,1)S(1)}, u32[]{:S(2)}, u32[]{:S(2)}) %collective-permute-start.23) | collective-permute-done | bytes 524320 | tf_op jit(solution)/shard_map/ppermute | solution.py:509
  302.2 21.8 %collective-permute-done.21 = bf16[128,2048]{1,0:T(8,128)(2,1)S(1)} collective-permute-done((bf16[128,2048]{1,0:T(8,128)(2,1)}, bf16[128,2048]{1,0:T(8,128)(2,1)S(1)}, u32[]{:S(2)}, u32[]{:S(2)}) %collective-permute-start.21) | collective-permute-done | bytes 524320 | tf_op jit(solution)/shard_map/ppermute | solution.py:509
  342.2 16.0 %collective-permute-done.18 = bf16[128,2176]{1,0:T(8,128)(2,1)S(1)} collective-permute-done((bf16[128,2176]{1,0:T(8,128)(2,1)}, bf16[128,2176]{1,0:T(8,128)(2,1)S(1)}, u32[]{:S(2)}, u32[]{:S(2)}) %collective-permute-start.18) | collective-permute-done | bytes 557088 | tf_op jit(solution)/shard_map/ppermute | solution.py:498
  358.2 15.0 %collective-permute-done.19 = bf16[128,2176]{1,0:T(8,128)(2,1)S(1)} collective-permute-done((bf16[128,2176]{1,0:T(8,128)(2,1)S(1)}, bf16[128,2176]{1,0:T(8,128)(2,1)S(1)}, u32[]{:S(2)}, u32[]{:S(2)}) %collective-permute-start.19) | collective-permute-done | bytes 557088 | tf_op jit(solution)/shard_map/ppermute | solution.py:498
  373.2 14.2 %collective-permute-done.20 = bf16[128,2176]{1,0:T(8,128)(2,1)S(1)} collective-permute-done((bf16[128,2176]{1,0:T(8,128)(2,1)S(1)}, bf16[128,2176]{1,0:T(8,128)(2,1)S(1)}, u32[]{:S(2)}, u32[]{:S(2)}) %collective-permute-start.20) | collective-permute-done | bytes 557088 | tf_op jit(solution)/shard_map/ppermute | solution.py:498
  398.6 30.2 %shard_map.252 = (bf16[1152,768]{1,0:T(8,128)(2,1)}, bf16[1152,768]{1,0:T(8,128)(2,1)}, bf16[1152,768]{1,0:T(8,128)(2,1)}, bf16[1152,2176]{1,0:T(8,128)(2,1)}, bf16[1152,2048]{1,0:T(8,128)(2,1)}) custom-call(s32[1]{0:T(128)} %bitcast.expert_ref, bf16[1152,2176]{1,0:T(8,128)(2,1)} %bitcast.46.rows_ref.gates_ref, ...), custom_call_target="tpu_custom_call" | custom-call | flops 5435817984 | bytes 9437184 | tf_op jit(solution)/shard_map/pallas_call | solution.py:459
  428.8 26.8 %all-to-all-done.3 = bf16[8,144,2176]{2,1,0:T(8,128)(2,1)} async-done(((bf16[8,144,2176]{2,1,0:T(8,128)(2,1)}), bf16[8,144,2176]{2,1,0:T(8,128)(2,1)}, u32[]{:S(2)}, u32[]{:S(2)}) %all-to-all-start.3) | async-done | bytes 5013536 | tf_op jit(solution)/shard_map/all_to_all | solution.py:601
  471.0 30.1 %shard_map.251 = (bf16[1152,768]{1,0:T(8,128)(2,1)}, bf16[1152,768]{1,0:T(8,128)(2,1)}, bf16[1152,768]{1,0:T(8,128)(2,1)}, bf16[1152,2176]{1,0:T(8,128)(2,1)}, bf16[1152,2048]{1,0:T(8,128)(2,1)}) custom-call(s32[1]{0:T(128)} %bitcast.expert_ref, bf16[1152,2176]{1,0:T(8,128)(2,1)} %bitcast.50.rows_ref.gates_ref, ...), custom_call_target="tpu_custom_call" | custom-call | flops 5435817984 | bytes 9437184 | tf_op jit(solution)/shard_map/pallas_call | solution.py:459
  501.1 16.4 %all-to-all-done.4 = bf16[8,144,2176]{2,1,0:T(8,128)(2,1)} async-done(((bf16[8,144,2176]{2,1,0:T(8,128)(2,1)}), bf16[8,144,2176]{2,1,0:T(8,128)(2,1)}, u32[]{:S(2)}, u32[]{:S(2)}) %all-to-all-start.4) | async-done | bytes 5013536 | tf_op jit(solution)/shard_map/all_to_all | solution.py:601
  533.0 7.0 fusion.95
  564.4 8.7 convolution_add_fusion
  596.4 32.3 %collective-permute-done.30 = bf16[128,2176]{1,0:T(8,128)(2,1)S(1)} collective-permute-done((bf16[128,2176]{1,0:T(8,128)(2,1)S(1)}, bf16[128,2176]{1,0:T(8,128)(2,1)S(1)}, u32[]{:S(2)}, u32[]{:S(2)}) %collective-permute-start.30) | collective-permute-done | bytes 557088 | tf_op jit(solution)/shard_map/ppermute | solution.py:518
  663.6 26.2 %all_to_all.131 = f32[32,1,2112]{2,1,0:T(1,128)S(1)} all-to-all(f32[32,1,2112]{2,1,0:T(1,128)S(1)} %copy.141), channel_id=1, replica_groups=mesh['dp'=4,'blk'=4,'head'=2] {'dp','blk','head'}, dimensions={0} | all-to-all | bytes 540672 | tf_op jit(solution)/shard_map/all_to_all | solution.py:597
  709.9 7.2 shard_map.253
  731.1 20.5 %shard_map.256 = (bf16[8,128,768]{2,1,0:T(8,128)(2,1)}, f32[8,128]{1,0:T(8,128)}) custom-call(s32[8]{0:T(128)} %copy-done.28, s32[4]{0:T(128)} %copy-done.29, f32[8,128,768]{2,1,0:T(8,128)} %copy-done.3, f32[8,128,768]{2,1,0:T(8,128)} %copy-done.3, f32[4,256,128]{2,1,0:T(8,128)} %copy-done.4, f32[4,256,128]{2,1,0:T(8,128)} %copy-done.5, f32[1,128]{1,0:T(1,128)} %bitcast.286, ...), custom_call_target="tpu_custom_call" | custom-call | flops 1073741824 | bytes 9437184 | tf_op jit(solution)/shard_map/pallas_call | solution.py:320
  753.7 23.5 %shard_map.254 = (bf16[8,128,768]{2,1,0:T(8,128)(2,1)}, f32[8,128]{1,0:T(8,128)}) custom-call(s32[8]{0:T(128)} %copy-done.27, s32[4]{0:T(128)} %copy-done.26, f32[8,128,768]{2,1,0:T(8,128)} %copy-done.2, f32[8,128,768]{2,1,0:T(8,128)} %copy-done.2, f32[4,256,128]{2,1,0:T(8,128)} %copy-done.4, f32[4,256,128]{2,1,0:T(8,128)} %copy-done.5, f32[1,128]{1,0:T(1,128)} %bitcast.287, ...), custom_call_target="tpu_custom_call" | custom-call | flops 1073741824 | bytes 9437184 | tf_op jit(solution)/shard_map/pallas_call | solution.py:320
  789.7 6.9 collective-permute-start.39
  806.0 7.4 all-to-all-start.9
  833.2 8.1 collective-permute-done.40
  897.5 7.4 all-to-all-done.11
  (497 shorter events, 419.1 us)
Async XLA Ops:
  7.2 70.2 %all-gather.3.cloned.1.call-start = ((), (), s32[]{:S(2)}) async-start(), calls=%async_computation.15 | async-start | bytes 3932160 | tf_op jit(solution)/shard_map/all_gather | solution.py:645
  10.4 118.8 %all-gather.5.cloned.1.call-start = ((), (), s32[]{:S(2)}) async-start(), calls=%async_computation.16 | async-start | bytes 2621440 | tf_op jit(solution)/shard_map/all_gather | solution.py:745
  149.8 25.9 %collective-permute-start.12 = (bf16[2,128,2048]{2,1,0:T(8,128)(2,1)}, bf16[2,128,2048]{2,1,0:T(8,128)(2,1)}, u32[]{:S(2)}, u32[]{:S(2)}) collective-permute-start(bf16[2,128,2048]{2,1,0:T(8,128)(2,1)} %slice.247), channel_id=1, source_target_pairs={{0,4},{1,5},{2,6},{3,7},{4,0},{5,1},{6,2},{7,3},{8,12},{9,13},{10,... | collective-permute-start | bytes 3145736 | tf_op jit(solution)/shard_map/ppermute | solution.py:585
  156.3 28.7 %collective-permute-start.17 = (bf16[128,2048]{1,0:T(8,128)(2,1)}, bf16[128,2048]{1,0:T(8,128)(2,1)S(1)}, u32[]{:S(2)}, u32[]{:S(2)}) collective-permute-start(bf16[128,2048]{1,0:T(8,128)(2,1)} %get-tuple-element.156), channel_id=1, source_target_pairs={{8,0},{24,8},{16,24},{0,16},{9,1},{25,9},{17,25},{1,17},{10,2},{26... | collective-permute-start | bytes 1572872 | tf_op jit(solution)/shard_map/ppermute | solution.py:509
  158.3 24.8 %collective-permute-start.11 = (bf16[2,128,2048]{2,1,0:T(8,128)(2,1)S(1)}, bf16[2,128,2048]{2,1,0:T(8,128)(2,1)S(1)}, u32[]{:S(2)}, u32[]{:S(2)}) collective-permute-start(bf16[2,128,2048]{2,1,0:T(8,128)(2,1)S(1)} %slice.245), channel_id=1, source_target_pairs={{0,1},{1,0},{2,3},{3,2},{4,5},{5,4},{6,7},{7,6},{8,9},{9,8},{10,11... | collective-permute-start | bytes 3145736 | tf_op jit(solution)/shard_map/ppermute | solution.py:585
  198.4 73.1 %all-to-all-start = ((bf16[8,144,2048]{2,1,0:T(8,128)(2,1)}), bf16[8,144,2048]{2,1,0:T(8,128)(2,1)}, u32[]{:S(2)}, u32[]{:S(2)}) async-start(bf16[8,144,2048]{2,1,0:T(8,128)(2,1)} %bitcast.310), calls=%async_computation | async-start | bytes 9437184 | tf_op jit(solution)/shard_map/all_to_all | solution.py:601
  210.5 24.4 %collective-permute-start.24 = (bf16[128,2176]{1,0:T(8,128)(2,1)}, bf16[128,2176]{1,0:T(8,128)(2,1)S(1)}, u32[]{:S(2)}, u32[]{:S(2)}) collective-permute-start(bf16[128,2176]{1,0:T(8,128)(2,1)} %concatenate.63), channel_id=1, source_target_pairs={{8,24},{24,16},{16,0},{0,8},{9,25},{25,17},{17,1},{1,9},{10,26},{2... | collective-permute-start | bytes 1671176 | tf_op jit(solution)/shard_map/ppermute | solution.py:498
  271.5 61.7 %all-to-all-start.1 = ((bf16[8,144,2176]{2,1,0:T(8,128)(2,1)}), bf16[8,144,2176]{2,1,0:T(8,128)(2,1)}, u32[]{:S(2)}, u32[]{:S(2)}) async-start(bf16[8,144,2176]{2,1,0:T(8,128)(2,1)} %bitcast.302), calls=%async_computation.1 | async-start | bytes 10027008 | tf_op jit(solution)/shard_map/all_to_all | solution.py:601
  276.1 25.3 %collective-permute-start.23 = (bf16[128,2048]{1,0:T(8,128)(2,1)}, bf16[128,2048]{1,0:T(8,128)(2,1)S(1)}, u32[]{:S(2)}, u32[]{:S(2)}) collective-permute-start(bf16[128,2048]{1,0:T(8,128)(2,1)} %get-tuple-element.161), channel_id=1, source_target_pairs={{8,0},{24,8},{16,24},{0,16},{9,1},{25,9},{17,25},{1,17},{10,2},{26... | collective-permute-start | bytes 1572872 | tf_op jit(solution)/shard_map/ppermute | solution.py:509
  276.2 26.0 %collective-permute-start.22 = (bf16[128,2048]{1,0:T(8,128)(2,1)}, bf16[128,2048]{1,0:T(8,128)(2,1)S(1)}, u32[]{:S(2)}, u32[]{:S(2)}) collective-permute-start(bf16[128,2048]{1,0:T(8,128)(2,1)} %get-tuple-element.161), channel_id=1, source_target_pairs={{8,16},{24,0},{16,8},{0,24},{9,17},{25,1},{17,9},{1,25},{10,18},{2... | collective-permute-start | bytes 1572872 | tf_op jit(solution)/shard_map/ppermute | solution.py:509
  277.9 46.1 %collective-permute-start.21 = (bf16[128,2048]{1,0:T(8,128)(2,1)}, bf16[128,2048]{1,0:T(8,128)(2,1)S(1)}, u32[]{:S(2)}, u32[]{:S(2)}) collective-permute-start(bf16[128,2048]{1,0:T(8,128)(2,1)} %get-tuple-element.161), channel_id=1, source_target_pairs={{8,24},{24,16},{16,0},{0,8},{9,25},{25,17},{17,1},{1,9},{10,26},{2... | collective-permute-start | bytes 1572872 | tf_op jit(solution)/shard_map/ppermute | solution.py:509
  333.2 60.6 %all-to-all-start.2 = ((bf16[8,144,2048]{2,1,0:T(8,128)(2,1)}), bf16[8,144,2048]{2,1,0:T(8,128)(2,1)}, u32[]{:S(2)}, u32[]{:S(2)}) async-start(bf16[8,144,2048]{2,1,0:T(8,128)(2,1)} %bitcast.311), calls=%async_computation.2 | async-start | bytes 9437184 | tf_op jit(solution)/shard_map/all_to_all | solution.py:601
  393.8 61.8 %all-to-all-start.3 = ((bf16[8,144,2176]{2,1,0:T(8,128)(2,1)}), bf16[8,144,2176]{2,1,0:T(8,128)(2,1)}, u32[]{:S(2)}, u32[]{:S(2)}) async-start(bf16[8,144,2176]{2,1,0:T(8,128)(2,1)} %bitcast.304), calls=%async_computation.3 | async-start | bytes 10027008 | tf_op jit(solution)/shard_map/all_to_all | solution.py:601
  455.6 61.9 %all-to-all-start.4 = ((bf16[8,144,2176]{2,1,0:T(8,128)(2,1)}), bf16[8,144,2176]{2,1,0:T(8,128)(2,1)}, u32[]{:S(2)}, u32[]{:S(2)}) async-start(bf16[8,144,2176]{2,1,0:T(8,128)(2,1)} %bitcast.303), calls=%async_computation.4 | async-start | bytes 10027008 | tf_op jit(solution)/shard_map/all_to_all | solution.py:601
  517.5 61.7 %all-to-all-start.5 = ((bf16[8,144,2176]{2,1,0:T(8,128)(2,1)}), bf16[8,144,2176]{2,1,0:T(8,128)(2,1)}, u32[]{:S(2)}, u32[]{:S(2)}) async-start(bf16[8,144,2176]{2,1,0:T(8,128)(2,1)} %bitcast.301), calls=%async_computation.5 | async-start | bytes 10027008 | tf_op jit(solution)/shard_map/all_to_all | solution.py:601
  529.2 62.7 %collective-permute-start.27 = (bf16[128,2176]{1,0:T(8,128)(2,1)}, bf16[128,2176]{1,0:T(8,128)(2,1)}, u32[]{:S(2)}, u32[]{:S(2)}) collective-permute-start(bf16[128,2176]{1,0:T(8,128)(2,1)} %get-tuple-element.330), channel_id=1, source_target_pairs={{8,0},{24,8},{16,24},{0,16},{9,1},{25,9},{17,25},{1,17},{10,2},{26... | collective-permute-start | bytes 1671176 | tf_op jit(solution)/shard_map/ppermute | solution.py:518
  530.0 63.4 %collective-permute-start.29 = (bf16[128,2176]{1,0:T(8,128)(2,1)}, bf16[128,2176]{1,0:T(8,128)(2,1)}, u32[]{:S(2)}, u32[]{:S(2)}) collective-permute-start(bf16[128,2176]{1,0:T(8,128)(2,1)} %get-tuple-element.331), channel_id=1, source_target_pairs={{8,24},{24,16},{16,0},{0,8},{9,25},{25,17},{17,1},{1,9},{10,26},{2... | collective-permute-start | bytes 1671176 | tf_op jit(solution)/shard_map/ppermute | solution.py:518
  531.7 61.7 %collective-permute-start.28 = (bf16[128,2176]{1,0:T(8,128)(2,1)}, bf16[128,2176]{1,0:T(8,128)(2,1)}, u32[]{:S(2)}, u32[]{:S(2)}) collective-permute-start(bf16[128,2176]{1,0:T(8,128)(2,1)} %get-tuple-element.332), channel_id=1, source_target_pairs={{8,16},{24,0},{16,8},{0,24},{9,17},{25,1},{17,9},{1,25},{10,18},{2... | collective-permute-start | bytes 1671176 | tf_op jit(solution)/shard_map/ppermute | solution.py:518
  579.2 58.5 %all-to-all-start.6 = ((bf16[8,144,2048]{2,1,0:T(8,128)(2,1)}), bf16[8,144,2048]{2,1,0:T(8,128)(2,1)}, u32[]{:S(2)}, u32[]{:S(2)}) async-start(bf16[8,144,2048]{2,1,0:T(8,128)(2,1)} %bitcast.309), calls=%async_computation.6 | async-start | bytes 9437184 | tf_op jit(solution)/shard_map/all_to_all | solution.py:601
  583.8 167.8 %reduce-scatter.4.cloned.1.call-start = ((), (), s32[]{:S(2)}) async-start(), calls=%async_computation.17 | async-start | bytes 2621440 | tf_op jit(solution)/shard_map/reduce_scatter | solution.py:877
  589.9 38.8 %collective-permute-start.30 = (bf16[128,2176]{1,0:T(8,128)(2,1)S(1)}, bf16[128,2176]{1,0:T(8,128)(2,1)S(1)}, u32[]{:S(2)}, u32[]{:S(2)}) collective-permute-start(bf16[128,2176]{1,0:T(8,128)(2,1)S(1)} %get-tuple-element.327), channel_id=1, source_target_pairs={{8,0},{24,8},{16,24},{0,16},{9,1},{25,9},{17,25},{1,17},{10,2},{26... | collective-permute-start | bytes 1671176 | tf_op jit(solution)/shard_map/ppermute | solution.py:518
  590.0 38.7 %collective-permute-start.32 = (bf16[128,2176]{1,0:T(8,128)(2,1)S(1)}, bf16[128,2176]{1,0:T(8,128)(2,1)S(1)}, u32[]{:S(2)}, u32[]{:S(2)}) collective-permute-start(bf16[128,2176]{1,0:T(8,128)(2,1)S(1)} %get-tuple-element.328), channel_id=1, source_target_pairs={{8,24},{24,16},{16,0},{0,8},{9,25},{25,17},{17,1},{1,9},{10,26},{2... | collective-permute-start | bytes 1671176 | tf_op jit(solution)/shard_map/ppermute | solution.py:518
  592.0 36.7 %collective-permute-start.31 = (bf16[128,2176]{1,0:T(8,128)(2,1)S(1)}, bf16[128,2176]{1,0:T(8,128)(2,1)S(1)}, u32[]{:S(2)}, u32[]{:S(2)}) collective-permute-start(bf16[128,2176]{1,0:T(8,128)(2,1)S(1)} %get-tuple-element.329), channel_id=1, source_target_pairs={{8,16},{24,0},{16,8},{0,24},{9,17},{25,1},{17,9},{1,25},{10,18},{2... | collective-permute-start | bytes 1671176 | tf_op jit(solution)/shard_map/ppermute | solution.py:518
  661.2 29.4 %collective-permute-start.35 = (bf16[2,128,2048]{2,1,0:T(8,128)(2,1)S(1)}, bf16[2,128,2048]{2,1,0:T(8,128)(2,1)S(1)}, u32[]{:S(2)}, u32[]{:S(2)}) collective-permute-start(bf16[2,128,2048]{2,1,0:T(8,128)(2,1)S(1)} %pad_maximum_fusion.6), channel_id=1, source_target_pairs={{0,1},{1,0},{2,3},{3,2},{4,5},{5,4},{6,7},{7,6},{8,9},{9,8},{10,11... | collective-permute-start | bytes 3145736 | tf_op jit(solution)/shard_map/ppermute | solution.py:536
  662.6 29.5 %collective-permute-start.36 = (bf16[2,128,2048]{2,1,0:T(8,128)(2,1)S(1)}, bf16[2,128,2048]{2,1,0:T(8,128)(2,1)S(1)}, u32[]{:S(2)}, u32[]{:S(2)}) collective-permute-start(bf16[2,128,2048]{2,1,0:T(8,128)(2,1)S(1)} %pad_maximum_fusion.7), channel_id=1, source_target_pairs={{0,4},{1,5},{2,6},{3,7},{4,0},{5,1},{6,2},{7,3},{8,12},{9,13},{10,... | collective-permute-start | bytes 3145736 | tf_op jit(solution)/shard_map/ppermute | solution.py:536
  701.1 77.2 %all-to-all-start.8 = ((bf16[8,144,2048]{2,1,0:T(8,128)(2,1)}), bf16[8,144,2048]{2,1,0:T(8,128)(2,1)}, u32[]{:S(2)}, u32[]{:S(2)}) async-start(bf16[8,144,2048]{2,1,0:T(8,128)(2,1)} %bitcast.308), calls=%async_computation.9 | async-start | bytes 9437184 | tf_op jit(solution)/shard_map/all_to_all | solution.py:601
  705.9 123.8 %reduce-scatter.8.cloned.1.call-start = ((), (), s32[]{:S(2)}) async-start(), calls=%async_computation.19 | async-start | bytes 2621440 | tf_op jit(solution)/shard_map/reduce_scatter | solution.py:924
  789.7 27.7 %collective-permute-start.39 = (bf16[512,768]{1,0:T(8,128)(2,1)}, bf16[512,768]{1,0:T(8,128)(2,1)}, u32[]{:S(2)}, u32[]{:S(2)}) collective-permute-start(bf16[512,768]{1,0:T(8,128)(2,1)} %constant_dynamic-slice_fusion), channel_id=1, source_target_pairs={{24,8},{16,24},{0,16},{8,0},{25,9},{17,25},{1,17},{9,1},{26,10},{1... | collective-permute-start | bytes 2359304 | tf_op jit(solution)/shard_map/ppermute | solution.py:526
  800.7 42.2 %collective-permute-start.41 = (bf16[4,128,2048]{2,1,0:T(8,128)(2,1)}, bf16[4,128,2048]{2,1,0:T(8,128)(2,1)}, u32[]{:S(2)}, u32[]{:S(2)}) collective-permute-start(bf16[4,128,2048]{2,1,0:T(8,128)(2,1)} %bitcast.88), channel_id=1, source_target_pairs={{0,2},{1,3},{2,0},{3,1},{4,6},{5,7},{6,4},{7,5},{8,10},{9,11},{10,... | collective-permute-start | bytes 6291464 | tf_op jit(solution)/shard_map/ppermute | solution.py:582
  804.9 40.5 %collective-permute-start.42 = (bf16[4,128,2048]{2,1,0:T(8,128)(2,1)}, bf16[4,128,2048]{2,1,0:T(8,128)(2,1)}, u32[]{:S(2)}, u32[]{:S(2)}) collective-permute-start(bf16[4,128,2048]{2,1,0:T(8,128)(2,1)} %bitcast.92), channel_id=1, source_target_pairs={{0,2},{1,3},{2,0},{3,1},{4,6},{5,7},{6,4},{7,5},{8,10},{9,11},{10,... | collective-permute-start | bytes 6291464 | tf_op jit(solution)/shard_map/ppermute | solution.py:582
  833.1 76.4 %reduce-scatter.6.cloned.1.call-start = ((), (), s32[]{:S(2)}) async-start(), calls=%async_computation.18 | async-start | bytes 2621440 | tf_op jit(solution)/shard_map/reduce_scatter | solution.py:877
  854.6 24.3 %collective-permute-start.44 = (bf16[2,128,2048]{2,1,0:T(8,128)(2,1)}, bf16[2,128,2048]{2,1,0:T(8,128)(2,1)}, u32[]{:S(2)}, u32[]{:S(2)}) collective-permute-start(bf16[2,128,2048]{2,1,0:T(8,128)(2,1)} %slice.286), channel_id=1, source_target_pairs={{0,1},{1,0},{2,3},{3,2},{4,5},{5,4},{6,7},{7,6},{8,9},{9,8},{10,11... | collective-permute-start | bytes 3145736 | tf_op jit(solution)/shard_map/ppermute | solution.py:585
  (128 other events, 1733.8 us)
Sparse Core Ops, SparseCore 0:
  10.5 66.8 all-gather.2
  79.6 44.5 all-gather.4
  694.3 49.6 reduce-scatter.3
  746.2 43.5 reduce-scatter.7
  861.9 43.8 reduce-scatter.5

commit v5 on v4

--- a/solution.py
+++ b/solution.py
@@ -845,8 +845,9 @@
     gate_grad = sum(dot_tn(rows, grad) for rows, _, _, grad, _ in kept)
     up_grad = sum(dot_tn(rows, grad) for rows, _, _, _, grad in kept)
     down_grad = sum(dot_tn(gated, cot) for _, gated, cot, _, _ in kept)
-    *grad_mids, out_lines[0], gate_grad, up_grad, down_grad = tie(
-        *grad_mids, out_lines[0], gate_grad, up_grad, down_grad
+    grad_sends = [grad_mid.astype(BF16) for grad_mid in grad_mids]
+    *grad_sends, out_lines[0], gate_grad, up_grad, down_grad = tie(
+        *grad_sends, out_lines[0], gate_grad, up_grad, down_grad
     )
     devices = dp_ways * plane_ways
 
@@ -863,7 +864,7 @@
         yield outcome_lines[0]
 
     *pieces, small, _ = together(
-        *[plane_gather_steps(grad_mids[s].astype(BF16), s, pair) for s in range(seqs)],
+        *[plane_gather_steps(by_rows(grad_sends[s]), s, pair) for s in range(seqs)],
         small_steps(),
         outcome_steps(),
     )
@@ -936,8 +937,11 @@
     qkv_rows, head_small = tie(qkv_rows, head_small)
     for turn in range(dp_ways - 1):
         qkv_rows = ring_sum.send(qkv_rows) if turn else qkv_rows
+        if pair and turn == dp_ways - 2:
+            _, *held = tie(qkv_rows, *held)
+        elif pair and turn:
+            qkv_rows, *held = tie(qkv_rows, *held)
         if pair and turn:
-            qkv_rows, *held = tie(qkv_rows, *held)
             held = [move.send(by_rows(h)) for move, h in zip(sums, held)]
         if turn == 1:
             qkv_rows, out_rows = tie(qkv_rows, out_rows)

time: 934 us -> 933 us (level)
    ppermute x8, waiting for transfers between devices: 27.8 us -> 38.2 us  [plane_reduce(): came = lax.ppermute(parts[half:], PLANE, move)]
  transfers between devices with their start and end apart: 64 -> 64, of which waited for: 37 -> 38; matrix products, arithmetic and copies ran while one was open for 26% -> 26% of each run, Pallas kernels for 17% -> 17%
where the time goes in v5:
time: 933 us; the launch traced here: 921 us
  waiting for transfers between devices  338 us (36%)
  Pallas kernels  156 us (17%)
  matrix products  136 us (15%)
  starting transfers between devices  113 us (12%)
  other arithmetic  68.5 us (7%)
  local copies, waits for them, and re-layouts  64.8 us (7%)
  blocking collectives  26.2 us (3%)
  between operations  18.3 us (2%)
    ppermute x6, waiting for transfers between devices, line_gather(): held = lax.ppermute(held, 'dp', ring_steps(ways))  88.5 us
    dot_general x16, matrix products, dot_tn(): lax.dot_general(a, b, (((0,), (0,)), ((), ())), preferred_element_type=F32)  85.2 us
    pallas_call x2, Pallas kernels, expert_pass(): pl.pallas_call(functools.partial(expert_kernel, experts), grid_spec=pltpu...  60.3 us
    ppermute x9, waiting for transfers between devices, line_spread(): lax.ppermute(rows, 'dp', ring_jumps(ways, k))  57.9 us
    all_to_all x10, waiting for transfers between devices, plane_exchange(): return lax.all_to_all(rows, PLANE, split_axis=0, concat_axis=0, tiled=True)  56.5 us
    pallas_call x2, Pallas kernels, attend_back(): pl.pallas_call(functools.partial(attend_back_kernel, heads), grid_spec=pl...  47.4 us
    all_to_all x10, starting transfers between devices, plane_exchange(): return lax.all_to_all(rows, PLANE, split_axis=0, concat_axis=0, tiled=True)  45.6 us
    ppermute x8, waiting for transfers between devices, plane_reduce(): came = lax.ppermute(parts[half:], PLANE, move)  38.2 us
  transfers between devices with their start and end apart: 64, of which 38 were waited for; matrix products, arithmetic and copies ran while one was open for 26% of the time, Pallas kernels for 17%

profile of v5, /device:TPU:0, one launch (start us, length us, event | category | flops | bytes accessed | tf_op | source)
XLA Modules:
  0.0 921.1 jit_solution(177346984958114819)
XLA Ops:
  15.8 10.0 %collective-permute-done.1 = bf16[128,2048]{1,0:T(8,128)(2,1)} collective-permute-done((bf16[128,2048]{1,0:T(8,128)(2,1)S(1)}, bf16[128,2048]{1,0:T(8,128)(2,1)}, u32[]{:S(2)}, u32[]{:S(2)}) %collective-permute-start.1) | collective-permute-done | bytes 524320 | tf_op jit(solution)/shard_map/ppermute | solution.py:535
  39.1 12.4 %collective-permute-done.2 = bf16[2,128,2048]{2,1,0:T(8,128)(2,1)S(1)} collective-permute-done((bf16[2,128,2048]{2,1,0:T(8,128)(2,1)S(1)}, bf16[2,128,2048]{2,1,0:T(8,128)(2,1)S(1)}, u32[]{:S(2)}, u32[]{:S(2)}) %collective-permute-start.2) | collective-permute-done | bytes 1048608 | tf_op jit(solution)/shard_map/ppermute | solution.py:536
  60.5 16.9 %all-gather.3.cloned.1.call-done.refs_3_ = bf16[2048,768]{1,0:T(8,128)(2,1)} async-done(((bf16[512,768]{1,0:T(8,128)(2,1)}), bf16[2048,768]{1,0:T(8,128)(2,1)}) %all-gather.3.cloned.1.call-update) | async-done | bytes 3145744 | tf_op jit(solution)/shard_map/all_gather | solution.py:645
  86.4 8.4 shard_map.247
  98.4 8.9 shard_map.248
  108.7 8.3 shard_map.249
  118.7 9.5 %shard_map.250 = (bf16[8,128,512]{2,1,0:T(8,128)(2,1)S(1)}, f32[4,4,256,128]{3,2,1,0:T(8,128)S(1)}) custom-call(s32[8]{0:T(128)S(1)} %add_add_fusion.order_ref, s32[4]{0:T(128)S(1)} %convert_reduce_fusion.low_ref, f32[8,128,768]{2,1,0:T(8,128)} %copy-done.3, f32[8,128,768]{2,1,0:T(8,128)} %copy-done.3, f32[4,256,128]{2,1,0:T(8,128)S(1)} %get-tuple-element.386.cos_ref, ...), custom_call_target="tpu_custom_call" | custom-call | flops 536870912 | bytes 6291456 | tf_op jit(solution)/shard_map/pallas_call | solution.py:288
  163.2 8.5 collective-permute-done.16
  212.7 10.1 %collective-permute-start.24 = (bf16[128,2176]{1,0:T(8,128)(2,1)}, bf16[128,2176]{1,0:T(8,128)(2,1)S(1)}, u32[]{:S(2)}, u32[]{:S(2)}) collective-permute-start(bf16[128,2176]{1,0:T(8,128)(2,1)} %concatenate.63), channel_id=1, source_target_pairs={{8,24},{24,16},{16,0},{0,8},{9,25},{25,17},{17,1},{1,9},{10,26},{2... | collective-permute-start | bytes 1671176 | tf_op jit(solution)/shard_map/ppermute | solution.py:498
  222.8 14.3 %collective-permute-done.24 = bf16[128,2176]{1,0:T(8,128)(2,1)S(1)} collective-permute-done((bf16[128,2176]{1,0:T(8,128)(2,1)}, bf16[128,2176]{1,0:T(8,128)(2,1)S(1)}, u32[]{:S(2)}, u32[]{:S(2)}) %collective-permute-start.24) | collective-permute-done | bytes 557088 | tf_op jit(solution)/shard_map/ppermute | solution.py:498
  237.9 14.6 %collective-permute-done.25 = bf16[128,2176]{1,0:T(8,128)(2,1)S(1)} collective-permute-done((bf16[128,2176]{1,0:T(8,128)(2,1)S(1)}, bf16[128,2176]{1,0:T(8,128)(2,1)S(1)}, u32[]{:S(2)}, u32[]{:S(2)}) %collective-permute-start.25) | collective-permute-done | bytes 557088 | tf_op jit(solution)/shard_map/ppermute | solution.py:498
  252.8 14.4 %collective-permute-done.26 = bf16[128,2176]{1,0:T(8,128)(2,1)S(1)} collective-permute-done((bf16[128,2176]{1,0:T(8,128)(2,1)S(1)}, bf16[128,2176]{1,0:T(8,128)(2,1)S(1)}, u32[]{:S(2)}, u32[]{:S(2)}) %collective-permute-start.26) | collective-permute-done | bytes 557088 | tf_op jit(solution)/shard_map/ppermute | solution.py:498
  280.9 22.7 %collective-permute-done.23 = bf16[128,2048]{1,0:T(8,128)(2,1)S(1)} collective-permute-done((bf16[128,2048]{1,0:T(8,128)(2,1)}, bf16[128,2048]{1,0:T(8,128)(2,1)S(1)}, u32[]{:S(2)}, u32[]{:S(2)}) %collective-permute-start.23) | collective-permute-done | bytes 524320 | tf_op jit(solution)/shard_map/ppermute | solution.py:509
  304.4 21.8 %collective-permute-done.21 = bf16[128,2048]{1,0:T(8,128)(2,1)S(1)} collective-permute-done((bf16[128,2048]{1,0:T(8,128)(2,1)}, bf16[128,2048]{1,0:T(8,128)(2,1)S(1)}, u32[]{:S(2)}, u32[]{:S(2)}) %collective-permute-start.21) | collective-permute-done | bytes 524320 | tf_op jit(solution)/shard_map/ppermute | solution.py:509
  344.4 16.0 %collective-permute-done.18 = bf16[128,2176]{1,0:T(8,128)(2,1)S(1)} collective-permute-done((bf16[128,2176]{1,0:T(8,128)(2,1)}, bf16[128,2176]{1,0:T(8,128)(2,1)S(1)}, u32[]{:S(2)}, u32[]{:S(2)}) %collective-permute-start.18) | collective-permute-done | bytes 557088 | tf_op jit(solution)/shard_map/ppermute | solution.py:498
  360.4 15.0 %collective-permute-done.19 = bf16[128,2176]{1,0:T(8,128)(2,1)S(1)} collective-permute-done((bf16[128,2176]{1,0:T(8,128)(2,1)S(1)}, bf16[128,2176]{1,0:T(8,128)(2,1)S(1)}, u32[]{:S(2)}, u32[]{:S(2)}) %collective-permute-start.19) | collective-permute-done | bytes 557088 | tf_op jit(solution)/shard_map/ppermute | solution.py:498
  375.4 14.2 %collective-permute-done.20 = bf16[128,2176]{1,0:T(8,128)(2,1)S(1)} collective-permute-done((bf16[128,2176]{1,0:T(8,128)(2,1)S(1)}, bf16[128,2176]{1,0:T(8,128)(2,1)S(1)}, u32[]{:S(2)}, u32[]{:S(2)}) %collective-permute-start.20) | collective-permute-done | bytes 557088 | tf_op jit(solution)/shard_map/ppermute | solution.py:498
  400.8 30.2 %shard_map.252 = (bf16[1152,768]{1,0:T(8,128)(2,1)}, bf16[1152,768]{1,0:T(8,128)(2,1)}, bf16[1152,768]{1,0:T(8,128)(2,1)}, bf16[1152,2176]{1,0:T(8,128)(2,1)}, bf16[1152,2048]{1,0:T(8,128)(2,1)}) custom-call(s32[1]{0:T(128)} %bitcast.expert_ref, bf16[1152,2176]{1,0:T(8,128)(2,1)} %bitcast.46.rows_ref.gates_ref, ...), custom_call_target="tpu_custom_call" | custom-call | flops 5435817984 | bytes 9437184 | tf_op jit(solution)/shard_map/pallas_call | solution.py:459
  431.0 26.8 %all-to-all-done.3 = bf16[8,144,2176]{2,1,0:T(8,128)(2,1)} async-done(((bf16[8,144,2176]{2,1,0:T(8,128)(2,1)}), bf16[8,144,2176]{2,1,0:T(8,128)(2,1)}, u32[]{:S(2)}, u32[]{:S(2)}) %all-to-all-start.3) | async-done | bytes 5013536 | tf_op jit(solution)/shard_map/all_to_all | solution.py:601
  473.2 30.1 %shard_map.251 = (bf16[1152,768]{1,0:T(8,128)(2,1)}, bf16[1152,768]{1,0:T(8,128)(2,1)}, bf16[1152,768]{1,0:T(8,128)(2,1)}, bf16[1152,2176]{1,0:T(8,128)(2,1)}, bf16[1152,2048]{1,0:T(8,128)(2,1)}) custom-call(s32[1]{0:T(128)} %bitcast.expert_ref, bf16[1152,2176]{1,0:T(8,128)(2,1)} %bitcast.50.rows_ref.gates_ref, ...), custom_call_target="tpu_custom_call" | custom-call | flops 5435817984 | bytes 9437184 | tf_op jit(solution)/shard_map/pallas_call | solution.py:459
  503.3 16.5 %all-to-all-done.4 = bf16[8,144,2176]{2,1,0:T(8,128)(2,1)} async-done(((bf16[8,144,2176]{2,1,0:T(8,128)(2,1)}), bf16[8,144,2176]{2,1,0:T(8,128)(2,1)}, u32[]{:S(2)}, u32[]{:S(2)}) %all-to-all-start.4) | async-done | bytes 5013536 | tf_op jit(solution)/shard_map/all_to_all | solution.py:601
  535.1 6.9 fusion.97
  559.8 7.0 convolution_add_fusion.1
  566.8 8.7 convolution_add_fusion
  598.8 32.1 %collective-permute-done.30 = bf16[128,2176]{1,0:T(8,128)(2,1)S(1)} collective-permute-done((bf16[128,2176]{1,0:T(8,128)(2,1)S(1)}, bf16[128,2176]{1,0:T(8,128)(2,1)S(1)}, u32[]{:S(2)}, u32[]{:S(2)}) %collective-permute-start.30) | collective-permute-done | bytes 557088 | tf_op jit(solution)/shard_map/ppermute | solution.py:518
  641.9 6.9 convolution_convert_fusion.6
  660.0 26.2 %all_to_all.131 = f32[32,1,2112]{2,1,0:T(1,128)S(1)} all-to-all(f32[32,1,2112]{2,1,0:T(1,128)S(1)} %copy.141), channel_id=1, replica_groups=mesh['dp'=4,'blk'=4,'head'=2] {'dp','blk','head'}, dimensions={0} | all-to-all | bytes 540672 | tf_op jit(solution)/shard_map/all_to_all | solution.py:597
  716.6 6.8 shard_map.255
  729.6 23.8 %shard_map.256 = (bf16[8,128,768]{2,1,0:T(8,128)(2,1)}, f32[8,128]{1,0:T(8,128)}) custom-call(s32[8]{0:T(128)} %copy-done.28, s32[4]{0:T(128)} %copy-done.29, f32[8,128,768]{2,1,0:T(8,128)} %copy-done.3, f32[8,128,768]{2,1,0:T(8,128)} %copy-done.3, f32[4,256,128]{2,1,0:T(8,128)} %copy-done.4, f32[4,256,128]{2,1,0:T(8,128)} %copy-done.5, f32[1,128]{1,0:T(1,128)} %bitcast.288, ...), custom_call_target="tpu_custom_call" | custom-call | flops 1073741824 | bytes 9437184 | tf_op jit(solution)/shard_map/pallas_call | solution.py:320
  755.6 23.6 %shard_map.254 = (bf16[8,128,768]{2,1,0:T(8,128)(2,1)}, f32[8,128]{1,0:T(8,128)}) custom-call(s32[8]{0:T(128)} %copy-done.27, s32[4]{0:T(128)} %copy-done.26, f32[8,128,768]{2,1,0:T(8,128)} %copy-done.2, f32[8,128,768]{2,1,0:T(8,128)} %copy-done.2, f32[4,256,128]{2,1,0:T(8,128)} %copy-done.4, f32[4,256,128]{2,1,0:T(8,128)} %copy-done.5, f32[1,128]{1,0:T(1,128)} %bitcast.289, ...), custom_call_target="tpu_custom_call" | custom-call | flops 1073741824 | bytes 9437184 | tf_op jit(solution)/shard_map/pallas_call | solution.py:320
  791.8 6.8 collective-permute-start.39
  878.3 13.6 %collective-permute-done.44 = bf16[2,128,2048]{2,1,0:T(8,128)(2,1)} collective-permute-done((bf16[2,128,2048]{2,1,0:T(8,128)(2,1)}, bf16[2,128,2048]{2,1,0:T(8,128)(2,1)}, u32[]{:S(2)}, u32[]{:S(2)}) %collective-permute-start.44) | collective-permute-done | bytes 1048608 | tf_op jit(solution)/shard_map/ppermute | solution.py:585
  (479 shorter events, 410.8 us)
Async XLA Ops:
  7.2 70.2 %all-gather.3.cloned.1.call-start = ((), (), s32[]{:S(2)}) async-start(), calls=%async_computation.15 | async-start | bytes 3932160 | tf_op jit(solution)/shard_map/all_gather | solution.py:645
  10.4 121.0 %all-gather.5.cloned.1.call-start = ((), (), s32[]{:S(2)}) async-start(), calls=%async_computation.16 | async-start | bytes 2621440 | tf_op jit(solution)/shard_map/all_gather | solution.py:745
  152.0 25.9 %collective-permute-start.12 = (bf16[2,128,2048]{2,1,0:T(8,128)(2,1)}, bf16[2,128,2048]{2,1,0:T(8,128)(2,1)}, u32[]{:S(2)}, u32[]{:S(2)}) collective-permute-start(bf16[2,128,2048]{2,1,0:T(8,128)(2,1)} %slice.247), channel_id=1, source_target_pairs={{0,4},{1,5},{2,6},{3,7},{4,0},{5,1},{6,2},{7,3},{8,12},{9,13},{10,... | collective-permute-start | bytes 3145736 | tf_op jit(solution)/shard_map/ppermute | solution.py:585
  158.6 28.7 %collective-permute-start.17 = (bf16[128,2048]{1,0:T(8,128)(2,1)}, bf16[128,2048]{1,0:T(8,128)(2,1)S(1)}, u32[]{:S(2)}, u32[]{:S(2)}) collective-permute-start(bf16[128,2048]{1,0:T(8,128)(2,1)} %get-tuple-element.155), channel_id=1, source_target_pairs={{8,0},{24,8},{16,24},{0,16},{9,1},{25,9},{17,25},{1,17},{10,2},{26... | collective-permute-start | bytes 1572872 | tf_op jit(solution)/shard_map/ppermute | solution.py:509
  160.5 24.8 %collective-permute-start.11 = (bf16[2,128,2048]{2,1,0:T(8,128)(2,1)S(1)}, bf16[2,128,2048]{2,1,0:T(8,128)(2,1)S(1)}, u32[]{:S(2)}, u32[]{:S(2)}) collective-permute-start(bf16[2,128,2048]{2,1,0:T(8,128)(2,1)S(1)} %slice.245), channel_id=1, source_target_pairs={{0,1},{1,0},{2,3},{3,2},{4,5},{5,4},{6,7},{7,6},{8,9},{9,8},{10,11... | collective-permute-start | bytes 3145736 | tf_op jit(solution)/shard_map/ppermute | solution.py:585
  200.7 73.0 %all-to-all-start = ((bf16[8,144,2048]{2,1,0:T(8,128)(2,1)}), bf16[8,144,2048]{2,1,0:T(8,128)(2,1)}, u32[]{:S(2)}, u32[]{:S(2)}) async-start(bf16[8,144,2048]{2,1,0:T(8,128)(2,1)} %bitcast.312), calls=%async_computation | async-start | bytes 9437184 | tf_op jit(solution)/shard_map/all_to_all | solution.py:601
  273.7 61.7 %all-to-all-start.1 = ((bf16[8,144,2176]{2,1,0:T(8,128)(2,1)}), bf16[8,144,2176]{2,1,0:T(8,128)(2,1)}, u32[]{:S(2)}, u32[]{:S(2)}) async-start(bf16[8,144,2176]{2,1,0:T(8,128)(2,1)} %bitcast.304), calls=%async_computation.1 | async-start | bytes 10027008 | tf_op jit(solution)/shard_map/all_to_all | solution.py:601
  278.4 25.3 %collective-permute-start.23 = (bf16[128,2048]{1,0:T(8,128)(2,1)}, bf16[128,2048]{1,0:T(8,128)(2,1)S(1)}, u32[]{:S(2)}, u32[]{:S(2)}) collective-permute-start(bf16[128,2048]{1,0:T(8,128)(2,1)} %get-tuple-element.160), channel_id=1, source_target_pairs={{8,0},{24,8},{16,24},{0,16},{9,1},{25,9},{17,25},{1,17},{10,2},{26... | collective-permute-start | bytes 1572872 | tf_op jit(solution)/shard_map/ppermute | solution.py:509
  278.4 26.0 %collective-permute-start.22 = (bf16[128,2048]{1,0:T(8,128)(2,1)}, bf16[128,2048]{1,0:T(8,128)(2,1)S(1)}, u32[]{:S(2)}, u32[]{:S(2)}) collective-permute-start(bf16[128,2048]{1,0:T(8,128)(2,1)} %get-tuple-element.160), channel_id=1, source_target_pairs={{8,16},{24,0},{16,8},{0,24},{9,17},{25,1},{17,9},{1,25},{10,18},{2... | collective-permute-start | bytes 1572872 | tf_op jit(solution)/shard_map/ppermute | solution.py:509
  280.2 46.1 %collective-permute-start.21 = (bf16[128,2048]{1,0:T(8,128)(2,1)}, bf16[128,2048]{1,0:T(8,128)(2,1)S(1)}, u32[]{:S(2)}, u32[]{:S(2)}) collective-permute-start(bf16[128,2048]{1,0:T(8,128)(2,1)} %get-tuple-element.160), channel_id=1, source_target_pairs={{8,24},{24,16},{16,0},{0,8},{9,25},{25,17},{17,1},{1,9},{10,26},{2... | collective-permute-start | bytes 1572872 | tf_op jit(solution)/shard_map/ppermute | solution.py:509
  335.4 60.6 %all-to-all-start.2 = ((bf16[8,144,2048]{2,1,0:T(8,128)(2,1)}), bf16[8,144,2048]{2,1,0:T(8,128)(2,1)}, u32[]{:S(2)}, u32[]{:S(2)}) async-start(bf16[8,144,2048]{2,1,0:T(8,128)(2,1)} %bitcast.313), calls=%async_computation.2 | async-start | bytes 9437184 | tf_op jit(solution)/shard_map/all_to_all | solution.py:601
  396.0 61.8 %all-to-all-start.3 = ((bf16[8,144,2176]{2,1,0:T(8,128)(2,1)}), bf16[8,144,2176]{2,1,0:T(8,128)(2,1)}, u32[]{:S(2)}, u32[]{:S(2)}) async-start(bf16[8,144,2176]{2,1,0:T(8,128)(2,1)} %bitcast.306), calls=%async_computation.3 | async-start | bytes 10027008 | tf_op jit(solution)/shard_map/all_to_all | solution.py:601
  457.9 61.9 %all-to-all-start.4 = ((bf16[8,144,2176]{2,1,0:T(8,128)(2,1)}), bf16[8,144,2176]{2,1,0:T(8,128)(2,1)}, u32[]{:S(2)}, u32[]{:S(2)}) async-start(bf16[8,144,2176]{2,1,0:T(8,128)(2,1)} %bitcast.305), calls=%async_computation.4 | async-start | bytes 10027008 | tf_op jit(solution)/shard_map/all_to_all | solution.py:601
  519.7 61.7 %all-to-all-start.5 = ((bf16[8,144,2176]{2,1,0:T(8,128)(2,1)}), bf16[8,144,2176]{2,1,0:T(8,128)(2,1)}, u32[]{:S(2)}, u32[]{:S(2)}) async-start(bf16[8,144,2176]{2,1,0:T(8,128)(2,1)} %bitcast.303), calls=%async_computation.5 | async-start | bytes 10027008 | tf_op jit(solution)/shard_map/all_to_all | solution.py:601
  531.4 62.9 %collective-permute-start.27 = (bf16[128,2176]{1,0:T(8,128)(2,1)}, bf16[128,2176]{1,0:T(8,128)(2,1)}, u32[]{:S(2)}, u32[]{:S(2)}) collective-permute-start(bf16[128,2176]{1,0:T(8,128)(2,1)} %get-tuple-element.332), channel_id=1, source_target_pairs={{8,0},{24,8},{16,24},{0,16},{9,1},{25,9},{17,25},{1,17},{10,2},{26... | collective-permute-start | bytes 1671176 | tf_op jit(solution)/shard_map/ppermute | solution.py:518
  532.2 63.5 %collective-permute-start.29 = (bf16[128,2176]{1,0:T(8,128)(2,1)}, bf16[128,2176]{1,0:T(8,128)(2,1)}, u32[]{:S(2)}, u32[]{:S(2)}) collective-permute-start(bf16[128,2176]{1,0:T(8,128)(2,1)} %get-tuple-element.333), channel_id=1, source_target_pairs={{8,24},{24,16},{16,0},{0,8},{9,25},{25,17},{17,1},{1,9},{10,26},{2... | collective-permute-start | bytes 1671176 | tf_op jit(solution)/shard_map/ppermute | solution.py:518
  533.7 62.0 %collective-permute-start.28 = (bf16[128,2176]{1,0:T(8,128)(2,1)}, bf16[128,2176]{1,0:T(8,128)(2,1)}, u32[]{:S(2)}, u32[]{:S(2)}) collective-permute-start(bf16[128,2176]{1,0:T(8,128)(2,1)} %get-tuple-element.334), channel_id=1, source_target_pairs={{8,16},{24,0},{16,8},{0,24},{9,17},{25,1},{17,9},{1,25},{10,18},{2... | collective-permute-start | bytes 1671176 | tf_op jit(solution)/shard_map/ppermute | solution.py:518
  581.4 58.5 %all-to-all-start.6 = ((bf16[8,144,2048]{2,1,0:T(8,128)(2,1)}), bf16[8,144,2048]{2,1,0:T(8,128)(2,1)}, u32[]{:S(2)}, u32[]{:S(2)}) async-start(bf16[8,144,2048]{2,1,0:T(8,128)(2,1)} %bitcast.311), calls=%async_computation.6 | async-start | bytes 9437184 | tf_op jit(solution)/shard_map/all_to_all | solution.py:601
  586.0 167.5 %reduce-scatter.4.cloned.1.call-start = ((), (), s32[]{:S(2)}) async-start(), calls=%async_computation.17 | async-start | bytes 2621440 | tf_op jit(solution)/shard_map/reduce_scatter | solution.py:878
  592.1 38.8 %collective-permute-start.30 = (bf16[128,2176]{1,0:T(8,128)(2,1)S(1)}, bf16[128,2176]{1,0:T(8,128)(2,1)S(1)}, u32[]{:S(2)}, u32[]{:S(2)}) collective-permute-start(bf16[128,2176]{1,0:T(8,128)(2,1)S(1)} %get-tuple-element.329), channel_id=1, source_target_pairs={{8,0},{24,8},{16,24},{0,16},{9,1},{25,9},{17,25},{1,17},{10,2},{26... | collective-permute-start | bytes 1671176 | tf_op jit(solution)/shard_map/ppermute | solution.py:518
  592.2 38.7 %collective-permute-start.32 = (bf16[128,2176]{1,0:T(8,128)(2,1)S(1)}, bf16[128,2176]{1,0:T(8,128)(2,1)S(1)}, u32[]{:S(2)}, u32[]{:S(2)}) collective-permute-start(bf16[128,2176]{1,0:T(8,128)(2,1)S(1)} %get-tuple-element.330), channel_id=1, source_target_pairs={{8,24},{24,16},{16,0},{0,8},{9,25},{25,17},{17,1},{1,9},{10,26},{2... | collective-permute-start | bytes 1671176 | tf_op jit(solution)/shard_map/ppermute | solution.py:518
  594.4 36.5 %collective-permute-start.31 = (bf16[128,2176]{1,0:T(8,128)(2,1)S(1)}, bf16[128,2176]{1,0:T(8,128)(2,1)S(1)}, u32[]{:S(2)}, u32[]{:S(2)}) collective-permute-start(bf16[128,2176]{1,0:T(8,128)(2,1)S(1)} %get-tuple-element.331), channel_id=1, source_target_pairs={{8,16},{24,0},{16,8},{0,24},{9,17},{25,1},{17,9},{1,25},{10,18},{2... | collective-permute-start | bytes 1671176 | tf_op jit(solution)/shard_map/ppermute | solution.py:518
  657.6 29.3 %collective-permute-start.35 = (bf16[2,128,2048]{2,1,0:T(8,128)(2,1)S(1)}, bf16[2,128,2048]{2,1,0:T(8,128)(2,1)S(1)}, u32[]{:S(2)}, u32[]{:S(2)}) collective-permute-start(bf16[2,128,2048]{2,1,0:T(8,128)(2,1)S(1)} %pad_maximum_fusion.6), channel_id=1, source_target_pairs={{0,1},{1,0},{2,3},{3,2},{4,5},{5,4},{6,7},{7,6},{8,9},{9,8},{10,11... | collective-permute-start | bytes 3145736 | tf_op jit(solution)/shard_map/ppermute | solution.py:536
  659.0 29.5 %collective-permute-start.36 = (bf16[2,128,2048]{2,1,0:T(8,128)(2,1)S(1)}, bf16[2,128,2048]{2,1,0:T(8,128)(2,1)S(1)}, u32[]{:S(2)}, u32[]{:S(2)}) collective-permute-start(bf16[2,128,2048]{2,1,0:T(8,128)(2,1)S(1)} %pad_maximum_fusion.7), channel_id=1, source_target_pairs={{0,4},{1,5},{2,6},{3,7},{4,0},{5,1},{6,2},{7,3},{8,12},{9,13},{10,... | collective-permute-start | bytes 3145736 | tf_op jit(solution)/shard_map/ppermute | solution.py:536
  697.5 82.7 %all-to-all-start.8 = ((bf16[8,144,2048]{2,1,0:T(8,128)(2,1)}), bf16[8,144,2048]{2,1,0:T(8,128)(2,1)}, u32[]{:S(2)}, u32[]{:S(2)}) async-start(bf16[8,144,2048]{2,1,0:T(8,128)(2,1)} %bitcast.310), calls=%async_computation.9 | async-start | bytes 9437184 | tf_op jit(solution)/shard_map/all_to_all | solution.py:601
  702.3 127.6 %reduce-scatter.8.cloned.1.call-start = ((), (), s32[]{:S(2)}) async-start(), calls=%async_computation.19 | async-start | bytes 2621440 | tf_op jit(solution)/shard_map/reduce_scatter | solution.py:925
  791.8 24.6 %collective-permute-start.39 = (bf16[512,768]{1,0:T(8,128)(2,1)}, bf16[512,768]{1,0:T(8,128)(2,1)}, u32[]{:S(2)}, u32[]{:S(2)}) collective-permute-start(bf16[512,768]{1,0:T(8,128)(2,1)} %constant_dynamic-slice_fusion), channel_id=1, source_target_pairs={{24,8},{16,24},{0,16},{8,0},{25,9},{17,25},{1,17},{9,1},{26,10},{1... | collective-permute-start | bytes 2359304 | tf_op jit(solution)/shard_map/ppermute | solution.py:526
  802.7 38.8 %collective-permute-start.41 = (bf16[4,128,2048]{2,1,0:T(8,128)(2,1)}, bf16[4,128,2048]{2,1,0:T(8,128)(2,1)}, u32[]{:S(2)}, u32[]{:S(2)}) collective-permute-start(bf16[4,128,2048]{2,1,0:T(8,128)(2,1)} %bitcast.88), channel_id=1, source_target_pairs={{0,2},{1,3},{2,0},{3,1},{4,6},{5,7},{6,4},{7,5},{8,10},{9,11},{10,... | collective-permute-start | bytes 6291464 | tf_op jit(solution)/shard_map/ppermute | solution.py:582
  806.9 37.1 %collective-permute-start.42 = (bf16[4,128,2048]{2,1,0:T(8,128)(2,1)}, bf16[4,128,2048]{2,1,0:T(8,128)(2,1)}, u32[]{:S(2)}, u32[]{:S(2)}) collective-permute-start(bf16[4,128,2048]{2,1,0:T(8,128)(2,1)} %bitcast.92), channel_id=1, source_target_pairs={{0,2},{1,3},{2,0},{3,1},{4,6},{5,7},{6,4},{7,5},{8,10},{9,11},{10,... | collective-permute-start | bytes 6291464 | tf_op jit(solution)/shard_map/ppermute | solution.py:582
  833.7 75.2 %reduce-scatter.6.cloned.1.call-start = ((), (), s32[]{:S(2)}) async-start(), calls=%async_computation.18 | async-start | bytes 2621440 | tf_op jit(solution)/shard_map/reduce_scatter | solution.py:878
  862.4 29.5 %collective-permute-start.44 = (bf16[2,128,2048]{2,1,0:T(8,128)(2,1)}, bf16[2,128,2048]{2,1,0:T(8,128)(2,1)}, u32[]{:S(2)}, u32[]{:S(2)}) collective-permute-start(bf16[2,128,2048]{2,1,0:T(8,128)(2,1)} %slice.286), channel_id=1, source_target_pairs={{0,1},{1,0},{2,3},{3,2},{4,5},{5,4},{6,7},{7,6},{8,9},{9,8},{10,11... | collective-permute-start | bytes 3145736 | tf_op jit(solution)/shard_map/ppermute | solution.py:585
  870.2 28.0 %all-to-all-start.11 = ((bf16[8,64,768]{2,1,0:T(8,128)(2,1)}), bf16[8,64,768]{2,1,0:T(8,128)(2,1)}, u32[]{:S(2)}, u32[]{:S(2)}) async-start(bf16[8,64,768]{2,1,0:T(8,128)(2,1)} %bitcast.101), calls=%async_computation.14 | async-start | bytes 1572864 | tf_op jit(solution)/shard_map/all_to_all | solution.py:601
  (121 other events, 1688.2 us)
Sparse Core Ops, SparseCore 0:
  10.5 66.8 all-gather.2
  79.6 44.5 all-gather.4
  690.7 49.8 reduce-scatter.3
  742.8 43.1 reduce-scatter.7
  860.8 41.9 reduce-scatter.5
